TPU v7x, 32 devices: a whole 2x2x4 slice. The times are simulated.
32 devices in a mesh: seq: 8 (over y, x, core), head: 4 (over z).
Axes of the slice: x: 2, y: 2, z: 4, core: 2. Of those that a mesh axis runs over, the one named last changes fastest.
Arguments:
- inputs: bfloat16 [2, 7168, 512], P(None, 'seq'), may hold values from -8 to 8
- doc_ids: int32 [2, 7168], P(None, 'seq'), may hold values from 0 to 7167, as said below
- pad_mask: int32 [2, 7168], P(None, 'seq'), may hold values 0 or 1
- ln1_gain: float32 [512], replicated, may hold values from 0.25 to 1.75
- ln1_shift: float32 [512], replicated, may hold values from -3 to 3
- w_query: bfloat16 [512, 512], P(None, 'head'), may hold values from -0.25 to 0.25
- w_key: bfloat16 [512, 512], P(None, 'head'), may hold values from -0.25 to 0.25
- w_value: bfloat16 [512, 512], P(None, 'head'), may hold values from -0.25 to 0.25
- w_out: bfloat16 [512, 512], P('head'), may hold values from -0.375 to 0.375
- ln2_gain: float32 [512], replicated, may hold values from 0.25 to 1.75
- ln2_shift: float32 [512], replicated, may hold values from -3 to 3
- w_up: bfloat16 [512, 2048], P(None, 'head'), may hold values from -0.25 to 0.25
- b_up: float32 [2048], P('head'), may hold values from -3 to 3
- w_down: bfloat16 [2048, 512], P('head'), may hold values from -0.125 to 0.125
- b_down: float32 [512], replicated, may hold values from -3 to 3
- out_grad: bfloat16 [2, 7168, 512], P(None, 'seq'), may hold values from -6 to 6
Outputs:
- out: bfloat16 [2, 7168, 512], P(None, 'seq')
- grad_inputs: float32 [2, 7168, 512], P(None, 'seq')
- grad_ln1_gain: float32 [512], replicated
- grad_ln1_shift: float32 [512], replicated
- grad_w_query: float32 [512, 512], P(None, 'head')
- grad_w_key: float32 [512, 512], P(None, 'head')
- grad_w_value: float32 [512, 512], P(None, 'head')
- grad_w_out: float32 [512, 512], P('head')
- grad_ln2_gain: float32 [512], replicated
- grad_ln2_shift: float32 [512], replicated
- grad_w_up: float32 [512, 2048], P(None, 'head')
- grad_b_up: float32 [2048], P('head')
- grad_w_down: float32 [2048, 512], P('head')
- grad_b_down: float32 [512], replicated
Inputs may be any that keep to these rules, and one draw needn't show every extreme that they name: `doc_ids`: ids never fall along a row, so that equal ids stand together; each row begins with id 0 and its last document has id 7168 - 1.
All inputs are finite; a program needn't handle non-finite values. No bound on the sum of `pad_mask` on one device may be relied on, other than what follows from the above.
Results may differ from a plain program's by a relative error of at most 0.013.
Values sent between devices are 32-bit elements; how exact they have to be, the bound alone decides.
No kernel may reach another device: no remote copies, remote signals or barrier semaphores. Data moves between devices by JAX's collectives and lax.ppermute only.
A program may use at most 128 MiB of HBM per device.

v0:
```python
import math

import jax
import jax.numpy as jnp
from jax import lax
from jax.sharding import PartitionSpec as P

HEAD_DIM = 64
SPAN = 128


norm_eps = 1e-05
masked_score = -1e30


def entering(value, axis, combine, identity, reverse):
    devices, here = (lax.axis_size(axis), lax.axis_index(axis))
    everything = jax.tree.map(lambda part: lax.all_gather(part, axis), value)
    start = jax.tree.map(
        lambda part, zero: jnp.broadcast_to(jnp.asarray(zero, part.dtype), part.shape),
        value,
        identity,
    )

    def lap(k, before):
        at = devices - 1 - k if reverse else k
        reached = at > here if reverse else at < here
        new = combine(before, jax.tree.map(lambda part: part[at], everything))
        return jax.tree.map(lambda a, b: jnp.where(reached, a, b), new, before)

    return lax.fori_loop(0, devices, lap, start)


def layer_norm(values, norm_gain, norm_shift):
    average = jnp.mean(values, axis=-1, keepdims=True)
    centred = values - average
    spread = jnp.mean(centred * centred, axis=-1, keepdims=True)
    return centred * lax.rsqrt(spread + norm_eps) * norm_gain + norm_shift


def gelu_exact(values):
    return jax.nn.gelu(values, approximate=False)


def join_forward(earlier, later_part):
    keys_before, values_before, count_before, tag_before = earlier
    keys_after, values_after, count_after, tag_after = later_part
    same_doc = tag_after == tag_before
    is_empty = tag_after < 0.0
    sum_keys = jnp.where(same_doc[..., None], keys_before + keys_after, keys_after)
    sum_values = jnp.where(same_doc[..., None], values_before + values_after, values_after)
    token_count = jnp.where(same_doc, count_before + count_after, count_after)
    sum_keys = jnp.where(is_empty[..., None], keys_before, sum_keys)
    sum_values = jnp.where(is_empty[..., None], values_before, sum_values)
    token_count = jnp.where(is_empty, count_before, token_count)
    doc_tag = jnp.where(is_empty, tag_before, tag_after)
    return (sum_keys, sum_values, token_count, doc_tag)


def join_back(higher, lower_part):
    keys_high, values_high, tag_high = higher
    keys_low, values_low, tag_low = lower_part
    same_doc = tag_high == tag_low
    is_empty = tag_low < 0.0
    grad_keys = jnp.where(same_doc[..., None], keys_low + keys_high, keys_low)
    grad_values = jnp.where(same_doc[..., None], values_low + values_high, values_low)
    grad_keys = jnp.where(is_empty[..., None], keys_high, grad_keys)
    grad_values = jnp.where(is_empty[..., None], values_high, grad_values)
    doc_tag = jnp.where(is_empty, tag_high, tag_low)
    return (grad_keys, grad_values, doc_tag)


def product_t(left, right):
    return lax.dot_general(
        left, right, (((0,), (0,)), ((), ())), preferred_element_type=jnp.float32
    )


def product_nt(left, right):
    return lax.dot_general(
        left, right, (((1,), (1,)), ((), ())), preferred_element_type=jnp.float32
    )


def carry_forward(total, identity):
    carried = entering(total, "seq", join_forward, identity, False)
    return carried


def carry_back(total, identity):
    carried = entering(total, "seq", join_back, identity, True)
    return carried


def on_device(
    inputs,
    doc_ids,
    pad_mask,
    ln1_gain,
    ln1_shift,
    w_query,
    w_key,
    w_value,
    w_out,
    ln2_gain,
    ln2_shift,
    w_up,
    b_up,
    w_down,
    b_down,
    out_grad,
):
    row_count, region_len, width = inputs.shape
    local_width = w_query.shape[1]
    head_count = local_width // HEAD_DIM
    span_count = region_len // SPAN
    token_total = row_count * region_len
    score_scale = 1.0 / math.sqrt(HEAD_DIM)
    span_shape = (row_count, span_count, SPAN, head_count, HEAD_DIM)
    x_flat = inputs.reshape(token_total, width).astype(jnp.float32)
    normed1, norm1_back = jax.vjp(layer_norm, x_flat, ln1_gain, ln1_shift)
    hidden1 = normed1.astype(jnp.bfloat16)
    queries = (jnp.dot(hidden1, w_query, preferred_element_type=jnp.float32) * score_scale).astype(
        jnp.bfloat16
    )
    key_rows = jnp.dot(hidden1, w_key, preferred_element_type=jnp.float32).astype(jnp.bfloat16)
    value_rows = jnp.dot(hidden1, w_value, preferred_element_type=jnp.float32).astype(jnp.bfloat16)
    query_spans = queries.reshape(span_shape)
    key_spans = key_rows.reshape(span_shape)
    value_spans = value_rows.reshape(span_shape)
    doc_span = doc_ids.reshape(row_count, span_count, SPAN)
    doc_float = doc_span.astype(jnp.float32)
    alive = pad_mask.reshape(row_count, span_count, SPAN) == 1
    last_doc = doc_span[:, :, SPAN - 1]
    picked = ((doc_span == last_doc[:, :, None]) & alive).astype(jnp.bfloat16)
    part_keys = jnp.einsum(
        "rst,rstc->rsc",
        picked,
        key_rows.reshape(row_count, span_count, SPAN, local_width),
        preferred_element_type=jnp.float32,
    )
    part_values = jnp.einsum(
        "rst,rstc->rsc",
        picked,
        value_rows.reshape(row_count, span_count, SPAN, local_width),
        preferred_element_type=jnp.float32,
    )
    part_count = jnp.sum(picked, axis=2, dtype=jnp.float32)
    part_tag = last_doc.astype(jnp.float32)

    def span_part(span_index):
        return (
            part_keys[:, span_index],
            part_values[:, span_index],
            part_count[:, span_index],
            part_tag[:, span_index],
        )

    device_total = span_part(0)
    for span_index in range(1, span_count):
        device_total = join_forward(device_total, span_part(span_index))
    identity = (
        jnp.zeros((row_count, local_width), jnp.float32),
        jnp.zeros((row_count, local_width), jnp.float32),
        jnp.zeros((row_count,), jnp.float32),
        jnp.full((row_count,), -1.0, jnp.float32),
    )
    state = carry_forward(device_total, identity)
    prefixes = []
    for span_index in range(span_count):
        prefixes.append(state)
        state = join_forward(state, span_part(span_index))
    prefix_keys = jnp.stack([entry[0] for entry in prefixes], axis=1)
    prefix_values = jnp.stack([entry[1] for entry in prefixes], axis=1)
    prefix_count = jnp.stack([entry[2] for entry in prefixes], axis=1)
    prefix_tag = jnp.stack([entry[3] for entry in prefixes], axis=1)
    divisor = jnp.maximum(prefix_count, 1.0)[:, :, None]
    bar_shape = (row_count, span_count, head_count, HEAD_DIM)
    key_bar = (prefix_keys / divisor).astype(jnp.bfloat16).reshape(bar_shape)
    value_bar = (prefix_values / divisor).astype(jnp.bfloat16).reshape(bar_shape)
    position = jnp.arange(SPAN)
    causal = position[:, None] >= position[None, :]
    diagonal = position[:, None] == position[None, :]
    local_ok = (
        causal[None, None]
        & (doc_span[:, :, :, None] == doc_span[:, :, None, :])
        & (alive[:, :, None, :] | diagonal[None, None])
    )
    local_ok = local_ok[:, :, None]
    summary_ok = (doc_float == prefix_tag[:, :, None]) & (prefix_count > 0.0)[:, :, None]
    summary_ok = summary_ok[:, :, None, :]

    def span_scores():
        local_scores = jnp.einsum(
            "rsthd,rsuhd->rshtu", query_spans, key_spans, preferred_element_type=jnp.float32
        )
        summary_scores = jnp.einsum(
            "rsthd,rshd->rsht", query_spans, key_bar, preferred_element_type=jnp.float32
        ) + math.log(SPAN)
        return (
            jnp.where(local_ok, local_scores, masked_score),
            jnp.where(summary_ok, summary_scores, masked_score),
        )

    local_scores, summary_scores = span_scores()
    top_score = jnp.maximum(jnp.max(local_scores, axis=-1), summary_scores)
    local_exp = jnp.exp(local_scores - top_score[..., None])
    summary_exp = jnp.exp(summary_scores - top_score)
    total_exp = jnp.sum(local_exp, axis=-1) + summary_exp
    local_prob = (local_exp / total_exp[..., None]).astype(jnp.bfloat16)
    summary_prob = (summary_exp / total_exp).astype(jnp.bfloat16)
    mixed_heads = jnp.einsum(
        "rshtu,rsuhd->rsthd", local_prob, value_spans, preferred_element_type=jnp.float32
    )
    mixed_heads = mixed_heads + jnp.einsum(
        "rsht,rshd->rsthd", summary_prob, value_bar, preferred_element_type=jnp.float32
    )
    heads_out = mixed_heads.reshape(token_total, local_width).astype(jnp.bfloat16)
    attention = lax.psum(jnp.dot(heads_out, w_out, preferred_element_type=jnp.float32), "head")
    x_mid = x_flat + attention
    normed2, norm2_back = jax.vjp(layer_norm, x_mid, ln2_gain, ln2_shift)
    hidden2 = normed2.astype(jnp.bfloat16)
    up_proj = jnp.dot(hidden2, w_up, preferred_element_type=jnp.float32) + b_up
    activation, gelu_back = jax.vjp(gelu_exact, up_proj)
    act_rounded = activation.astype(jnp.bfloat16)
    branch = lax.psum(jnp.dot(act_rounded, w_down, preferred_element_type=jnp.float32), "head")
    result = x_mid + branch + b_down
    out = result.astype(jnp.bfloat16).reshape(row_count, region_len, width)
    grad_top = out_grad.reshape(token_total, width).astype(jnp.float32)
    grad_b_down = jnp.sum(grad_top, axis=0)
    grad_branch = grad_top.astype(jnp.bfloat16)
    grad_w_down = product_t(act_rounded, grad_branch)
    grad_act = product_nt(grad_branch, w_down)
    grad_up = gelu_back(grad_act)[0].astype(jnp.bfloat16)
    grad_b_up = jnp.sum(grad_up, axis=0, dtype=jnp.float32)
    grad_w_up = product_t(hidden2, grad_up)
    grad_normed2 = lax.psum(product_nt(grad_up, w_up), "head")
    grad_mid_norm, grad_ln2_gain, grad_ln2_shift = norm2_back(grad_normed2)
    grad_mid = grad_top + grad_mid_norm
    grad_attn = grad_mid.astype(jnp.bfloat16)
    grad_w_out = product_t(heads_out, grad_attn)
    grad_heads = product_nt(grad_attn, w_out).astype(jnp.bfloat16)
    grad_spans = grad_heads.reshape(span_shape)
    local_scores, summary_scores = span_scores()
    local_exp = jnp.exp(local_scores - top_score[..., None])
    summary_exp = jnp.exp(summary_scores - top_score)
    local_full = local_exp / total_exp[..., None]
    summary_full = summary_exp / total_exp
    local_prob = local_full.astype(jnp.bfloat16)
    summary_prob = summary_full.astype(jnp.bfloat16)
    grad_local_p = jnp.einsum(
        "rsthd,rsuhd->rshtu", grad_spans, value_spans, preferred_element_type=jnp.float32
    )
    grad_summary_p = jnp.einsum(
        "rsthd,rshd->rsht", grad_spans, value_bar, preferred_element_type=jnp.float32
    )
    weighted = jnp.sum(local_full * grad_local_p, axis=-1) + summary_full * grad_summary_p
    grad_local_s = (local_full * (grad_local_p - weighted[..., None])).astype(jnp.bfloat16)
    grad_summary_s = (summary_full * (grad_summary_p - weighted)).astype(jnp.bfloat16)
    grad_query = jnp.einsum(
        "rshtu,rsuhd->rsthd", grad_local_s, key_spans, preferred_element_type=jnp.float32
    )
    grad_query = grad_query + jnp.einsum(
        "rsht,rshd->rsthd", grad_summary_s, key_bar, preferred_element_type=jnp.float32
    )
    grad_query = (grad_query.astype(jnp.bfloat16) * score_scale).reshape(token_total, local_width)
    grad_key_bar = jnp.einsum(
        "rsht,rsthd->rshd", grad_summary_s, query_spans, preferred_element_type=jnp.float32
    )
    grad_value_bar = jnp.einsum(
        "rsht,rsthd->rshd", summary_prob, grad_spans, preferred_element_type=jnp.float32
    )
    share_keys = grad_key_bar.reshape(row_count, span_count, local_width) / divisor
    share_values = grad_value_bar.reshape(row_count, span_count, local_width) / divisor
    grad_keys = jnp.einsum(
        "rshtu,rsthd->rsuhd", grad_local_s, query_spans, preferred_element_type=jnp.float32
    )
    grad_values = jnp.einsum(
        "rshtu,rsthd->rsuhd", local_prob, grad_spans, preferred_element_type=jnp.float32
    )

    def span_grad(span_index):
        return (share_keys[:, span_index], share_values[:, span_index], prefix_tag[:, span_index])

    device_back = span_grad(span_count - 1)
    for span_index in reversed(range(span_count - 1)):
        device_back = join_back(device_back, span_grad(span_index))
    back_identity = (
        jnp.zeros((row_count, local_width), jnp.float32),
        jnp.zeros((row_count, local_width), jnp.float32),
        jnp.full((row_count,), -1.0, jnp.float32),
    )
    state = carry_back(device_back, back_identity)
    suffixes = [None] * span_count
    for span_index in reversed(range(span_count)):
        suffixes[span_index] = state
        state = join_back(state, span_grad(span_index))
    after_keys = jnp.stack([entry[0] for entry in suffixes], axis=1)
    after_values = jnp.stack([entry[1] for entry in suffixes], axis=1)
    after_tag = jnp.stack([entry[2] for entry in suffixes], axis=1)
    receives = ((doc_float == after_tag[:, :, None]) & alive).astype(jnp.float32)[..., None]
    grad_keys = (
        grad_keys.reshape(row_count, span_count, SPAN, local_width)
        + receives * after_keys[:, :, None, :]
    )
    grad_values = (
        grad_values.reshape(row_count, span_count, SPAN, local_width)
        + receives * after_values[:, :, None, :]
    )
    grad_keys = grad_keys.astype(jnp.bfloat16).reshape(token_total, local_width)
    grad_values = grad_values.astype(jnp.bfloat16).reshape(token_total, local_width)
    grad_w_query = product_t(hidden1, grad_query)
    grad_w_key = product_t(hidden1, grad_keys)
    grad_w_value = product_t(hidden1, grad_values)
    grad_normed1 = (
        product_nt(grad_query, w_query)
        + product_nt(grad_keys, w_key)
        + product_nt(grad_values, w_value)
    )
    grad_normed1 = lax.psum(grad_normed1, "head")
    grad_in_norm, grad_ln1_gain, grad_ln1_shift = norm1_back(grad_normed1)
    grad_inputs = (grad_mid + grad_in_norm).reshape(row_count, region_len, width)
    (
        grad_w_up,
        grad_b_up,
        grad_w_down,
        grad_b_down,
        grad_ln2_gain,
        grad_ln2_shift,
        grad_w_query,
        grad_w_key,
        grad_w_value,
        grad_w_out,
        grad_ln1_gain,
        grad_ln1_shift,
    ) = lax.psum(
        (
            grad_w_up,
            grad_b_up,
            grad_w_down,
            grad_b_down,
            grad_ln2_gain,
            grad_ln2_shift,
            grad_w_query,
            grad_w_key,
            grad_w_value,
            grad_w_out,
            grad_ln1_gain,
            grad_ln1_shift,
        ),
        "seq",
    )
    return (
        out,
        grad_inputs,
        grad_ln1_gain,
        grad_ln1_shift,
        grad_w_query,
        grad_w_key,
        grad_w_value,
        grad_w_out,
        grad_ln2_gain,
        grad_ln2_shift,
        grad_w_up,
        grad_b_up,
        grad_w_down,
        grad_b_down,
    )


def solution(mesh):
    in_specs = (
        P(None, "seq", None),
        P(None, "seq"),
        P(None, "seq"),
        P(),
        P(),
        P(None, "head"),
        P(None, "head"),
        P(None, "head"),
        P("head", None),
        P(),
        P(),
        P(None, "head"),
        P("head"),
        P("head", None),
        P(),
        P(None, "seq", None),
    )
    out_specs = (
        P(None, "seq", None),
        P(None, "seq", None),
        P(),
        P(),
        P(None, "head"),
        P(None, "head"),
        P(None, "head"),
        P("head", None),
        P(),
        P(),
        P(None, "head"),
        P("head"),
        P("head", None),
        P(),
    )
    return jax.shard_map(
        on_device, mesh=mesh, in_specs=in_specs, out_specs=out_specs, check_vma=False
    )
```

profile of v0, /device:TPU:0, one launch (start us, length us, event | category | flops | bytes accessed | tf_op | source)
XLA Modules:
  0.0 888.7 jit_solution(1478527586491654071)
XLA Ops:
  7.4 2.0 convert_reduce_fusion
  9.3 2.3 fusion.16
  14.0 10.9 %all-gather.2 = f32[8,1,2]{2,1,0:T(1,128)} all-gather(f32[1,1,2]{2,1,0:T(1,128)S(1)} %get-tuple-element.673), channel_id=1, replica_groups=mesh['seq'=8,'head'=4] {'seq'}, dimensions={0}, use_global_device_ids=true | all-gather | bytes 72 | tf_op jit(solution)/shard_map/all_gather | solution.py:18
  24.9 9.6 %all-gather.1 = f32[8,1,2]{2,1,0:T(1,128)} all-gather(f32[1,1,2]{2,1,0:T(1,128)S(1)} %get-tuple-element.674), channel_id=1, replica_groups=mesh['seq'=8,'head'=4] {'seq'}, dimensions={0}, use_global_device_ids=true | all-gather | bytes 72 | tf_op jit(solution)/shard_map/all_gather | solution.py:18
  38.4 9.2 %all_gather.31 = f32[8,2,128]{2,1,0:T(2,128)} all-gather(f32[1,2,128]{2,1,0:T(2,128)S(1)} %fusion.99), channel_id=1, replica_groups=mesh['seq'=8,'head'=4] {'seq'}, dimensions={0}, use_global_device_ids=true | all-gather | bytes 9216 | tf_op jit(solution)/shard_map/all_gather | solution.py:18
  50.0 8.8 all_gather.32
  58.8 26.2 %while.40 = (s32[]{:T(128)}, f32[2,128]{1,0:T(2,128)}, f32[2,128]{1,0:T(2,128)}, f32[2]{0:T(128)}, f32[2]{0:T(128)}, /*index=5*/s32[]{:T(128)}, f32[8,2]{1,0:T(8...) while((s32[]{:T(128)}, f32[2,128]{1,0:T(2,128)}, ...), condition=%wide.region_5.6_spmd.clone, body=%wide.region_4.5_spmd.clone.sunk | while | flops 2586 | bytes 6367 | solution.py:31
  98.5 2.1 fusion.26
  115.3 2.9 copy.286
  118.2 3.5 copy.313
  121.7 2.9 copy.287
  148.0 3.5 fusion.173
  151.8 138.3 %all-reduce.9.cloned.1.call-done = f32[1792,512]{1,0:T(8,128)} async-done(((f32[1792,512]{1,0:T(8,128)}), f32[1792,512]{1,0:T(8,128)}) %all-reduce.9.cloned.1.call-update) | async-done | bytes 3670032 | tf_op jit(solution)/shard_map/psum | solution.py:219
  290.0 2.5 fusion.158
  296.9 11.2 %convert_reduce_fusion.2 = (f32[512]{0:T(512)}, bf16[1792,512]{1,0:T(8,128)(2,1)S(1)}, f32[1792,512]{1,0:T(8,128)}) fusion(f32[1792,512]{1,0:T(8,128)S(1)} %convolution_add_fusion, bf16[1792,512]{1,0:T(8,128)(2,1)S(1)} %bitcast.530, bf16[512,512]{1,0:T(8,128)(2,1)S(1)} %copy-done), kind=kOutput, calls=%fused_computation.49 | convolution fusion | flops 1007418880 | bytes 11536384 | tf_op jit(solution)/shard_map/dot_general | solution.py:80
  309.3 3.0 fusion.175
  315.6 14.4 %all-reduce = f32[16]{0:T(128)S(1)} all-reduce(f32[16]{0:T(128)S(1)} %select_dynamic-update-slice_fusion), channel_id=2, replica_groups=mesh['seq'=8,'head'=4] {'seq'}, use_global_device_ids=true, to_apply=%add | all-reduce | flops 16 | bytes 128
  333.1 4.1 multiply_convert_fusion
  338.6 2.9 fusion.174
  341.5 108.2 %all-reduce.11.cloned.1.call-done = f32[1792,512]{1,0:T(8,128)} async-done(((f32[1792,512]{1,0:T(8,128)}), f32[1792,512]{1,0:T(8,128)}) %all-reduce.11.cloned.1.call-update) | async-done | bytes 3670032 | tf_op jit(solution)/shard_map/psum | solution.py:237
  449.7 5.0 multiply_reduce_fusion
  455.1 1.9 fusion.157
  462.0 2.9 copy.324
  465.1 3.6 multiply_reduce_fusion.3
  470.9 8.9 all_gather.36
  479.8 9.0 %all_gather.37 = f32[8,2,128]{2,1,0:T(2,128)S(1)} all-gather(f32[1,2,128]{2,1,0:T(2,128)S(1)} %fusion.69), channel_id=1, replica_groups=mesh['seq'=8,'head'=4] {'seq'}, dimensions={0}, use_global_device_ids=true | all-gather | bytes 9216 | tf_op jit(solution)/shard_map/all_gather | solution.py:18
  488.8 11.6 %while.41 = (s32[]{:T(128)}, f32[2,128]{1,0:T(2,128)S(1)}, f32[2,128]{1,0:T(2,128)S(1)}, f32[2]{0:T(128)S(1)}, s32[]{:T(128)}, /*index=5*/f32[8,2]{1,0:T(8,128)}...) while((s32[]{:T(128)}, f32[2,128]{1,0:T(2,128)S(1)}, ...), condition=%wide.region_16.17_spmd.clone, body=%wide.region_15.16_spmd.clone.sunk | while | flops 2582 | bytes 6398 | solution.py:31
  502.1 2.7 multiply_convert_fusion.1
  504.9 1.7 convolution_bitcast_fusion.1
  517.2 1.9 copy.331
  531.2 3.6 add_convert_fusion.3
  538.7 2.5 add_add_fusion.3
  541.6 2.0 convert_reduce_fusion.1
  543.6 1.8 fusion.19
  545.4 2.1 fusion.181
  547.5 2.1 fusion.182
  553.9 2.8 fusion.180
  556.6 2.9 fusion.177
  562.3 234.3 %all-reduce.15.cloned.1.call-done = (f32[1792,512]{1,0:T(8,128)}, f32[1792,512]{1,0:T(8,128)}) async-done(((f32[1792,512]{1,0:T(8,128)}, f32[1792,512]{1,0:T(8,128)}), (f32[1792,512]{1,0:T(8,128)}, f32[1792,512]{1,0:T(8,128)})) %all-reduce.15.cloned.1.call-update) | async-done | bytes 7340048 | tf_op jit(solution)/shard_map/psum | solution.py:226
  796.7 3.3 fusion.133
  800.1 1.9 fusion.15
  802.1 24.9 %all-reduce.1 = (f32[512]{0:T(512)}, f32[512]{0:T(512)}, f32[512]{0:T(512)}, f32[512]{0:T(512)}, f32[512]{0:T(512)}, /*index=5*/f32[512]{0:T(512)}) all-reduce(f32[512]{0:T(512)S(1)} %get-tuple-element.505, f32[512]{0:T(512)S(1)} %get-tuple-element.508, f32[512]{0:T(512)S(1)} %copy-done.114, ...), channel_id=1, replica_groups=mesh['seq'=8,'head'=4] {'seq'}, use_global_device_ids=true, to_apply=%region_21.22 | all-reduce | flops 3072 | bytes 24576 | tf_op jit(solution)/shard_map/psum | solution.py:336
  827.0 5.7 add_convert_fusion.1
  833.7 3.3 add_add_fusion.2
  837.0 34.7 %all-reduce.13.cloned.1.call-done = (f32[512,128]{1,0:T(8,128)}, f32[512,128]{1,0:T(8,128)}, f32[512,128]{1,0:T(8,128)}, f32[128,512]{1,0:T(8,128)}, f32[512,512]{1,0:T(8,128)}, /*index=5*/f32[512,512]{1,0:T(8,128)}) async-done(((f32[512,128]{1,0:T(8,128)}, f32[512,128]{1,0:T(8,128)}, f32[512,128]{1,0:T(8,128)}, f32[128,512]{1,0:T(8,128)}, f32[512,512]{1,0:T(8,128)}, /*index=5*/f32[512,512]{1,0:T(8,128)}), ...) | async-done | bytes 3145744 | tf_op jit(solution)/shard_map/psum | solution.py:336
  871.7 1.8 copy.482
  876.8 1.7 copy.485
  878.5 2.3 copy.486
  (597 shorter events, 158.1 us)
Async XLA Ops:
  7.2 288.8 %copy-start = (bf16[512,512]{1,0:T(8,128)(2,1)S(1)}, bf16[512,512]{1,0:T(8,128)(2,1)}, u32[]{:S(2)}) copy-start(bf16[512,512]{1,0:T(8,128)(2,1)} %param.33) | copy-start | bytes 1572868
  7.2 28.4 %copy-start.4 = (bf16[2,896,512]{2,1,0:T(8,128)(2,1)S(1)}, bf16[2,896,512]{2,1,0:T(8,128)(2,1)}, u32[]{:S(2)}) copy-start(bf16[2,896,512]{2,1,0:T(8,128)(2,1)} %param.20) | copy-start | bytes 5505028
  7.2 28.4 %copy-start.71 = (f32[512]{0:T(512)S(1)}, f32[512]{0:T(512)}, u32[]{:S(2)}) copy-start(f32[512]{0:T(512)} %param.23) | copy-start | bytes 6148
  7.2 28.4 %copy-start.112 = (f32[512]{0:T(512)S(1)}, f32[512]{0:T(512)}, u32[]{:S(2)}) copy-start(f32[512]{0:T(512)} %param.24) | copy-start | bytes 6148
  7.3 282.8 %all-reduce.9.cloned.1.call-start = ((), (), s32[]{:S(2)}) async-start(), calls=%async_computation | async-start | bytes 7340032 | tf_op jit(solution)/shard_map/psum | solution.py:219
  7.3 29.6 %copy-start.47 = (bf16[512,128]{1,0:T(8,128)(2,1)S(1)}, bf16[512,128]{1,0:T(8,128)(2,1)}, u32[]{:S(2)}) copy-start(bf16[512,128]{1,0:T(8,128)(2,1)} %param.26) | copy-start | bytes 393220
  11.6 36.0 %copy-start.41 = (bf16[512,128]{1,0:T(8,128)(2,1)S(1)}, bf16[512,128]{1,0:T(8,128)(2,1)}, u32[]{:S(2)}) copy-start(bf16[512,128]{1,0:T(8,128)(2,1)} %param.27) | copy-start | bytes 393220
  12.3 23.2 %copy-start.78 = (pred[2,896]{1,0:T(4,128)(4,1)}, pred[2,896]{1,0:T(4,128)(4,1)S(1)}, u32[]{:S(2)}) copy-start(pred[2,896]{1,0:T(4,128)(4,1)S(1)} %broadcast_compare_fusion.2) | copy-start | bytes 5380
  12.3 23.1 %copy-start.75 = (pred[2,7,128]{2,1,0:T(8,128)(4,1)}, pred[2,7,128]{2,1,0:T(8,128)(4,1)S(1)}, u32[]{:S(2)}) copy-start(pred[2,7,128]{2,1,0:T(8,128)(4,1)S(1)} %eq.245) | copy-start | bytes 5380
  13.3 24.6 %copy-start.54 = (pred[2,7,128]{2,1,0:T(8,128)(4,1)}, pred[2,7,128]{2,1,0:T(8,128)(4,1)S(1)}, u32[]{:S(2)}) copy-start(pred[2,7,128]{2,1,0:T(8,128)(4,1)S(1)} %get-tuple-element.657) | copy-start | bytes 5380
  13.6 23.2 %copy-start.146 = (f32[2]{0:T(128)}, f32[2]{0:T(128)S(1)}, u32[]{:S(2)}) copy-start(f32[2]{0:T(128)S(1)} %get-tuple-element.514) | copy-start | bytes 28
  13.6 23.2 %copy-start.147 = (f32[2]{0:T(128)}, f32[2]{0:T(128)S(1)}, u32[]{:S(2)}) copy-start(f32[2]{0:T(128)S(1)} %get-tuple-element.516) | copy-start | bytes 28
  13.6 23.2 %copy-start.148 = (f32[2]{0:T(128)}, f32[2]{0:T(128)S(1)}, u32[]{:S(2)}) copy-start(f32[2]{0:T(128)S(1)} %get-tuple-element.517) | copy-start | bytes 28
  13.6 23.2 %copy-start.149 = (f32[2]{0:T(128)}, f32[2]{0:T(128)S(1)}, u32[]{:S(2)}) copy-start(f32[2]{0:T(128)S(1)} %get-tuple-element.518) | copy-start | bytes 28
  13.6 23.2 %copy-start.150 = (f32[2]{0:T(128)}, f32[2]{0:T(128)S(1)}, u32[]{:S(2)}) copy-start(f32[2]{0:T(128)S(1)} %get-tuple-element.519) | copy-start | bytes 28
  13.6 23.2 %copy-start.151 = (f32[2]{0:T(128)}, f32[2]{0:T(128)S(1)}, u32[]{:S(2)}) copy-start(f32[2]{0:T(128)S(1)} %get-tuple-element.520) | copy-start | bytes 28
  14.0 22.9 %copy-start.126 = (f32[2]{0:T(128)}, f32[2]{0:T(128)S(1)}, u32[]{:S(2)}) copy-start(f32[2]{0:T(128)S(1)} %get-tuple-element.530) | copy-start | bytes 28
  14.0 22.9 %copy-start.127 = (f32[2]{0:T(128)}, f32[2]{0:T(128)S(1)}, u32[]{:S(2)}) copy-start(f32[2]{0:T(128)S(1)} %get-tuple-element.531) | copy-start | bytes 28
  14.0 22.9 %copy-start.128 = (f32[2]{0:T(128)}, f32[2]{0:T(128)S(1)}, u32[]{:S(2)}) copy-start(f32[2]{0:T(128)S(1)} %get-tuple-element.532) | copy-start | bytes 28
  14.0 22.9 %copy-start.129 = (f32[2]{0:T(128)}, f32[2]{0:T(128)S(1)}, u32[]{:S(2)}) copy-start(f32[2]{0:T(128)S(1)} %get-tuple-element.533) | copy-start | bytes 28
  37.6 60.9 %copy-start.45 = (bf16[512,128]{1,0:T(8,128)(2,1)S(1)}, bf16[512,128]{1,0:T(8,128)(2,1)}, u32[]{:S(2)}) copy-start(bf16[512,128]{1,0:T(8,128)(2,1)} %param.25) | copy-start | bytes 393220
  87.8 30.4 %copy-start.83 = (f32[2]{0:T(128)}, f32[2]{0:T(128)S(1)}, u32[]{:S(2)}) copy-start(f32[2]{0:T(128)S(1)} %get-tuple-element.615) | copy-start | bytes 28
  87.8 30.4 %copy-start.87 = (f32[2]{0:T(128)}, f32[2]{0:T(128)S(1)}, u32[]{:S(2)}) copy-start(f32[2]{0:T(128)S(1)} %get-tuple-element.614) | copy-start | bytes 28
  87.8 30.4 %copy-start.90 = (f32[2]{0:T(128)}, f32[2]{0:T(128)S(1)}, u32[]{:S(2)}) copy-start(f32[2]{0:T(128)S(1)} %get-tuple-element.612) | copy-start | bytes 28
  87.8 30.4 %copy-start.93 = (f32[2]{0:T(128)}, f32[2]{0:T(128)S(1)}, u32[]{:S(2)}) copy-start(f32[2]{0:T(128)S(1)} %get-tuple-element.613) | copy-start | bytes 28
  87.8 30.4 %copy-start.103 = (f32[2]{0:T(128)}, f32[2]{0:T(128)S(1)}, u32[]{:S(2)}) copy-start(f32[2]{0:T(128)S(1)} %get-tuple-element.611) | copy-start | bytes 28
  87.9 30.4 %copy-start.132 = (f32[2]{0:T(128)}, f32[2]{0:T(128)S(1)}, u32[]{:S(2)}) copy-start(f32[2]{0:T(128)S(1)} %get-tuple-element.610) | copy-start | bytes 28
  100.7 23.9 %copy-start.66 = (pred[128,128]{0,1:T(8,128)(4,1)S(1)}, pred[128,128]{0,1:T(8,128)(4,1)}, u32[]{:S(2)}) copy-start(pred[128,128]{0,1:T(8,128)(4,1)} %get-tuple-element.700) | copy-start | bytes 49156
  100.7 23.9 %copy-start.67 = (pred[128,128]{0,1:T(8,128)(4,1)S(1)}, pred[128,128]{0,1:T(8,128)(4,1)}, u32[]{:S(2)}) copy-start(pred[128,128]{0,1:T(8,128)(4,1)} %get-tuple-element.701) | copy-start | bytes 49156
  126.0 376.1 %copy-start.29 = (pred[2,7,128,128]{2,3,1,0:T(8,128)(4,1)}, pred[2,7,128,128]{2,3,1,0:T(8,128)(4,1)S(1)}, u32[]{:S(2)}) copy-start(pred[2,7,128,128]{2,3,1,0:T(8,128)(4,1)S(1)} %or_and_fusion) | copy-start | bytes 688132
  151.6 298.2 %all-reduce.11.cloned.1.call-start = ((), (), s32[]{:S(2)}) async-start(), calls=%async_computation.1 | async-start | bytes 7340032 | tf_op jit(solution)/shard_map/psum | solution.py:237
  312.5 484.2 %all-reduce.15.cloned.1.call-start = ((), (), s32[]{:S(2)}) async-start(), calls=%async_computation.3 | async-start | bytes 14680064 | tf_op jit(solution)/shard_map/psum | solution.py:226
  465.0 23.8 %copy-start.63 = (f32[2]{0:T(128)S(1)}, f32[2]{0:T(128)}, u32[]{:S(2)}) copy-start(f32[2]{0:T(128)} %custom-call.6) | copy-start | bytes 28
  465.0 23.8 %copy-start.64 = (f32[2,128]{1,0:T(2,128)S(1)}, f32[2,128]{1,0:T(2,128)}, u32[]{:S(2)}) copy-start(f32[2,128]{1,0:T(2,128)} %custom-call.5) | copy-start | bytes 3076
  465.0 23.8 %copy-start.65 = (f32[2,128]{1,0:T(2,128)S(1)}, f32[2,128]{1,0:T(2,128)}, u32[]{:S(2)}) copy-start(f32[2,128]{1,0:T(2,128)} %custom-call.4) | copy-start | bytes 3076
  465.0 35.4 %copy-start.105 = (f32[2]{0:T(128)S(1)}, f32[2]{0:T(128)}, u32[]{:S(2)}) copy-start(f32[2]{0:T(128)} %copy-done.103) | copy-start | bytes 28
  465.1 35.4 %copy-start.134 = (f32[2]{0:T(128)S(1)}, f32[2]{0:T(128)}, u32[]{:S(2)}) copy-start(f32[2]{0:T(128)} %copy-done.132) | copy-start | bytes 28
  465.1 35.4 %copy-start.92 = (f32[2]{0:T(128)S(1)}, f32[2]{0:T(128)}, u32[]{:S(2)}) copy-start(f32[2]{0:T(128)} %copy-done.90) | copy-start | bytes 28
  465.1 35.4 %copy-start.95 = (f32[2]{0:T(128)S(1)}, f32[2]{0:T(128)}, u32[]{:S(2)}) copy-start(f32[2]{0:T(128)} %copy-done.93) | copy-start | bytes 28
  465.1 35.4 %copy-start.89 = (f32[2]{0:T(128)S(1)}, f32[2]{0:T(128)}, u32[]{:S(2)}) copy-start(f32[2]{0:T(128)} %copy-done.87) | copy-start | bytes 28
  465.1 35.4 %copy-start.85 = (f32[2]{0:T(128)S(1)}, f32[2]{0:T(128)}, u32[]{:S(2)}) copy-start(f32[2]{0:T(128)} %copy-done.83) | copy-start | bytes 28
  465.1 36.8 %copy-start.144 = (pred[2]{0:T(512)(128)(4,1)S(1)}, pred[2]{0:T(512)(128)(4,1)}, u32[]{:S(2)}) copy-start(pred[2]{0:T(512)(128)(4,1)} %get-tuple-element.609) | copy-start | bytes 10
  541.2 330.5 %all-reduce.13.cloned.1.call-start = ((), (), s32[]{:S(2)}) async-start(), calls=%async_computation.2 | async-start | bytes 6291456 | tf_op jit(solution)/shard_map/psum | solution.py:336
  562.3 237.7 %copy-start.62 = (f32[1792]{0:T(1024)S(1)}, f32[1792]{0:T(1024)}, u32[]{:S(2)}) copy-start(f32[1792]{0:T(1024)} %copy-done.61) | copy-start | bytes 21508
  562.3 237.7 %copy-start.53 = (f32[1792]{0:T(1024)S(1)}, f32[1792]{0:T(1024)}, u32[]{:S(2)}) copy-start(f32[1792]{0:T(1024)} %copy-done.52) | copy-start | bytes 21508
  800.0 27.0 %copy-start.160 = (f32[512]{0:T(512)S(1)}, f32[512]{0:T(512)}, u32[]{:S(2)}) copy-start(f32[512]{0:T(512)} %param.34) | copy-start | bytes 6148
  800.1 32.6 %copy-start.60 = (f32[1792]{0:T(1024)S(1)}, f32[1792]{0:T(1024)}, u32[]{:S(2)}) copy-start(f32[1792]{0:T(1024)} %copy-done.59) | copy-start | bytes 21508
  833.7 48.0 %copy-start.1 = (bf16[512,512]{1,0:T(8,128)(2,1)S(1)}, bf16[512,512]{1,0:T(8,128)(2,1)}, u32[]{:S(2)}) copy-start(bf16[512,512]{1,0:T(8,128)(2,1)} %param.33) | copy-start | bytes 1572868
  (120 other events, 612.0 us)
Sparse Core Ops, SparseCore 0:
  151.7 138.3 all-reduce.8
  312.6 137.0 all-reduce.10
  541.4 255.2 all-reduce.14
  801.6 70.0 all-reduce.12
where the time goes:
time: 899 us; the launch traced here: 889 us
  waiting for transfers between devices  516 us (57%)
  local copies, waits for them, and re-layouts  107 us (12%)
  other arithmetic  96.3 us (11%)
  blocking collectives  95.7 us (11%)
  matrix products  56.3 us (6%)
  between operations  17.1 us (2%)
    psum x1, waiting for transfers between devices, on_device(): lax.psum(jnp.dot(act_rounded, w_down, preferred_element_type=jnp.float32)...  234 us
    psum x1, waiting for transfers between devices, on_device(): lax.psum(jnp.dot(heads_out, w_out, preferred_element_type=jnp.float32), '...  138 us
    psum x1, waiting for transfers between devices, on_device(): grad_normed2 = lax.psum(product_nt(grad_up, w_up), 'head')  108 us
    all_gather x6, blocking collectives, entering(): everything = jax.tree.map(lambda part: lax.all_gather(part, axis), value)  56.4 us
    unnamed x370, local copies, waits for them, and re-layouts  42.3 us
    psum x1, waiting for transfers between devices, on_device(): lax.psum((grad_w_up, grad_b_up, grad_w_down, grad_b_down, grad_ln2_gain,...  34.7 us
    select_n x32, other arithmetic, lap(): return jax.tree.map(lambda a, b: jnp.where(reached, a, b), new, before)  26.9 us
    psum x1, blocking collectives, on_device(): lax.psum((grad_w_up, grad_b_up, grad_w_down, grad_b_down, grad_ln2_gain,...  24.9 us
  transfers between devices with their start and end apart: 4, of which 4 were waited for; matrix products, arithmetic and copies ran while one was open for 5% of the time, Pallas kernels for 0%

commit v1 on v0

v1 whole, which is shorter than its diff:
```python
import math

import jax
import jax.numpy as jnp
from jax import lax
from jax.experimental import pallas as pl
from jax.experimental.pallas import tpu as pltpu
from jax.sharding import PartitionSpec as P

HEAD_DIM = 64
SPAN = 128
LANES = 128
NORM_EPS = 1e-05
MASKED = -1e30
VMEM_BYTES = 56 * 2**20
f32, bf16 = jnp.float32, jnp.bfloat16


def nn(a, b):
    return lax.dot_general(a, b, (((1,), (0,)), ((), ())), preferred_element_type=f32)


def nt(a, b):
    return lax.dot_general(a, b, (((1,), (1,)), ((), ())), preferred_element_type=f32)


def tn(a, b):
    return lax.dot_general(a, b, (((0,), (0,)), ((), ())), preferred_element_type=f32)


def hi_lo(v):
    hi = v.astype(bf16).astype(f32)
    return jnp.concatenate([hi, v - hi], axis=0).astype(bf16)


def twice(v):
    return jnp.concatenate([v, v], axis=0).astype(bf16)


def norm_parts(x):
    mean = jnp.mean(x, axis=-1, keepdims=True)
    centred = x - mean
    rstd = lax.rsqrt(jnp.mean(centred * centred, axis=-1, keepdims=True) + NORM_EPS)
    return centred * rstd, rstd


def norm_back(y, xhat, rstd):
    return rstd * (
        y
        - jnp.mean(y, axis=-1, keepdims=True)
        - xhat * jnp.mean(y * xhat, axis=-1, keepdims=True)
    )


def gelu_parts(u):
    z = jnp.abs(u)
    t = 1.0 / (1.0 + (0.3275911 * math.sqrt(0.5)) * z)
    e = jnp.exp(-0.5 * u * u)
    poly = t * (
        0.5 * 0.254829592
        + t
        * (
            0.5 * -0.284496736
            + t * (0.5 * 1.421413741 + t * (0.5 * -1.453152027 + t * (0.5 * 1.061405429)))
        )
    )
    tail = poly * e
    phi = jnp.where(u >= 0.0, 1.0 - tail, tail)
    return phi, phi + u * e * (1.0 / math.sqrt(2.0 * math.pi))


def call(body, grid, prefetch, in_specs, out_specs, out_shape, scratch=(), flops=0, nbytes=0):
    return pl.pallas_call(
        body,
        grid_spec=pltpu.PrefetchScalarGridSpec(
            num_scalar_prefetch=prefetch,
            grid=grid,
            in_specs=in_specs,
            out_specs=out_specs,
            scratch_shapes=list(scratch),
        ),
        out_shape=out_shape,
        compiler_params=pltpu.CompilerParams(vmem_limit_bytes=VMEM_BYTES),
        cost_estimate=pl.CostEstimate(flops=flops, bytes_accessed=nbytes, transcendentals=0),
    )


def whole(shape):
    return pl.BlockSpec(shape, lambda *_: (0,) * len(shape))


def shape(dims, dtype):
    return jax.ShapeDtypeStruct(dims, dtype)


def project_body(spans, doc_s, doc_ref, pad_ref, x_ref, g_ref, b_ref, w_ref, h_ref, q_ref, k_ref, v_ref, m_ref, p_ref):
    row_at = pl.program_id(0)
    width = x_ref.shape[-1]
    xhat, _ = norm_parts(x_ref[...].astype(f32))
    h = (xhat * g_ref[...] + b_ref[...]).astype(bf16)
    h_ref[...] = h
    q_ref[...] = (nn(h, w_ref[:, :width]) * (1.0 / math.sqrt(HEAD_DIM))).astype(bf16)
    k = nn(h, w_ref[:, width : 2 * width]).astype(bf16)
    v = nn(h, w_ref[:, 2 * width :]).astype(bf16)
    k_ref[...] = k
    v_ref[...] = v
    doc = doc_ref[0]
    alive = pad_ref[0] == 1
    rows, region = m_ref.shape[1:]
    lane = lax.broadcasted_iota(jnp.int32, (rows, region), 1)
    line = lax.broadcasted_iota(jnp.int32, (rows, region), 0)
    tag_line = lax.broadcasted_iota(jnp.int32, (rows, LANES), 0)
    picked = jnp.zeros((rows, region), f32)
    tag = jnp.zeros((rows, LANES), f32)
    for s in range(1, spans + 1):
        last = doc_s[row_at, s * SPAN - 1]
        hit = (line == s) & (lane < s * SPAN) & (doc == last) & alive
        picked = jnp.where(hit, 1.0, picked)
        tag = jnp.where(tag_line == s, last.astype(f32), tag)
    m_ref[0] = picked
    mb = picked.astype(bf16)
    p_ref[0, :, :width] = nn(mb, k)
    p_ref[0, :, width : 2 * width] = nn(mb, v)
    p_ref[0, :, 2 * width : 3 * width] = nn(mb, h)
    count = jnp.sum(picked, axis=1, keepdims=True)
    p_ref[0, :, 3 * width : 3 * width + LANES] = jnp.broadcast_to(count, (rows, LANES))
    p_ref[0, :, 3 * width + LANES :] = tag


def project(docs, pads, x, gain, shift, w, rows, region):
    tokens, width = x.shape
    spans = region // SPAN
    lines = -(-(spans + 1) // 8) * 8
    wide = 3 * width + 2 * LANES
    tok = pl.BlockSpec((region, width), lambda i, *_: (i, 0))
    ids = pl.BlockSpec((1, 1, region), lambda i, *_: (i, 0, 0))

    def body(*refs):
        project_body(spans, *refs)

    return call(
        body,
        (rows,),
        1,
        [ids, ids, tok, whole((1, width)), whole((1, width)), whole(w.shape)],
        [
            tok,
            tok,
            tok,
            tok,
            pl.BlockSpec((1, lines, region), lambda i, *_: (i, 0, 0)),
            pl.BlockSpec((1, lines, wide), lambda i, *_: (i, 0, 0)),
        ],
        [shape((tokens, width), bf16)] * 4
        + [shape((rows, lines, region), f32), shape((rows, lines, wide), f32)],
        flops=2 * tokens * width * 3 * width,
        nbytes=12 * tokens * width,
    )(docs, docs[:, None], pads[:, None], x, gain[None], shift[None], w)


def halves():
    lane = lax.broadcasted_iota(jnp.int32, (1, LANES), 1)
    first = (lane < HEAD_DIM).astype(f32)
    return first.astype(bf16), (1.0 - first).astype(bf16)


def split(v, masks):
    return jnp.concatenate([v * masks[0], v * masks[1]], axis=0)


def local_body(doc_ref, pad_ref, q_ref, k_ref, v_ref, e_ref, o_ref, top_ref, sum_ref):
    doc = doc_ref[0].astype(f32)
    code = jnp.where(pad_ref[0] == 1, doc, -2.0)
    code_u = jnp.broadcast_to(code, (SPAN, SPAN)).T
    u = lax.broadcasted_iota(jnp.int32, (SPAN, SPAN), 0)
    t = lax.broadcasted_iota(jnp.int32, (SPAN, SPAN), 1)
    ok = ((u < t) & (code_u == doc)) | (u == t)
    masks = halves()
    for pair in range(q_ref.shape[-1] // LANES):
        lanes = slice(pair * LANES, (pair + 1) * LANES)
        scores = nt(split(k_ref[:, lanes], masks), q_ref[:, lanes])
        parts = []
        for half in range(2):
            head = 2 * pair + half
            s = jnp.where(ok, scores[half * SPAN : (half + 1) * SPAN], MASKED)
            top = jnp.max(s, axis=0, keepdims=True)
            e = jnp.exp(s - top)
            top_ref[0, head : head + 1, :] = top
            sum_ref[0, head : head + 1, :] = jnp.sum(e, axis=0, keepdims=True)
            parts.append(e.astype(bf16))
        both = jnp.concatenate(parts, axis=0)
        e_ref[0, pair * 2 * SPAN : (pair + 1) * 2 * SPAN, :] = both
        o_ref[:, lanes] = tn(both, split(v_ref[:, lanes], masks))


def local_attention(docs3, pads3, q, k, v):
    tokens, width = q.shape
    count = tokens // SPAN
    heads = width // HEAD_DIM
    ids = pl.BlockSpec((1, 1, SPAN), lambda i: (i, 0, 0))
    tok = pl.BlockSpec((SPAN, width), lambda i: (i, 0))
    per_head = pl.BlockSpec((1, heads, SPAN), lambda i: (i, 0, 0))
    return call(
        local_body,
        (count,),
        0,
        [ids, ids, tok, tok, tok],
        [pl.BlockSpec((1, heads * SPAN, SPAN), lambda i: (i, 0, 0)), tok, per_head, per_head],
        [shape((count, heads * SPAN, SPAN), bf16), shape((tokens, width), f32)]
        + [shape((count, heads, SPAN), f32)] * 2,
        flops=8 * tokens * SPAN * width,
        nbytes=12 * tokens * width,
    )(docs3, pads3, q, k, v)


def head_rows(rows, width):
    line = lax.broadcasted_iota(jnp.int32, (rows, width), 0)
    lane = lax.broadcasted_iota(jnp.int32, (rows, width), 1)
    return lane // HEAD_DIM == line


def merge_body(
    spans, me_s, doc_s, every_ref, p_ref, doc_ref, q_ref, o_ref, top_ref, sum_ref, x_ref, w_ref,
    heads_ref, mid_ref, kb_ref, vb_ref, scale_ref, ps_ref, misc_ref,
):
    row_at = pl.program_id(0)
    me = me_s[0]
    devices = every_ref.shape[0]
    width = q_ref.shape[-1]
    heads = width // HEAD_DIM
    at_count = 3 * width
    at_tag = at_count + LANES

    carry = jnp.zeros((1, at_tag), f32)
    tag_in = jnp.full((1, LANES), -1.0, f32)
    run = carry
    run_tag = tag_in
    for d in range(1, devices):
        before = every_ref[d - 1, row_at]
        tag = before[:, at_tag:]
        same = (tag == run_tag).astype(f32)[:, :1]
        run = before[:, :at_tag] + same * run
        run_tag = tag
        mine = me == d
        carry = jnp.where(mine, run, carry)
        tag_in = jnp.where(mine, tag, tag_in)

    own = head_rows(heads, width)
    spread = twice(own.astype(f32))
    for s in range(spans):
        toks = slice(s * SPAN, (s + 1) * SPAN)
        if s == 0:
            run_doc = tag_in
        else:
            run_doc = jnp.full((1, LANES), doc_s[row_at, s * SPAN - 1].astype(f32))
        flag = (tag_in == run_doc).astype(f32)
        total = p_ref[0, s : s + 1, :at_tag] + flag[:, :1] * carry
        count = total[:, at_count:]
        divisor = jnp.maximum(count, 1.0)
        k_bar = total[:, :width] / divisor[:, :1]
        v_bar = total[:, width : 2 * width] / divisor[:, :1]
        k_bd = jnp.where(own, k_bar, 0.0).astype(bf16)
        v_bd = jnp.where(own, v_bar, 0.0).astype(bf16)
        kb_ref[s] = k_bd
        vb_ref[s] = v_bd
        present = (doc_ref[s].astype(f32) == run_doc) & (count > 0.0)
        scores = nt(k_bd, q_ref[toks]) + math.log(SPAN)
        scores = jnp.where(present, scores, MASKED)
        top_local = top_ref[s]
        top = jnp.maximum(top_local, scores)
        scale = jnp.exp(top_local - top)
        weight = jnp.exp(scores - top)
        inverse = 1.0 / (scale * sum_ref[s] + weight)
        scale = scale * inverse
        weight = weight * inverse
        scale_ref[s] = scale
        ps_ref[s] = weight
        misc_ref[s] = jnp.concatenate([1.0 / divisor, flag], axis=0)
        mixed = o_ref[toks] * tn(hi_lo(scale), spread) + tn(weight.astype(bf16), v_bd)
        heads_ref[toks] = mixed.astype(bf16)
    mid_ref[...] = x_ref[...].astype(f32) + nn(heads_ref[...], w_ref[...])


def merge(me, docs, docs3, every, prefix, q, o_local, top, total, x, w_out, rows, region):
    tokens, width = q.shape
    spans = region // SPAN
    heads = width // HEAD_DIM
    count = tokens // SPAN
    tok = pl.BlockSpec((region, width), lambda i, *_: (i, 0))
    ids = pl.BlockSpec((spans, 1, SPAN), lambda i, *_: (i, 0, 0))
    per_head = pl.BlockSpec((spans, heads, SPAN), lambda i, *_: (i, 0, 0))
    bars = pl.BlockSpec((spans, heads, width), lambda i, *_: (i, 0, 0))

    def body(*refs):
        merge_body(spans, *refs)

    return call(
        body,
        (rows,),
        2,
        [
            whole(every.shape),
            pl.BlockSpec((1,) + prefix.shape[1:], lambda i, *_: (i, 0, 0)),
            ids, tok, tok, per_head, per_head, tok, whole(w_out.shape),
        ],
        [tok, tok, bars, bars, per_head, per_head, pl.BlockSpec((spans, 2, SPAN), lambda i, *_: (i, 0, 0))],
        [
            shape((tokens, width), bf16),
            shape((tokens, width), f32),
            shape((count, heads, width), bf16),
            shape((count, heads, width), bf16),
            shape((count, heads, SPAN), f32),
            shape((count, heads, SPAN), f32),
            shape((count, 2, SPAN), f32),
        ],
        flops=2 * tokens * width * width,
        nbytes=14 * tokens * width,
    )(me, docs, every, prefix, docs3, q, o_local, top, total, x, w_out)


def ffn_body(
    at_s, mid_ref, g_ref, heads_ref, gain_ref, shift_ref, wu_ref, bu_ref, wd_ref, bd_ref, wo_ref,
    out_ref, dmid_ref, do_ref, gwu_ref, gwd_ref, gwo_ref, gbu_ref, small_ref, y_acc, dn_acc,
):
    groups = wu_ref.shape[0]

    @pl.when(pl.program_id(0) == 0)
    def _():
        gwu_ref[...] = jnp.zeros_like(gwu_ref)
        gwd_ref[...] = jnp.zeros_like(gwd_ref)
        gwo_ref[...] = jnp.zeros_like(gwo_ref)
        gbu_ref[...] = jnp.zeros_like(gbu_ref)
        small_ref[...] = jnp.zeros_like(small_ref)

    xhat, _ = norm_parts(mid_ref[...])
    h = (xhat * gain_ref[...] + shift_ref[...]).astype(bf16)
    y_acc[...] = jnp.zeros_like(y_acc)
    dn_acc[...] = jnp.zeros_like(dn_acc)

    def hidden(j, _):
        gm = g_ref[...]
        up = nn(h, wu_ref[j]) + bu_ref[j]
        phi, slope = gelu_parts(up)
        a = (up * phi).astype(bf16)
        y_acc[...] += nn(a, wd_ref[j])
        du = (nt(gm, wd_ref[j]) * slope).astype(bf16)
        dn_acc[...] += nt(du, wu_ref[j])

        @pl.when(j == at_s[0])
        def _():
            gwd_ref[...] += tn(a, gm)
            gwu_ref[...] += tn(h, du)
            gbu_ref[...] += jnp.sum(du.astype(f32), axis=0, keepdims=True)

        return 0

    lax.fori_loop(0, groups, hidden, 0)
    mid = mid_ref[...]
    out_ref[...] = (mid + y_acc[...] + bd_ref[...]).astype(bf16)
    xhat, rstd = norm_parts(mid)
    g = g_ref[...].astype(f32)
    dn = dn_acc[...]
    small_ref[0:1] += jnp.sum(dn * xhat, axis=0, keepdims=True)
    small_ref[1:2] += jnp.sum(dn, axis=0, keepdims=True)
    small_ref[2:3] += jnp.sum(g, axis=0, keepdims=True)
    dmid = g + norm_back(dn * gain_ref[...], xhat, rstd)
    dmid_ref[...] = dmid
    gx = dmid.astype(bf16)
    do_ref[...] = nt(gx, wo_ref[...]).astype(bf16)
    gwo_ref[...] += tn(heads_ref[...], gx)


def feed_forward(at, mid, g, heads_out, gain, shift, wu, bu, wd, bd, wo, block):
    tokens, width = mid.shape
    groups, _, hidden = wu.shape
    chunk = tokens // 4
    tok = pl.BlockSpec((chunk, width), lambda i, *_: (i, 0))
    fixed = whole
    return call(
        ffn_body,
        (4,),
        1,
        [
            tok, tok,
            pl.BlockSpec((chunk, block), lambda i, s: (i, s[1])),
            fixed((1, width)), fixed((1, width)), fixed(wu.shape), fixed((groups, 1, hidden)), fixed(wd.shape),
            fixed((1, width)), fixed(wo.shape),
        ],
        [tok, tok, tok, fixed((width, hidden)), fixed((hidden, width)), fixed((block, width)),
         fixed((1, hidden)), fixed((8, width))],
        [
            shape((tokens, width), bf16),
            shape((tokens, width), f32),
            shape((tokens, width), bf16),
            shape((width, hidden), f32),
            shape((hidden, width), f32),
            shape((block, width), f32),
            shape((1, hidden), f32),
            shape((8, width), f32),
        ],
        scratch=[pltpu.VMEM((chunk, width), f32)] * 2,
        flops=8 * tokens * width * hidden * groups,
        nbytes=16 * tokens * width,
    )(at, mid, g, heads_out, gain[None], shift[None], wu, bu.reshape(groups, 1, hidden), wd, bd[None], wo)


def back_body(
    spans, q_ref, k_ref, v_ref, do_ref, e_ref, scale_ref, ps_ref, kb_ref, vb_ref, m_ref, misc_ref,
    dq_ref, dk_ref, dv_ref, g_ref, shares,
):
    s = spans - 1 - pl.program_id(1)
    width = q_ref.shape[-1]

    @pl.when(pl.program_id(1) == 0)
    def _():
        shares[...] = jnp.zeros_like(shares)
        g_ref[...] = jnp.zeros_like(g_ref)

    masks = halves()
    own = head_rows(width // HEAD_DIM, width)
    later = hi_lo(shares[...])
    reach = twice(m_ref[0])
    do_all = do_ref[...]
    weight = ps_ref[0]
    dp_sum = nt(vb_ref[0], do_all)
    r_rows = []
    for pair in range(width // LANES):
        lanes = slice(pair * LANES, (pair + 1) * LANES)
        q, k, v, do = q_ref[:, lanes], k_ref[:, lanes], v_ref[:, lanes], do_ref[:, lanes]
        dp = nt(split(v, masks), do)
        probs, grads = [], []
        for half in range(2):
            head = 2 * pair + half
            p = e_ref[0, head * SPAN : (head + 1) * SPAN, :].astype(f32) * scale_ref[0, head : head + 1, :]
            dp_head = dp[half * SPAN : (half + 1) * SPAN]
            r = jnp.sum(p * dp_head, axis=0, keepdims=True)
            r = r + weight[head : head + 1] * dp_sum[head : head + 1]
            r_rows.append(r)
            probs.append(p.astype(bf16))
            grads.append((p * (dp_head - r)).astype(bf16))
        dv = nn(jnp.concatenate(probs, axis=1), split(do, masks))
        dk = nn(jnp.concatenate(grads, axis=1), split(q, masks))
        dq_ref[:, lanes] = tn(jnp.concatenate(grads, axis=0), split(k, masks)).astype(bf16)
        wide = slice(width + pair * LANES, width + (pair + 1) * LANES)
        dk_ref[:, lanes] = (dk + tn(reach, later[:, lanes])).astype(bf16)
        dv_ref[:, lanes] = (dv + tn(reach, later[:, wide])).astype(bf16)
    ds_sum = (weight * (dp_sum - jnp.concatenate(r_rows, axis=0))).astype(bf16)
    dq = dq_ref[...].astype(f32) + tn(ds_sum, kb_ref[0])
    dq_ref[...] = (dq.astype(bf16).astype(f32) * (1.0 / math.sqrt(HEAD_DIM))).astype(bf16)
    inverse = misc_ref[0, 0:1, :1]
    flag = misc_ref[0, 1:2, :1]
    gk = jnp.sum(jnp.where(own, nn(ds_sum, q_ref[...]), 0.0), axis=0, keepdims=True) * inverse
    gv = jnp.sum(jnp.where(own, nn(weight.astype(bf16), do_all), 0.0), axis=0, keepdims=True) * inverse
    shares[pl.ds(s, 1), :width] = gk
    shares[pl.ds(s, 1), width:] = gv
    g_ref[0, :, :width] += flag * gk
    g_ref[0, :, width:] += flag * gv


def attention_back(q, k, v, do, e, scale, ps, kb, vb, m, misc, rows, region):
    tokens, width = q.shape
    spans = region // SPAN
    heads = width // HEAD_DIM
    lines = m.shape[1]

    def at(r, i):
        return r * spans + spans - 1 - i

    tok = pl.BlockSpec((SPAN, width), lambda r, i: (at(r, i), 0))
    per_head = pl.BlockSpec((1, heads, SPAN), lambda r, i: (at(r, i), 0, 0))
    bars = pl.BlockSpec((1, heads, width), lambda r, i: (at(r, i), 0, 0))

    def body(*refs):
        back_body(spans, *refs)

    return call(
        body,
        (rows, spans),
        0,
        [
            tok, tok, tok, tok,
            pl.BlockSpec((1, heads * SPAN, SPAN), lambda r, i: (at(r, i), 0, 0)),
            per_head, per_head, bars, bars,
            pl.BlockSpec((1, lines, SPAN), lambda r, i: (r, 0, spans - 1 - i)),
            pl.BlockSpec((1, 2, SPAN), lambda r, i: (at(r, i), 0, 0)),
        ],
        [tok, tok, tok, pl.BlockSpec((1, 1, 2 * width), lambda r, i: (r, 0, 0))],
        [shape((tokens, width), bf16)] * 3 + [shape((rows, 1, 2 * width), f32)],
        scratch=[pltpu.VMEM((lines, 2 * width), f32)],
        flops=16 * tokens * SPAN * width,
        nbytes=20 * tokens * width,
    )(q, k, v, do, e, scale, ps, kb, vb, m, misc)


def weights_body(h_ref, dq_ref, dk_ref, dv_ref, o_ref):
    @pl.when(pl.program_id(0) == 0)
    def _():
        o_ref[...] = jnp.zeros_like(o_ref)

    h = h_ref[...]
    for i, ref in enumerate((dq_ref, dk_ref, dv_ref)):
        o_ref[i] += tn(h, ref[...])


def weight_grads(at, h, dq, dk, dv, block):
    tokens, width = h.shape
    chunk = tokens // 2
    mine = pl.BlockSpec((chunk, block), lambda i, s: (i, s[1]))

    def body(at_s, *refs):
        weights_body(*refs)

    return call(
        body,
        (2,),
        1,
        [pl.BlockSpec((chunk, width), lambda i, *_: (i, 0)), mine, mine, mine],
        whole((3, width, block)),
        shape((3, width, block), f32),
        flops=6 * tokens * width * block,
        nbytes=2 * tokens * (width + 3 * block),
    )(at, h, dq, dk, dv)


def input_body(
    spans, me_s, every_ref, back_ref, m_ref, x_ref, gain_ref, dmid_ref, dq_ref, dk_ref, dv_ref, w_ref,
    gi_ref, small_ref, in_ref,
):
    row_at = pl.program_id(0)
    me = me_s[0]
    devices = every_ref.shape[0]
    width = x_ref.shape[-1]
    at_tag = 3 * width + LANES

    @pl.when(row_at == 0)
    def _():
        small_ref[...] = jnp.zeros_like(small_ref)

    run = jnp.zeros((1, 2 * width), f32)
    mine = run
    in_ref[0, devices - 1 : devices, :] = run
    tag = every_ref[devices - 1, row_at][:, at_tag:]
    for d in reversed(range(devices - 1)):
        tag_here = every_ref[d, row_at][:, at_tag:]
        same = (tag == tag_here).astype(f32)[:, :1]
        run = back_ref[d + 1, row_at] + same * run
        tag = tag_here
        in_ref[0, d : d + 1, :] = run
        mine = jnp.where(me == d, run, mine)

    lines = m_ref.shape[1]
    arrived = jnp.broadcast_to(mine, (8, 2 * width))
    through = nt(hi_lo(arrived), w_ref[:, width:])
    through = through[0:8] + through[8:16]
    line = lax.broadcasted_iota(jnp.int32, (lines, width), 0)
    through = jnp.where(line == spans, jnp.broadcast_to(through[:1], (lines, width)), 0.0)
    dn = (
        nt(dq_ref[...], w_ref[:, :width])
        + nt(dk_ref[...], w_ref[:, width : 2 * width])
        + nt(dv_ref[...], w_ref[:, 2 * width :])
        + tn(twice(m_ref[0]), hi_lo(through))
    )
    xhat, rstd = norm_parts(x_ref[...].astype(f32))
    small_ref[0:1] += jnp.sum(dn * xhat, axis=0, keepdims=True)
    small_ref[1:2] += jnp.sum(dn, axis=0, keepdims=True)
    gi_ref[...] = dmid_ref[...] + norm_back(dn * gain_ref[...], xhat, rstd)


def input_grads(me, every, back, m, x, gain, dmid, dq, dk, dv, w, rows, region):
    tokens, width = x.shape
    devices = every.shape[0]
    tok = pl.BlockSpec((region, width), lambda i, *_: (i, 0))

    def body(*refs):
        input_body(region // SPAN, *refs)

    return call(
        body,
        (rows,),
        1,
        [
            whole(every.shape), whole(back.shape),
            pl.BlockSpec((1,) + m.shape[1:], lambda i, *_: (i, 0, 0)),
            tok, whole((1, width)), tok, tok, tok, tok, whole(w.shape),
        ],
        [tok, whole((8, width)), pl.BlockSpec((1, devices, 2 * width), lambda i, *_: (i, 0, 0))],
        [shape((tokens, width), f32), shape((8, width), f32), shape((rows, devices, 2 * width), f32)],
        flops=6 * tokens * width * width,
        nbytes=16 * tokens * width,
    )(me, every, back, m, x, gain[None], dmid, dq, dk, dv, w)


def narrow_body(w_ref, o_ref):
    o_ref[...] = w_ref[...].astype(bf16)


def narrow(w):
    lines, width = w.shape
    chunk = lines // 4
    block = pl.BlockSpec((chunk, width), lambda i: (i, 0))
    return call(narrow_body, (4,), 0, [block], block, shape(w.shape, bf16), nbytes=6 * w.size)(w)


def side_by_side(every, parts):
    groups, width, wide = every.shape
    share = wide // parts
    if share % LANES:
        flat = narrow(every.reshape(groups * width, wide)).reshape(groups, width, parts, share)
        return flat.transpose(1, 2, 0, 3).reshape(width, parts * groups * share)

    def body(w_ref, o_ref):
        o_ref[...] = w_ref[0].astype(bf16)

    return call(
        body,
        (parts, groups),
        0,
        [pl.BlockSpec((1, width, share), lambda p, g: (g, 0, p))],
        pl.BlockSpec((width, share), lambda p, g: (0, p * groups + g)),
        shape((width, parts * groups * share), bf16),
        nbytes=6 * every.size,
    )(every)


def spread_weights(part, devices, here):
    rows = part.shape[0] // devices
    mine = lax.dynamic_slice_in_dim(part, here * rows, rows, 0).astype(f32)
    return lax.all_gather(mine, ("head", "seq"), tiled=True)


def on_device(
    inputs, doc_ids, pad_mask, ln1_gain, ln1_shift, w_query, w_key, w_value, w_out,
    ln2_gain, ln2_shift, w_up, b_up, w_down, b_down, out_grad,
):
    rows, region, width = inputs.shape
    tokens = rows * region
    devices = lax.axis_size("seq")
    groups = lax.axis_size("head")
    here = lax.axis_index("seq")
    group = lax.axis_index("head")
    share = width // groups
    block = max(share, LANES)
    me = here.astype(jnp.int32)[None]
    at = jnp.stack([group, group * share // block]).astype(jnp.int32)

    w_in = spread_weights(jnp.concatenate([w_query, w_key, w_value], axis=1), devices, here)
    w_in = side_by_side(w_in.reshape(groups, width, 3 * share), 3)
    wo = narrow(spread_weights(w_out, devices, here))
    wu = narrow(spread_weights(w_up, devices, here)).reshape((groups,) + w_up.shape)
    wd = narrow(spread_weights(w_down, devices, here)).reshape((groups,) + w_down.shape)
    bu = lax.all_gather(b_up, "head")

    x = inputs.reshape(tokens, width)
    g = out_grad.reshape(tokens, width)
    docs3 = doc_ids.reshape(tokens // SPAN, 1, SPAN)
    pads3 = pad_mask.reshape(tokens // SPAN, 1, SPAN)

    h1, q, k, v, m, prefix = project(doc_ids, pad_mask, x, ln1_gain, ln1_shift, w_in, rows, region)
    spans = region // SPAN
    every = lax.all_gather(prefix[:, spans : spans + 1], "seq")
    e, o_local, top, total = local_attention(docs3, pads3, q, k, v)
    heads_out, mid, kb, vb, scale, ps, misc = merge(
        me, doc_ids, docs3, every, prefix, q, o_local, top, total, x, wo, rows, region
    )
    out, dmid, do, gwu, gwd, gwo, gbu, small2 = feed_forward(
        at, mid, g, heads_out, ln2_gain, ln2_shift, wu, bu, wd, b_down, wo, block
    )
    dq, dk, dv, g_back = attention_back(q, k, v, do, e, scale, ps, kb, vb, m, misc, rows, region)
    back = lax.all_gather(g_back, "seq")
    gw = weight_grads(at, h1, dq, dk, dv, block)
    grad_inputs, small1, arrived = input_grads(
        me, every, back, m, x, ln1_gain, dmid, dq, dk, dv, w_in, rows, region
    )

    gwu, gwd, gwo, gbu, small2 = lax.psum((gwu, gwd, gwo, gbu, small2), "seq")
    gw = lax.psum(gw, "seq")
    small1 = lax.psum(small1, "seq")
    picked = every[:, :, 0, 2 * width : 3 * width].transpose(1, 0, 2).reshape(rows * devices, width)
    arrived = arrived.reshape(rows * devices, 2, width)
    arrived = lax.dynamic_slice_in_dim(arrived, at[1] * block, block, 2)
    late = jnp.einsum("nc,nie->ice", picked, arrived, precision=lax.Precision.HIGHEST)
    gw = gw + jnp.concatenate([jnp.zeros_like(late[:1]), late], axis=0)
    if block != share:
        inner = group * share - at[1] * block
        gw = lax.dynamic_slice_in_dim(gw, inner, share, 2)
        gwo = lax.dynamic_slice_in_dim(gwo, inner, share, 0)
    return (
        out.reshape(rows, region, width),
        grad_inputs.reshape(rows, region, width),
        small1[0],
        small1[1],
        gw[0],
        gw[1],
        gw[2],
        gwo,
        small2[0],
        small2[1],
        gwu,
        gbu[0],
        gwd,
        small2[2],
    )


def solution(mesh):
    tok = P(None, "seq", None)
    ids = P(None, "seq")
    cols, lines = P(None, "head"), P("head", None)
    in_specs = (
        tok, ids, ids, P(), P(), cols, cols, cols, lines, P(), P(), cols, P("head"), lines, P(), tok,
    )
    out_specs = (
        tok, tok, P(), P(), cols, cols, cols, lines, P(), P(), cols, P("head"), lines, P(),
    )
    return jax.shard_map(on_device, mesh=mesh, in_specs=in_specs, out_specs=out_specs, check_vma=False)
```

time: 899 us -> 410 us (0.46)
  waiting for transfers between devices: 516 us -> 182 us
  Pallas kernels: 0 us -> 131 us
  local copies, waits for them, and re-layouts: 107 us -> 12 us
  other arithmetic: 96.3 us -> 7.66 us
  matrix products: 56.3 us -> 0.62 us
  blocking collectives: 95.7 us -> 60.6 us
    psum x4 -> x1, waiting for transfers between devices: 516 us -> 20.1 us  [on_device(): gw = lax.psum(gw, 'seq')]
    all_gather x0 -> x4, waiting for transfers between devices: none -> 162 us  [spread_weights(): return lax.all_gather(mine, ('head', 'seq'), tiled=True)]
    pallas_call x0 -> x11, Pallas kernels: none -> 131 us  [the longest x1 41.8 us: feed_forward(): call(ffn_body, (4,), 1, [tok, tok, pl.BlockSpec((chunk, block), lambda i,...]
    dot_general x30 -> x1, matrix products: 56.3 us -> 0.62 us  [on_device(): jnp.einsum('nc,nie->ice', picked, arrived, precision=lax.Precision.HIGHEST)]
    unnamed x370 -> x16, local copies, waits for them, and re-layouts: 42.3 us -> 2.68 us
    select_n x38 -> x0, other arithmetic: 29.6 us -> none  [the longest x32 26.9 us: lap(): return jax.tree.map(lambda a, b: jnp.where(reached, a, b), new, before)]
    another operation x59 -> x0, local copies, waits for them, and re-layouts: 29 us -> none  [the longest x8 5.97 us: on_device(): prefix_keys = jnp.stack([entry[0] for entry in prefixes], axis=1)]
    reduce_sum x11 -> x0, other arithmetic: 22.1 us -> none  [the longest x3 10.2 us: layer_norm(): return centred * lax.rsqrt(spread + norm_eps) * norm_gain + norm_shift]
  transfers between devices with their start and end apart: 4 -> 5, of which waited for: 4 -> 5; matrix products, arithmetic and copies ran while one was open for 5% -> 3% of each run, Pallas kernels for 0% -> 15%
where the time goes in v1:
time: 410 us; the launch traced here: 408 us
  waiting for transfers between devices  182 us (44%)
  Pallas kernels  131 us (32%)
  blocking collectives  60.6 us (15%)
  between operations  13.9 us (3%)
  local copies, waits for them, and re-layouts  12 us (3%)
  other arithmetic  7.66 us (2%)
    all_gather x4, waiting for transfers between devices, spread_weights(): return lax.all_gather(mine, ('head', 'seq'), tiled=True)  162 us
    pallas_call x1, Pallas kernels, feed_forward(): call(ffn_body, (4,), 1, [tok, tok, pl.BlockSpec((chunk, block), lambda i,...  41.8 us
    psum x1, blocking collectives, on_device(): small1 = lax.psum(small1, 'seq')  25.1 us
    psum x1, waiting for transfers between devices, on_device(): gw = lax.psum(gw, 'seq')  20.1 us
    pallas_call x1, Pallas kernels, attention_back(): call(body, (rows, spans), 0, [tok, tok, tok, tok, pl.BlockSpec((1, heads...  19 us
    all_gather x1, blocking collectives, on_device(): bu = lax.all_gather(b_up, 'head')  15 us
    pallas_call x1, Pallas kernels, local_attention(): call(local_body, (count,), 0, [ids, ids, tok, tok, tok], [pl.BlockSpec((1...  14.8 us
    pallas_call x3, Pallas kernels, narrow(): call(narrow_body, (4,), 0, [block], block, shape(w.shape, bf16), nbytes=6...  11.7 us
  transfers between devices with their start and end apart: 5, of which 5 were waited for; matrix products, arithmetic and copies ran while one was open for 3% of the time, Pallas kernels for 15%

profile of v1, /device:TPU:0, one launch (start us, length us, event | category | flops | bytes accessed | tf_op | source)
XLA Modules:
  0.0 408.3 jit_solution(13188468143367666874)
XLA Ops:
  7.2 0.0 all-gather.11.cloned.1.call-start
  7.2 1.3 dynamic-slice_convert_fusion.2
  8.6 0.0 all-gather.11.cloned.1.call-update
  8.6 0.0 all-gather.9.cloned.1.call-start
  8.6 1.4 fusion.2
  10.1 0.0 all-gather.9.cloned.1.call-update
  10.1 0.0 all-gather.13.cloned.1.call-start
  10.1 1.5 dynamic-slice_convert_fusion.1
  11.6 0.0 all-gather.13.cloned.1.call-update
  11.7 0.0 all-gather.15.cloned.1.call-start
  11.7 1.5 dynamic-slice_convert_fusion
  13.2 0.0 all-gather.15.cloned.1.call-update
  13.2 0.0 all-reduce.5.cloned.1.call-start
  13.3 1.3 broadcast_in_dim.27.refs_1_
  14.6 1.3 reshape.66.doc_ref.refs_4_
  15.9 1.3 broadcast_in_dim.28.refs_2_
  17.2 1.3 reshape.67.pad_ref
  18.5 15.0 %all-gather.3.bu_ref = f32[4,1,512]{2,1,0:T(1,128)} all-gather(f32[1,1,512]{2,1,0:T(1,128)} %bitcast.55), channel_id=3, replica_groups=mesh['seq'=8,'head'=4] {'head'}, dimensions={0}, use_global_device_ids=true | all-gather | bytes 10240 | tf_op jit(solution)/shard_map/all_gather | solution.py:651
  33.5 0.6 pad_add_fusion.1.at_s
  34.1 33.7 %all-gather.11.cloned.1.call-done.w_ref = f32[512,512]{1,0:T(8,128)} async-done(((f32[16,512]{1,0:T(8,128)}), f32[512,512]{1,0:T(8,128)}) %all-gather.11.cloned.1.call-update) | async-done | bytes 1048592 | tf_op jit(solution)/shard_map/all_gather | solution.py:628
  67.8 3.3 shard_map.266.refs_10_.wo_ref
  71.1 58.1 %all-gather.9.cloned.1.call-done = f32[2048,384]{1,0:T(8,128)} async-done(((f32[64,384]{1,0:T(8,128)}), f32[2048,384]{1,0:T(8,128)}) %all-gather.9.cloned.1.call-update) | async-done | bytes 3145744 | tf_op jit(solution)/shard_map/all_gather | solution.py:628
  129.2 7.7 %shard_map.263.refs_6_.refs_10_ = bf16[512,1536]{1,0:T(8,128)(2,1)} custom-call(f32[4,512,384]{2,1,0:T(8,128)} %bitcast.45), custom_call_target="tpu_custom_call" | custom-call | bytes 4718592 | tf_op jit(solution)/shard_map/pallas_call | solution.py:614
  137.0 8.8 %shard_map.264 = (bf16[1792,512]{1,0:T(8,128)(2,1)}, bf16[1792,512]{1,0:T(8,128)(2,1)}, bf16[1792,512]{1,0:T(8,128)(2,1)}, bf16[1792,512]{1,0:T(8,128)(2,1)}, f3...) custom-call(s32[2,896]{1,0:T(2,128)} %refs_1_.1, s32[2,1,896]{2,1,0:T(1,128)} %broadcast_in_dim.27.refs_1_, ...), custom_call_target="tpu_custom_call" | custom-call | flops 2818572288 | bytes 11010048 | tf_op jit(solution)/shard_map/pallas_call | solution.py:141
  145.7 0.9 slice.30
  146.6 10.2 %all-gather = f32[16,1,1792]{2,1,0:T(1,128)} all-gather(f32[2,1,1792]{2,1,0:T(1,128)S(1)} %slice.30), channel_id=2, replica_groups=mesh['seq'=8,'head'=4] {'seq'}, dimensions={0}, use_global_device_ids=true | all-gather | bytes 129024 | tf_op jit(solution)/shard_map/all_gather | solution.py:660
  156.8 14.8 %shard_map.265 = (bf16[14,1024,128]{2,1,0:T(8,128)(2,1)}, f32[1792,512]{1,0:T(8,128)}, f32[14,8,128]{2,1,0:T(8,128)}, f32[14,8,128]{2,1,0:T(8,128)}) custom-call(s32[14,1,128]{2,1,0:T(1,128)} %reshape.66.doc_ref.refs_4_, s32[14,1,128]{2,1,0:T(1,128)} %reshape.67.pad_ref, bf16[1792,512]{1,0:T(8,128)(2,1)} %get-tuple-element.47.q_ref.refs_5_.refs_0_, ...), custom_call_target="tpu_custom_call" | custom-call | flops 939524096 | bytes 11010048 | tf_op jit(solution)/shard_map/pallas_call | solution.py:203
  171.6 11.3 %shard_map.267 = (bf16[1792,512]{1,0:T(8,128)(2,1)}, f32[1792,512]{1,0:T(8,128)}, bf16[14,8,512]{2,1,0:T(8,128)(2,1)}, bf16[14,8,512]{2,1,0:T(8,128)(2,1)}, f32[...) custom-call(s32[1]{0:T(128)} %bitcast.2.refs_0_, s32[2,896]{1,0:T(2,128)} %refs_1_.1, ...), custom_call_target="tpu_custom_call" | custom-call | flops 939524096 | bytes 12845056 | tf_op jit(solution)/shard_map/pallas_call | solution.py:297
  183.0 10.4 %all-gather.13.cloned.1.call-done.w_ref = f32[2048,512]{1,0:T(8,128)} async-done(((f32[64,512]{1,0:T(8,128)}), f32[2048,512]{1,0:T(8,128)}) %all-gather.13.cloned.1.call-update) | async-done | bytes 4194320 | tf_op jit(solution)/shard_map/all_gather | solution.py:628
  193.4 4.2 %shard_map.268 = bf16[2048,512]{1,0:T(8,128)(2,1)} custom-call(f32[2048,512]{1,0:T(8,128)} %all-gather.13.cloned.1.call-done.w_ref), custom_call_target="tpu_custom_call" | custom-call | bytes 6291456 | tf_op jit(solution)/shard_map/pallas_call | solution.py:601
  197.6 59.8 %all-gather.15.cloned.1.call-done.w_ref = f32[2048,512]{1,0:T(8,128)} async-done(((f32[64,512]{1,0:T(8,128)}), f32[2048,512]{1,0:T(8,128)}) %all-gather.15.cloned.1.call-update) | async-done | bytes 4194320 | tf_op jit(solution)/shard_map/all_gather | solution.py:628
  257.4 4.2 %shard_map.269 = bf16[2048,512]{1,0:T(8,128)(2,1)} custom-call(f32[2048,512]{1,0:T(8,128)} %all-gather.15.cloned.1.call-done.w_ref), custom_call_target="tpu_custom_call" | custom-call | bytes 6291456 | tf_op jit(solution)/shard_map/pallas_call | solution.py:601
  261.7 41.8 %shard_map.270 = (bf16[1792,512]{1,0:T(8,128)(2,1)}, f32[1792,512]{1,0:T(8,128)}, bf16[1792,512]{1,0:T(8,128)(2,1)}, f32[512,512]{1,0:T(8,128)}, f32[512,512]{1,...) custom-call(s32[2]{0:T(128)} %pad_add_fusion.1.at_s, f32[1792,512]{1,0:T(8,128)} %get-tuple-element.53.mid_ref, ...), custom_call_target="tpu_custom_call" | custom-call | flops 15032385536 | bytes 14680064 | tf_op jit(solution)/shard_map/pallas_call | solution.py:379
  303.5 19.0 %shard_map.271 = (bf16[1792,512]{1,0:T(8,128)(2,1)}, bf16[1792,512]{1,0:T(8,128)(2,1)}, bf16[1792,512]{1,0:T(8,128)(2,1)}, f32[2,1,1024]{2,1,0:T(1,128)}) custom-call(bf16[1792,512]{1,0:T(8,128)(2,1)} %get-tuple-element.47.q_ref.refs_5_.refs_0_, bf16[1792,512]{1,0:T(8,128)(2,1)} %get-tuple-element.48.k_ref.refs_1_, ...), custom_call_target="tpu_custom_call" | custom-call | flops 1879048192 | bytes 18350080 | tf_op jit(solution)/shard_map/pallas_call | solution.py:476
  322.5 4.9 %shard_map.273 = f32[3,512,128]{2,1,0:T(8,128)} custom-call(s32[2]{0:T(128)} %pad_add_fusion.1.at_s, bf16[1792,512]{1,0:T(8,128)(2,1)} %get-tuple-element.71.refs_0_, bf16[1792,512]{1,0:T(8,128)(2,1)} %get-tuple-element.66.refs_7_.refs_1_, bf16[1792,512]{1,0:T(8,128)(2,1)} %get-tuple-element.67.refs_8_.refs_2_, ...), custom_call_target="tpu_custom_call" | custom-call | flops 704643072 | bytes 3211264 | tf_op jit(solution)/shard_map/pallas_call | solution.py:513
  327.4 0.8 slice.42
  328.2 10.3 %all-gather.2 = f32[16,1,1024]{2,1,0:T(1,128)} all-gather(f32[2,1,1024]{2,1,0:T(1,128)S(1)} %copy-done.4), channel_id=4, replica_groups=mesh['seq'=8,'head'=4] {'seq'}, dimensions={0}, use_global_device_ids=true | all-gather | bytes 73728 | tf_op jit(solution)/shard_map/all_gather | solution.py:669
  338.6 10.9 %shard_map.272 = (f32[1792,512]{1,0:T(8,128)}, f32[8,512]{1,0:T(8,128)}, f32[2,8,1024]{2,1,0:T(8,128)}) custom-call(s32[1]{0:T(128)} %bitcast.2.refs_0_, f32[8,2,1,1792]{3,2,1,0:T(1,128)} %bitcast.50, f32[8,2,1,1024]{3,2,1,0:T(1,128)} %bitcast.51, f32[2,8,896]{2,1,0:T(8,128)} %get-tuple-element.62.refs_9_.refs_3_, bf16[1792,512]{1,0:T(8,128)(2,1)} %bitcast.44, ...), custom_call_target="tpu_custom_call" | custom-call | flops 2818572288 | bytes 14680064 | tf_op jit(solution)/shard_map/pallas_call | solution.py:577
  349.5 0.9 reshape.74
  350.4 25.1 %all-reduce.1 = (f32[8,512]{1,0:T(8,128)S(1)}, f32[8,512]{1,0:T(8,128)S(1)}, f32[512]{0:T(512)}) all-reduce(f32[8,512]{1,0:T(8,128)} %get-tuple-element.70, f32[8,512]{1,0:T(8,128)S(1)} %copy-done.3, f32[512]{0:T(512)S(1)} %bitcast.56), channel_id=1, replica_groups=mesh['seq'=8,'head'=4] {'seq'}, use_global_device_ids=true, to_apply=%region_0.1 | all-reduce | flops 8704 | bytes 69632 | tf_op jit(solution)/shard_map/psum | solution.py:677
  375.5 0.6 fusion.6
  376.1 0.6 convolution_bitcast_fusion
  376.8 20.1 %all-reduce.5.cloned.1.call-done = (f32[3,512,128]{2,1,0:T(8,128)}, f32[128,512]{1,0:T(8,128)}, f32[512,512]{1,0:T(8,128)}, f32[512,512]{1,0:T(8,128)}) async-done(((f32[3,512,128]{2,1,0:T(8,128)}, f32[128,512]{1,0:T(8,128)}, f32[512,512]{1,0:T(8,128)}, f32[512,512]{1,0:T(8,128)}), (f32[3,512,128]{2,1,0:T(8,128)}, f32[128,512]{1,0:T(8,128)}, f32[512,512]{1,0:T(8,128)}, ...) | async-done | bytes 3145744 | tf_op jit(solution)/shard_map/psum | solution.py:676
  396.9 1.3 pad_add_fusion
  398.2 0.9 slice_bitcast_fusion
  399.1 0.7 copy.53
  399.8 1.0 copy.54
  400.8 1.0 copy.55
  (15 shorter events, 0.1 us)
Async XLA Ops:
  7.2 60.7 %all-gather.11.cloned.1.call-start = ((), (), s32[]{:S(2)}) async-start(), calls=%async_computation.1 | async-start | bytes 1081344 | tf_op jit(solution)/shard_map/all_gather | solution.py:628
  8.6 120.6 %all-gather.9.cloned.1.call-start = ((), (), s32[]{:S(2)}) async-start(), calls=%async_computation | async-start | bytes 3244032 | tf_op jit(solution)/shard_map/all_gather | solution.py:628
  10.1 183.3 %all-gather.13.cloned.1.call-start = ((), (), s32[]{:S(2)}) async-start(), calls=%async_computation.2 | async-start | bytes 4325376 | tf_op jit(solution)/shard_map/all_gather | solution.py:628
  11.7 245.8 %all-gather.15.cloned.1.call-start = ((), (), s32[]{:S(2)}) async-start(), calls=%async_computation.3 | async-start | bytes 4325376 | tf_op jit(solution)/shard_map/all_gather | solution.py:628
  13.2 383.6 %all-reduce.5.cloned.1.call-start = ((), (), s32[]{:S(2)}) async-start(), calls=%async_computation.4 | async-start | bytes 6291456 | tf_op jit(solution)/shard_map/psum | solution.py:676
  327.4 0.8 copy-start.4
  338.6 11.8 %copy-start.3 = (f32[8,512]{1,0:T(8,128)S(1)}, f32[8,512]{1,0:T(8,128)}, u32[]{:S(2)}) copy-start(f32[8,512]{1,0:T(8,128)} %get-tuple-element.74) | copy-start | bytes 49156
  338.6 11.8 %copy-start.5 = (f32[1,512]{1,0:T(1,128)S(1)}, f32[1,512]{1,0:T(1,128)}, u32[]{:S(2)}) copy-start(f32[1,512]{1,0:T(1,128)} %get-tuple-element.76) | copy-start | bytes 6148
  396.9 2.2 copy-start.2
  396.9 2.9 copy-start.1
  398.2 2.6 copy-start
Sparse Core Ops, SparseCore 0:
  11.5 56.3 all-gather.10
  71.3 57.8 all-gather.8
  132.6 60.7 all-gather.12
  196.7 60.7 all-gather.14
  327.5 69.2 all-reduce.4

commit v2 on v1

v2 whole, which is shorter than its diff:
```python
import math

import jax
import jax.numpy as jnp
from jax import lax
from jax.experimental import pallas as pl
from jax.experimental.pallas import tpu as pltpu
from jax.sharding import PartitionSpec as P

HEAD_DIM = 64
SPAN = 128
LANES = 128
NORM_EPS = 1e-05
MASKED = -1e30
f32, bf16 = jnp.float32, jnp.bfloat16


def nn(a, b):
    return lax.dot_general(a, b, (((1,), (0,)), ((), ())), preferred_element_type=f32)


def nt(a, b):
    return lax.dot_general(a, b, (((1,), (1,)), ((), ())), preferred_element_type=f32)


def tn(a, b):
    return lax.dot_general(a, b, (((0,), (0,)), ((), ())), preferred_element_type=f32)


def hi_lo(v):
    hi = v.astype(bf16).astype(f32)
    return jnp.concatenate([hi, v - hi], axis=0).astype(bf16)


def twice(v):
    return jnp.concatenate([v, v], axis=0).astype(bf16)


def norm_parts(x):
    mean = jnp.mean(x, axis=-1, keepdims=True)
    centred = x - mean
    rstd = lax.rsqrt(jnp.mean(centred * centred, axis=-1, keepdims=True) + NORM_EPS)
    return centred * rstd, rstd


def norm_back(y, xhat, rstd):
    return rstd * (
        y
        - jnp.mean(y, axis=-1, keepdims=True)
        - xhat * jnp.mean(y * xhat, axis=-1, keepdims=True)
    )


def gelu_parts(u):
    z = jnp.abs(u)
    t = 1.0 / (1.0 + (0.3275911 * math.sqrt(0.5)) * z)
    e = jnp.exp(-0.5 * u * u)
    poly = t * (
        0.5 * 0.254829592
        + t
        * (
            0.5 * -0.284496736
            + t * (0.5 * 1.421413741 + t * (0.5 * -1.453152027 + t * (0.5 * 1.061405429)))
        )
    )
    tail = poly * e
    phi = jnp.where(u >= 0.0, 1.0 - tail, tail)
    return phi, phi + u * e * (1.0 / math.sqrt(2.0 * math.pi))


def call(body, grid, prefetch, in_specs, out_specs, out_shape, scratch=(), us=2, mib=56, aliases=None, after=()):
    first, last = prefetch + len(in_specs), prefetch + len(in_specs) + len(after)

    def only(*refs):
        body(*refs[:first], *refs[last:])

    kernel = pl.pallas_call(
        only,
        input_output_aliases=aliases or {},
        grid_spec=pltpu.PrefetchScalarGridSpec(
            num_scalar_prefetch=prefetch,
            grid=grid,
            in_specs=list(in_specs) + [pl.BlockSpec(memory_space=pl.ANY)] * len(after),
            out_specs=out_specs,
            scratch_shapes=list(scratch),
        ),
        out_shape=out_shape,
        compiler_params=pltpu.CompilerParams(vmem_limit_bytes=mib * 2**20),
        cost_estimate=pl.CostEstimate(flops=int(us * 1.1e9), bytes_accessed=int(us * 3.5e6), transcendentals=0),
    )
    return lambda *operands: kernel(*operands, *after)


def whole(shape):
    return pl.BlockSpec(shape, lambda *_: (0,) * len(shape))


def shape(dims, dtype):
    return jax.ShapeDtypeStruct(dims, dtype)


def halves():
    lane = lax.broadcasted_iota(jnp.int32, (1, LANES), 1)
    first = (lane < HEAD_DIM).astype(f32)
    return first.astype(bf16), (1.0 - first).astype(bf16)


def split(v, masks):
    return jnp.concatenate([v * masks[0], v * masks[1]], axis=0)


def head_lines(bars):
    line = lax.broadcasted_iota(jnp.int32, (8, LANES), 0)
    lane = lax.broadcasted_iota(jnp.int32, (8, LANES), 1)
    own = lane // HEAD_DIM == line
    lines = [jnp.where(own, bars[s : s + 1], 0.0) for s in range(bars.shape[0])]
    return jnp.concatenate(lines, axis=0).astype(bf16)


def eight(rows):
    return jnp.concatenate(rows + [jnp.zeros((8 - len(rows), rows[0].shape[1]), f32)], axis=0)


def diagonal(blocks, lines):
    zero = jnp.zeros_like(blocks[0])
    rows = [jnp.concatenate([b if i == j else zero for j in range(len(blocks))], axis=1) for i, b in enumerate(blocks)]
    rows += [jnp.zeros_like(rows[0])] * (lines - len(blocks))
    return jnp.concatenate(rows, axis=0).astype(bf16)


def shares_body(at_s, q_ref, k_ref, v_ref, a_ref):
    rows = q_ref.shape[0]
    for i, ref in enumerate((q_ref, k_ref, v_ref)):
        a_ref[i * rows : (i + 1) * rows] = ref[...].astype(f32)


def attention_share(at, wq, wk, wv, devices):
    width, share = wq.shape
    rows = width // devices
    spec = pl.BlockSpec((rows, share), lambda i, s: (s[0], 0))
    return call(
        shares_body, (1,), 1, [spec] * 3, whole((3 * rows, share)), shape((3 * rows, share), f32)
    )(at, wq, wk, wv)


def down_rows(device):
    return device % 4, device // 4 * 2 + device % 2


def hidden_body(at_s, u_ref, o_ref, b_ref, upper_ref, lower_ref, up_ref, down_ref):
    at = 0
    for ref in (u_ref, o_ref):
        up_ref[at : at + ref.shape[0]] = ref[...].astype(f32)
        at += ref.shape[0]
    up_ref[at:] = jnp.broadcast_to(b_ref[...], (8, b_ref.shape[1]))
    rows = upper_ref.shape[0]
    down_ref[:rows] = upper_ref[...].astype(f32)
    down_ref[rows:] = lower_ref[...].astype(f32)


def hidden_share(at, wu, wo, bu, wd, devices, after):
    width, hidden = wu.shape
    rows, lines, deep = width // devices, wo.shape[0] // devices, hidden // devices
    mine = lambda i, s: (s[0], 0)
    outs = [shape((rows + lines + 8, width), f32), shape((2 * deep, width), f32)]
    return call(
        hidden_body,
        (1,),
        1,
        [
            pl.BlockSpec((rows, hidden), mine),
            pl.BlockSpec((lines, width), mine),
            whole((1, hidden)),
            pl.BlockSpec((deep, width), lambda i, s: (down_rows(s[0])[0], 0)),
            pl.BlockSpec((deep, width), lambda i, s: (4 + down_rows(s[0])[1], 0)),
        ],
        [whole(v.shape) for v in outs],
        outs,
        after=after,
    )(at, wu, wo, bu[None], wd, wd)


def cat(groups, after=()):
    arrays, outs = [], []
    for group in groups:
        arrays += [v for v, _, _ in group]
        outs.append(shape((sum(n for _, _, n in group),) + group[0][0].shape[1:], f32))

    def body(*refs):
        ins, got = refs[: len(arrays)], 0
        for group, out in zip(groups, refs[len(arrays) :]):
            at = 0
            for _, first, n in group:
                out[at : at + n] = ins[got][first : first + n]
                at += n
                got += 1

    return call(body, (1,), 0, [whole(v.shape) for v in arrays], [whole(v.shape) for v in outs], outs, after=after)(*arrays)


def pile(parts, lines=None, after=()):
    lines = lines or parts[0].shape[0]
    rest = parts[0].shape[1:]
    zeros = (0,) * len(rest)

    def body(*refs):
        for i in range(len(parts)):
            refs[-1][i] = refs[i][...]

    return call(
        body,
        (1,),
        0,
        [pl.BlockSpec((lines,) + rest, lambda i: (0,) + zeros)] * len(parts),
        whole((len(parts), lines) + rest),
        shape((len(parts), lines) + rest, f32),
        after=after,
    )(*parts)


def norm_body(spans, doc_s, doc_ref, pad_ref, x_ref, g_ref, b_ref, h_ref, m_ref, p_ref, t_ref):
    row_at = pl.program_id(0)
    width = x_ref.shape[-1]
    xhat, _ = norm_parts(x_ref[...].astype(f32))
    h = (xhat * g_ref[...] + b_ref[...]).astype(bf16)
    h_ref[...] = h
    doc = doc_ref[pl.ds(row_at, 1)]
    alive = pad_ref[pl.ds(row_at, 1)] == 1
    rows, region = m_ref.shape[1:]
    lane = lax.broadcasted_iota(jnp.int32, (rows, region), 1)
    line = lax.broadcasted_iota(jnp.int32, (rows, region), 0)
    tag_line = lax.broadcasted_iota(jnp.int32, (rows, LANES), 0)
    picked = jnp.zeros((rows, region), f32)
    tag = jnp.zeros((rows, LANES), f32)
    for s in range(1, spans + 1):
        last = doc_s[row_at, s * SPAN - 1]
        hit = (line == s) & (lane < s * SPAN) & (doc == last) & alive
        picked = jnp.where(hit, 1.0, picked)
        tag = jnp.where(tag_line == s, last.astype(f32), tag)
    m_ref[0] = picked
    sums = nn(picked.astype(bf16), h)
    count = jnp.broadcast_to(jnp.sum(picked, axis=1, keepdims=True), (rows, LANES))
    p_ref[0, :, :width] = sums
    p_ref[0, :, width : width + LANES] = count
    p_ref[0, :, width + LANES :] = tag
    tiles = width // LANES
    for c in range(tiles):
        t_ref[0, c : c + 1] = sums[spans : spans + 1, c * LANES : (c + 1) * LANES]
    t_ref[0, tiles : tiles + 1] = count[spans : spans + 1]
    t_ref[0, tiles + 1 : tiles + 2] = tag[spans : spans + 1]
    t_ref[0, tiles + 2 :] = jnp.zeros((8 - tiles - 2, LANES), f32)


def first_norm(docs, pads, x, gain, shift, rows, region, after):
    tokens, width = x.shape
    spans = region // SPAN
    lines = -(-(spans + 1) // 8) * 8
    wide = width + 2 * LANES
    tok = pl.BlockSpec((region, width), lambda i, *_: (i, 0))

    def row(n, w):
        return pl.BlockSpec((1, n, w), lambda i, *_: (i, 0, 0))

    def body(*refs):
        norm_body(spans, *refs)

    return call(
        body,
        (rows,),
        1,
        [whole(docs.shape), whole(docs.shape), tok, whole((1, width)), whole((1, width))],
        [tok, row(lines, region), row(lines, wide), row(8, LANES)],
        [
            shape((tokens, width), bf16),
            shape((rows, lines, region), f32),
            shape((rows, lines, wide), f32),
            shape((rows, 8, LANES), f32),
        ],
        after=after,
        us=4,
    )(docs, docs, pads, x, gain[None], shift[None])


def state_of(every_ref, d, row_at, tiles):
    lines = every_ref[d, row_at * 8 : row_at * 8 + 8]
    sums = jnp.concatenate([lines[c : c + 1] for c in range(tiles)], axis=1)
    return sums, lines[tiles : tiles + 1], lines[tiles + 1 : tiles + 2]


def means_body(rows, spans, take, me_s, doc_s, doc_ref, pad_ref, p_ref, mean_ref, misc_ref, every_ref):
    me = me_s[0]
    take(me)
    devices = every_ref.shape[0]
    width = mean_ref.shape[-1]
    tiles = width // LANES
    mean_ref[...] = jnp.zeros_like(mean_ref)
    misc_ref[...] = jnp.zeros_like(misc_ref)
    for row_at in range(rows):
        sums = carry = jnp.zeros((1, width), f32)
        count = carry_count = jnp.zeros((1, LANES), f32)
        tag = tag_in = jnp.full((1, LANES), -1.0, f32)
        for d in range(1, devices):
            new_sums, new_count, new_tag = state_of(every_ref, d - 1, row_at, tiles)
            same = (new_tag == tag).astype(f32)
            sums = new_sums + same[:, :1] * sums
            count = new_count + same * count
            tag = new_tag
            mine = me == d
            carry = jnp.where(mine, sums, carry)
            carry_count = jnp.where(mine, count, carry_count)
            tag_in = jnp.where(mine, tag, tag_in)
        for s in range(spans):
            if s == 0:
                run_doc = tag_in
            else:
                run_doc = jnp.full((1, LANES), doc_s[row_at, s * SPAN - 1].astype(f32))
            flag = (tag_in == run_doc).astype(f32)
            total = p_ref[row_at, s : s + 1, :width] + flag[:, :1] * carry
            count_here = p_ref[row_at, s : s + 1, width : width + LANES] + flag * carry_count
            divisor = jnp.maximum(count_here, 1.0)
            mean_ref[row_at, s : s + 1] = total / divisor[:, :1]
            at = row_at * spans + s
            toks = slice(s * SPAN, (s + 1) * SPAN)
            doc = doc_ref[row_at : row_at + 1, toks].astype(f32)
            misc_ref[at, 0:1] = 1.0 / divisor
            misc_ref[at, 1:2] = flag
            misc_ref[at, 2:3] = run_doc
            misc_ref[at, 3:4] = count_here
            misc_ref[at, 4:5] = doc
            misc_ref[at, 5:6] = jnp.where(pad_ref[row_at : row_at + 1, toks] == 1, doc, -2.0)


def document_means(me, docs, pads, prefix, sent, devices, rows, region):
    spans = region // SPAN
    lines = prefix.shape[1]
    width = prefix.shape[2] - 2 * LANES
    in_order = len(sent) == 1
    tall = rows * 8
    outs = [
        shape((rows, lines, width), f32),
        shape((rows * spans, 8, LANES), f32),
        shape((devices, tall, LANES), f32),
    ]

    def body(me_s, doc_s, doc_ref, pad_ref, p_ref, *refs):
        got, outs = refs[: len(sent)], refs[len(sent) :]

        def take(me):
            if in_order:
                outs[2][...] = got[0][...]
                return
            for core, ref in enumerate(got):
                for j in range(ref.shape[0]):
                    outs[2][me ^ (2 * j + core)] = ref[j]

        means_body(rows, spans, take, me_s, doc_s, doc_ref, pad_ref, p_ref, *outs)

    def tail(v):
        last = v.shape[1] // tall - 1
        return pl.BlockSpec((v.shape[0], tall, LANES), lambda *_: (0, last, 0))

    return call(
        body,
        (1,),
        2,
        [whole(docs.shape), whole(docs.shape), whole(prefix.shape)] + [tail(v) for v in sent],
        [whole(v.shape) for v in outs],
        outs,
    )(me, docs, docs, pads, prefix, *sent)


def take_pieces(at_s, came, w_ref):
    here = at_s[0]
    for core, ref in enumerate(came):
        pieces = ref.shape[0]
        rows = w_ref.shape[0] // (2 * pieces)
        for j in range(pieces):
            at = pl.multiple_of((here ^ (2 * j + core)) * rows, rows)
            for i in range(3):
                w_ref[pl.ds(at, rows), i * LANES : (i + 1) * LANES] = ref[j, i * rows : (i + 1) * rows].astype(bf16)


def pair_body(spans, load, mean_ref, misc_ref, h_ref, w_ref, qkv_ref, p_ref, ps_ref, o_ref, bar_ref, mix_s):
    row_at = pl.program_id(1)

    @pl.when(row_at == 0)
    def _():
        load()
        both = nn(hi_lo(mean_ref[...].reshape(-1, mean_ref.shape[-1])), w_ref[:, LANES:])
        half = both.shape[0] // 2
        bar_ref[0] = (both[:half] + both[half:]).reshape(bar_ref.shape[1:])

    qkv = nn(h_ref[...], w_ref[...])
    qkv_ref[:, :LANES] = (qkv[:, :LANES] * (1.0 / math.sqrt(HEAD_DIM))).astype(bf16)
    qkv_ref[:, LANES:] = qkv[:, LANES:].astype(bf16)
    bars = bar_ref[0, row_at]
    k_lines, v_lines = head_lines(bars[:, :LANES]), head_lines(bars[:, LANES:])
    summaries = nt(k_lines, qkv_ref[:, :LANES]) + math.log(SPAN)
    masks = halves()
    u = lax.broadcasted_iota(jnp.int32, (SPAN, SPAN), 0)
    t = lax.broadcasted_iota(jnp.int32, (SPAN, SPAN), 1)
    all_weights = []
    for s in range(spans):
        toks = slice(s * SPAN, (s + 1) * SPAN)
        q, k, v = (qkv_ref[toks, i * LANES : (i + 1) * LANES] for i in range(3))
        doc, code = misc_ref[s, 4:5], misc_ref[s, 5:6]
        ok = ((u < t) & (jnp.broadcast_to(code, (SPAN, SPAN)).T == doc)) | (u == t)
        present = (doc == misc_ref[s, 2:3]) & (misc_ref[s, 3:4] > 0.0)
        scores = nt(split(k, masks), q)
        probs, weights = [], []
        for half in range(2):
            score = jnp.where(ok, scores[half * SPAN : (half + 1) * SPAN], MASKED)
            far = jnp.where(present, summaries[8 * s + half : 8 * s + half + 1, toks], MASKED)
            top = jnp.maximum(jnp.max(score, axis=0, keepdims=True), far)
            e = jnp.exp(score - top)
            w = jnp.exp(far - top)
            inverse = 1.0 / (jnp.sum(e, axis=0, keepdims=True) + w)
            probs.append((e * inverse).astype(bf16))
            weights.append(w * inverse)
        probs = jnp.concatenate(probs, axis=0)
        weights = eight(weights)
        p_ref[0, s] = probs
        ps_ref[0, s] = weights
        all_weights.append(weights)
        mix_s[toks] = tn(probs, split(v, masks))
    o_ref[...] = (mix_s[...] + tn(diagonal(all_weights, bars.shape[0]), v_lines)).astype(bf16)


def pair_forward(at, means, misc, h, source, first, parts, region, kept):
    tokens, width = h.shape
    rows = tokens // region
    spans = region // SPAN
    pairs = width // LANES
    lines = means.shape[1]
    kind, *weights = source

    def row(n, *rest):
        return pl.BlockSpec((n,) + rest, lambda i, r, s: (r,) + (0,) * len(rest))

    def pair(i, s):
        return i if kind == "all" else s[1] ^ (first + i)

    in_specs = [whole(means.shape), row(spans, 8, LANES), row(region, width)]
    w_spec = pl.BlockSpec((width, 3 * LANES), lambda i, r, s: (0, pair(i, s)))
    if kind == "all":
        in_specs.append(w_spec)
    else:
        pieces = 2 * weights[3].shape[0]
        in_specs += [whole(w.shape) for w in weights[:3]]
        in_specs += [
            pl.BlockSpec(
                (w.shape[0], 3 * width // pieces, LANES), lambda i, r, s: (0, jnp.maximum(first + i - 1, 0), 0)
            )
            for w in weights[3:]
        ]
    out_specs = [
        pl.BlockSpec((region, 3 * LANES), lambda i, r, s: (r, pair(i, s))),
        pl.BlockSpec((1, spans, 2 * SPAN, SPAN), lambda i, r, s: (pair(i, s), r, 0, 0)),
        pl.BlockSpec((1, spans, 8, SPAN), lambda i, r, s: (pair(i, s), r, 0, 0)),
        pl.BlockSpec((region, LANES), lambda i, r, s: (r, pair(i, s))),
        pl.BlockSpec((1, rows, lines, 2 * LANES), lambda i, r, s: (pair(i, s), 0, 0, 0)),
    ]
    out_shape = [
        shape((tokens, 3 * width), bf16),
        shape((pairs, tokens // SPAN, 2 * SPAN, SPAN), bf16),
        shape((pairs, tokens // SPAN, 8, SPAN), f32),
        shape((tokens, width), bf16),
        shape((pairs, rows, lines, 2 * LANES), f32),
    ]
    if kind != "all":
        out_specs.append(w_spec)
        out_shape.append(shape((width, 3 * width), bf16))
    n_in = 3 + len(weights)
    kept = list(kept or ())

    def body(at_s, *refs):
        ins, got, outs, mix_s = refs[:3], refs[3:n_in], refs[n_in + len(kept) : -1], refs[-1]
        if kind == "all":
            w_ref = got[0]
            load = lambda: None
        else:
            w_ref = outs[5]

            def load():
                if first == 0:

                    @pl.when(pl.program_id(0) == 0)
                    def _():
                        for i in range(3):
                            w_ref[:, i * LANES : (i + 1) * LANES] = got[i][...]

                @pl.when(first + pl.program_id(0) > 0)
                def _():
                    take_pieces(at_s, got[3:], w_ref)

        pair_body(spans, load, *ins, w_ref, *outs[:5], mix_s)

    return call(
        body,
        (parts, rows),
        1,
        in_specs + [pl.BlockSpec(memory_space=pl.ANY)] * len(kept),
        out_specs,
        out_shape,
        us=5 * parts,
        aliases={1 + n_in + i: i for i in range(len(kept))},
        scratch=[pltpu.VMEM((region, LANES), f32)],
    )(at, means, misc, h, *weights, *kept)


def take_hidden(at_s, own, came, wu_s, wo_s, wd_s, bu_s):
    here, group = at_s[0], at_s[2]
    others = wu_s.shape[0] - 1
    lines = own[1].shape[0]
    wu_s[group] = own[0][...]
    wo_s[pl.ds(pl.multiple_of(group * lines, lines), lines)] = own[1][...]
    bu_s[group] = jnp.broadcast_to(own[2][...], bu_s.shape[1:])
    wd_s[group] = own[3][...]
    for core, (up, down) in enumerate(came):
        pieces = up.shape[0]
        rows, thin = wu_s.shape[1] // (2 * pieces), lines // (2 * pieces)
        deep = down.shape[1] // others
        for k in range(others):
            to = group ^ (k + 1)
            for j in range(pieces):
                owner = here ^ (2 * j + core)
                first = k * (rows + thin)
                wu_s[to, pl.ds(pl.multiple_of(owner * rows, rows), rows)] = up[j, first : first + rows].astype(bf16)
                at = pl.multiple_of(to * lines + owner * thin, thin)
                wo_s[pl.ds(at, thin)] = up[j, first + rows : first + rows + thin].astype(bf16)
            for j in range(down.shape[0]):
                owner = here ^ core ^ (0, 2, 0, 4)[j]
                place = 4 * (j // 2) + down_rows(owner)[j // 2]
                at = pl.ds(pl.multiple_of(place * deep, deep), deep)
                wd_s[to, at] = down[j, k * deep : (k + 1) * deep].astype(bf16)


def ffn_body(
    at_s, x_ref, g_ref, o_ref, mine_ref, gain_ref, shift_ref, bd_ref, load, wo_ref,
    out_ref, dmid_ref, do_ref, gwu_ref, gwd_ref, gwo_ref, gbu_ref, small_ref, wu_ref, wd_ref, bu_ref, a_s, du_s,
):
    @pl.when(pl.program_id(0) == 0)
    def _():
        load()
        gwu_ref[...] = jnp.zeros_like(gwu_ref)
        gwd_ref[...] = jnp.zeros_like(gwd_ref)
        gwo_ref[...] = jnp.zeros_like(gwo_ref)
        gbu_ref[...] = jnp.zeros_like(gbu_ref)
        small_ref[...] = jnp.zeros_like(small_ref)

    mid = x_ref[...].astype(f32) + nn(o_ref[...], wo_ref[...])
    xhat, rstd = norm_parts(mid)
    h = (xhat * gain_ref[...] + shift_ref[...]).astype(bf16)
    gm = g_ref[...]
    y = dn = None
    for j in range(wu_ref.shape[0]):
        up = nn(h, wu_ref[j]) + bu_ref[j, :1]
        phi, slope = gelu_parts(up)
        a = (up * phi).astype(bf16)
        du = (nt(gm, wd_ref[j]) * slope).astype(bf16)
        a_s[j] = a
        du_s[j] = du
        y_part = nn(a, wd_ref[j])
        dn_part = nt(du, wu_ref[j])
        y = y_part if y is None else y + y_part
        dn = dn_part if dn is None else dn + dn_part
    out_ref[...] = (mid + y + bd_ref[...]).astype(bf16)
    g = gm.astype(f32)
    small_ref[2:3] += jnp.sum(dn * xhat, axis=0, keepdims=True)
    small_ref[3:4] += jnp.sum(dn, axis=0, keepdims=True)
    small_ref[4:5] += jnp.sum(g, axis=0, keepdims=True)
    dmid = g + norm_back(dn * gain_ref[...], xhat, rstd)
    dmid_ref[...] = dmid
    gx = dmid.astype(bf16)
    do_ref[...] = nt(gx, wo_ref[...]).astype(bf16)
    gwo_ref[...] += tn(mine_ref[...], gx)
    group = at_s[2]
    du = du_s[group]
    gwd_ref[...] += tn(a_s[group], gm)
    gwu_ref[...] += tn(h, du)
    gbu = jnp.sum(du.astype(f32), axis=0, keepdims=True)
    gbu_ref[...] += gbu
    if gbu.shape[1] == small_ref.shape[1]:
        small_ref[5:6] += gbu


def feed_forward(at, x, g, o, gain, shift, bd, source):
    tokens, width = x.shape
    kind, *weights = source
    came = kind == "came"
    if came:
        wu, wo, bu, wd, mine, theirs, biases = weights
        hidden, groups = wu.shape[1], 1 + len(biases)
        args = [wu, wo, bu, wd, *mine, *theirs, *biases]
        last = biases[0].shape[0] // 8 - 1
        specs = [whole(w.shape) for w in args[:8]]
        specs += [pl.BlockSpec((8, width), lambda i, *_: (last, 0))] * len(biases)
    else:
        args = weights
        groups, _, hidden = args[0].shape
        specs = [whole(w.shape) for w in args]
    steps = 4
    chunk = tokens // steps
    tok = pl.BlockSpec((chunk, width), lambda i, *_: (i, 0))
    n_w = len(args)
    scratch = [pltpu.VMEM((groups, chunk, hidden), bf16)] * 2
    if came:
        scratch += [
            pltpu.VMEM((groups, width, hidden), bf16),
            pltpu.VMEM((width, width), bf16),
            pltpu.VMEM((groups, 8, hidden), f32),
            pltpu.VMEM((groups, hidden, width), bf16),
        ]

    def body(at_s, *refs):
        ins, got = refs[:7], refs[7 : 7 + n_w]
        outs, acts, held = refs[7 + n_w : 15 + n_w], refs[15 + n_w : 17 + n_w], refs[17 + n_w :]

        def load():
            if came:
                wu_s, wo_s, bu_s, wd_s = held
                take_hidden(at_s, got[:4], (got[4:6], got[6:8]), wu_s, wo_s, wd_s, bu_s)
                for k, ref in enumerate(got[8:]):
                    bu_s[at_s[2] ^ (k + 1)] = ref[...]

        wu_r, wo_r, bu_r, wd_r = held if came else got
        ffn_body(at_s, *ins, load, wo_r, *outs, wu_r, wd_r, bu_r, *acts)

    return call(
        body,
        (steps,),
        1,
        [tok, tok, tok, pl.BlockSpec((chunk, LANES), lambda i, s: (i, s[1])),
         whole((1, width)), whole((1, width)), whole((1, width))] + specs,
        [tok, tok, tok, whole((width, hidden)), whole((hidden, width)), whole((LANES, width)),
         whole((1, hidden)), whole((8, width))],
        [
            shape((tokens, width), bf16),
            shape((tokens, width), f32),
            shape((tokens, width), bf16),
            shape((width, hidden), f32),
            shape((hidden, width), f32),
            shape((LANES, width), f32),
            shape((1, hidden), f32),
            shape((8, width), f32),
        ],
        scratch=scratch,
        us=38,
    )(at, x, g, o, o, gain[None], shift[None], bd[None], *args)


def pair_back_body(spans, qkv_ref, do_ref, p_ref, ps_ref, bar_ref, misc_ref, d_ref, g_ref, d_s):
    row_at = pl.program_id(1)
    masks = halves()
    wide = 2 * LANES
    bars = bar_ref[0, row_at]
    lines = bars.shape[0]
    k_lines, v_lines = head_lines(bars[:, :LANES]), head_lines(bars[:, LANES:])
    dp_far = nt(v_lines, do_ref[...])
    all_far, all_weights = [], []
    for s in range(spans):
        toks = slice(s * SPAN, (s + 1) * SPAN)
        q, k, v = (qkv_ref[toks, i * LANES : (i + 1) * LANES] for i in range(3))
        do = do_ref[toks]
        weight = ps_ref[0, s]
        dp = nt(split(v, masks), do)
        probs, grads, far = [], [], []
        for half in range(2):
            p_half = p_ref[0, s, half * SPAN : (half + 1) * SPAN, :]
            p = p_half.astype(f32)
            dp_half = dp[half * SPAN : (half + 1) * SPAN]
            w, dw = weight[half : half + 1], dp_far[8 * s + half : 8 * s + half + 1, toks]
            r = jnp.sum(p * dp_half, axis=0, keepdims=True) + w * dw
            probs.append(p_half)
            grads.append((p * (dp_half - r)).astype(bf16))
            far.append(w * (dw - r))
        all_far.append(eight(far))
        all_weights.append(weight)
        d_s[toks, :LANES] = tn(jnp.concatenate(grads, axis=0), split(k, masks))
        d_s[toks, LANES:wide] = nn(jnp.concatenate(grads, axis=1), split(q, masks))
        d_s[toks, wide:] = nn(jnp.concatenate(probs, axis=1), split(do, masks))
    far = diagonal(all_far, lines)
    dq = d_s[:, :LANES] + tn(far, k_lines)
    d_ref[:, :LANES] = (dq.astype(bf16).astype(f32) * (1.0 / math.sqrt(HEAD_DIM))).astype(bf16)
    line = lax.broadcasted_iota(jnp.int32, (8 * lines, LANES), 0)
    lane = lax.broadcasted_iota(jnp.int32, (8 * lines, LANES), 1)
    own = lane // HEAD_DIM == line % 8
    gk = jnp.where(own, nn(far, qkv_ref[:, :LANES]), 0.0)
    gv = jnp.where(own, nn(diagonal(all_weights, lines), do_ref[...]), 0.0)
    out = jnp.zeros((1, wide), f32)
    after = None
    for s in reversed(range(spans)):
        toks = slice(s * SPAN, (s + 1) * SPAN)
        dkv = d_s[toks, LANES:]
        gkv = [jnp.sum(v[8 * s : 8 * s + 8], axis=0, keepdims=True) for v in (gk, gv)]
        inverse, flag = misc_ref[s, 0:1, :], misc_ref[s, 1:2, :]
        gkv = jnp.concatenate(gkv, axis=1) * jnp.concatenate([inverse, inverse], axis=1)
        out = out + jnp.concatenate([flag, flag], axis=1) * gkv
        if after is None:
            after = gkv
        else:
            reached = jnp.broadcast_to(misc_ref[s, 5:6], (SPAN, SPAN)).T == misc_ref[s + 1, 2:3]
            dkv = dkv + jnp.where(jnp.concatenate([reached, reached], axis=1), after, 0.0)
            same = (misc_ref[s, 2:3] == misc_ref[s + 1, 2:3]).astype(f32)
            after = gkv + jnp.concatenate([same, same], axis=1) * after
        d_ref[toks, LANES:] = dkv.astype(bf16)
    g_ref[0, :, :LANES] = jnp.zeros((1, LANES), f32)
    g_ref[0, :, LANES:] = out


def pair_backward(at, qkv, do, p, ps, bars, misc, h, region, first, parts, kept):
    tokens, width = do.shape
    rows = tokens // region
    spans = region // SPAN
    lines = bars.shape[2]
    own = h is not None

    def pair(i, s):
        return s[1] ^ (first + i)

    def row(n, *rest):
        return pl.BlockSpec((n,) + rest, lambda i, r, s: (r,) + (0,) * len(rest))

    tok3 = pl.BlockSpec((region, 3 * LANES), lambda i, r, s: (r, pair(i, s)))
    back = pl.BlockSpec((1, 1, 3 * LANES), lambda i, r, s: (r, 0, pair(i, s)))
    in_specs = [
        tok3,
        pl.BlockSpec((region, LANES), lambda i, r, s: (r, pair(i, s))),
        pl.BlockSpec((1, spans, 2 * SPAN, SPAN), lambda i, r, s: (pair(i, s), r, 0, 0)),
        pl.BlockSpec((1, spans, 8, SPAN), lambda i, r, s: (pair(i, s), r, 0, 0)),
        pl.BlockSpec((1, rows, lines, 2 * LANES), lambda i, r, s: (pair(i, s), 0, 0, 0)),
        row(spans, 8, LANES),
    ]
    args = [qkv, do, p, ps, bars, misc]
    out_specs = [tok3, back]
    out_shape = [shape((tokens, 3 * width), bf16), shape((rows, 1, 3 * width), f32)]
    if own:
        in_specs.append(row(region, width))
        args.append(h)
        out_specs.append(whole((width, 3 * LANES)))
        out_shape.append(shape((width, 3 * LANES), f32))
    n_in = len(args)
    kept = list(kept or ())

    def body(at_s, *refs):
        outs = refs[n_in + len(kept) : -1]
        pair_back_body(spans, *refs[:6], outs[0], outs[1], refs[-1])
        if own:
            grads = tn(refs[6][...], outs[0][...])

            @pl.when(pl.program_id(1) == 0)
            def _():
                outs[2][...] = grads

            @pl.when(pl.program_id(1) > 0)
            def _():
                outs[2][...] += grads

    return call(
        body,
        (parts, rows),
        1,
        in_specs + [pl.BlockSpec(memory_space=pl.ANY)] * len(kept),
        out_specs,
        out_shape,
        us=6 * parts,
        aliases={1 + n_in + i: i for i in range(len(kept))},
        scratch=[pltpu.VMEM((region, 3 * LANES), f32)],
    )(at, *args, *kept)


def input_body(
    spans, at_s, every_ref, back_ref, mine_ref, m_ref, x_ref, gain_ref, dmid_ref, d_ref, w_ref, so_far_ref,
    gi_ref, small_ref, late_ref,
):
    row_at = pl.program_id(0)
    me = at_s[0]
    devices = every_ref.shape[0]
    rows = back_ref.shape[1]
    width = x_ref.shape[-1]
    tiles = width // LANES
    wide = w_ref.shape[1]
    lines = m_ref.shape[1]

    @pl.when(row_at == 0)
    def _():
        small_ref[...] = so_far_ref[...]
        heads, tails = [], []
        for r in range(rows):
            run = jnp.zeros((1, mine_ref.shape[-1]), f32)
            tag = None
            for d in reversed(range(devices)):
                sums, _, tag_here = state_of(every_ref, d, r, tiles)
                if tag is not None:
                    run = mine_ref[d + 1, r] + (tag == tag_here).astype(f32)[:, :1] * run
                tag = tag_here
                heads.append(sums)
                tails.append(run)
        late_ref[...] = lax.dot_general(
            jnp.concatenate(heads, axis=0), jnp.concatenate(tails, axis=0), (((0,), (0,)), ((), ())),
            preferred_element_type=f32, precision=lax.Precision.HIGHEST,
        )

    run = jnp.zeros((1, wide), f32)
    mine = run
    tag = None
    for d in reversed(range(devices)):
        tag_here = every_ref[d, pl.ds(row_at * 8, 8)][tiles + 1 : tiles + 2]
        if tag is not None:
            run = back_ref[d + 1, row_at] + (tag == tag_here).astype(f32)[:, :1] * run
            mine = jnp.where(me == d, run, mine)
        tag = tag_here

    through = nt(hi_lo(jnp.broadcast_to(mine, (8, wide))), w_ref[...])
    through = through[0:1] + through[8:9]
    line = lax.broadcasted_iota(jnp.int32, (lines, width), 0)
    through = jnp.where(line == spans, jnp.broadcast_to(through, (lines, width)), 0.0)
    dn = nt(d_ref[...], w_ref[...]) + tn(twice(m_ref[0]), hi_lo(through))
    xhat, rstd = norm_parts(x_ref[...].astype(f32))
    small_ref[0:1] += jnp.sum(dn * xhat, axis=0, keepdims=True)
    small_ref[1:2] += jnp.sum(dn, axis=0, keepdims=True)
    gi_ref[...] = dmid_ref[...] + norm_back(dn * gain_ref[...], xhat, rstd)


def input_grads(at, every, back, m, x, gain, dmid, d, w, small, region):
    tokens, width = x.shape
    rows = tokens // region
    devices = every.shape[0]
    tok = pl.BlockSpec((region, width), lambda i, *_: (i, 0))

    def body(*refs):
        input_body(region // SPAN, *refs)

    return call(
        body,
        (rows,),
        1,
        [
            whole(every.shape), whole(back.shape),
            pl.BlockSpec((devices, rows, 1, 3 * LANES), lambda i, s: (0, 0, 0, s[1])),
            pl.BlockSpec((1,) + m.shape[1:], lambda i, *_: (i, 0, 0)),
            tok, whole((1, width)), tok,
            pl.BlockSpec((region, 3 * width), lambda i, *_: (i, 0)),
            whole(w.shape),
            whole(small.shape),
        ],
        [tok, whole((8, width)), whole((width, 3 * LANES))],
        [shape((tokens, width), f32), shape((8, width), f32), shape((width, 3 * LANES), f32)],
        us=12,
    )(at, every, back, back, m, x, gain[None], dmid, d, w, small)


def pack_body(at_s, gu_ref, gd_ref, go_ref, gw_ref, keep_ref, give_ref):
    core = at_s[0] % 2
    chips = keep_ref.shape[0]
    rows = gu_ref.shape[0] // (2 * chips)
    lines = go_ref.shape[0] // (2 * chips)
    for out, c in ((keep_ref, core), (give_ref, 1 - core)):
        for j in range(chips):
            at = pl.multiple_of((2 * j + c) * rows, rows)
            out[j, :rows] = gu_ref[pl.ds(at, rows)]
            out[j, rows : 2 * rows] = gd_ref[pl.ds(at, rows)]
            out[j, 2 * rows :, : 3 * LANES] = gw_ref[pl.ds(at, rows)]
            at = pl.multiple_of((2 * j + c) * lines, lines)
            go = go_ref[pl.ds(at, lines)]
            for i in range(go.shape[1] // LANES):
                out[j, 2 * rows + i * lines : 2 * rows + (i + 1) * lines, 3 * LANES :] = go[:, i * LANES : (i + 1) * LANES]


def pack(at, gu, gd, go, gw, devices):
    width = gu.shape[1]
    rows = gu.shape[0] // devices
    out = (devices // 2, 3 * rows, width)
    return call(
        pack_body, (1,), 1, [whole(v.shape) for v in (gu, gd, go, gw)], [whole(out), whole(out)], [shape(out, f32)] * 2
    )(at, gu, gd, go, gw)


def fold_body(at_s, keep_ref, got_ref, *outs):
    chip = at_s[0] // 2
    for j, out in enumerate(outs):
        out[...] = keep_ref[chip ^ j] + got_ref[chip ^ j]


def fold(at, keep, got, after):
    chips = keep.shape[0]
    return call(
        fold_body, (1,), 1, [whole(keep.shape)] * 2, [whole(keep.shape[1:])] * chips,
        [shape(keep.shape[1:], f32)] * chips,
        after=after,
    )(at, keep, got)


def add_body(*refs):
    total = refs[0][...]
    for ref in refs[1:-1]:
        total = total + ref[...]
    refs[-1][...] = total


def add_up(parts, after):
    spec = whole(parts[0].shape)
    return call(add_body, (1,), 0, [spec] * len(parts), spec, shape(parts[0].shape, f32), after=after)(*parts)


def unpack_body(at_s, mine_ref, theirs_ref, late_ref, small_ref, gq_ref, gk_ref, gv_ref, go_ref, gu_ref, gd_ref, *tiny):
    here = at_s[0]
    rows = gu_ref.shape[0] // (2 * mine_ref.shape[0])
    lines = go_ref.shape[0] // (2 * mine_ref.shape[0])
    for core, ref in enumerate((mine_ref, theirs_ref)):
        for j in range(ref.shape[0]):
            owner = here ^ (2 * j + core)
            at = pl.ds(pl.multiple_of(owner * rows, rows), rows)
            gu_ref[at] = ref[j, :rows]
            gd_ref[at] = ref[j, rows : 2 * rows]
            for i, out in enumerate((gq_ref, gk_ref, gv_ref)):
                lanes = slice(i * LANES, (i + 1) * LANES)
                out[at] = ref[j, 2 * rows :, lanes] + late_ref[at, lanes]
            at = pl.ds(pl.multiple_of(owner * lines, lines), lines)
            for i in range(go_ref.shape[1] // LANES):
                first = 2 * rows + i * lines
                go_ref[at, i * LANES : (i + 1) * LANES] = ref[j, first : first + lines, 3 * LANES :]
    total = small_ref[0]
    for d in range(1, small_ref.shape[0]):
        total = total + small_ref[d]
    for i, out in enumerate(tiny):
        out[...] = total[i : i + 1]


def unpack(at, mine, theirs, late, small):
    width = mine.shape[2]
    thin = shape((width, LANES), f32)
    outs = [thin, thin, thin, shape((LANES, width), f32), shape((width, width), f32), shape((width, width), f32)]
    outs += [shape((1, width), f32)] * 6
    return call(
        unpack_body, (1,), 1, [whole(v.shape) for v in (mine, theirs, late, small)], [whole(v.shape) for v in outs], outs
    )(at, mine, theirs, late, small)


def narrow_body(w_ref, o_ref):
    o_ref[...] = w_ref[...].astype(bf16)


def gathered(part):
    every = lax.all_gather(part.astype(f32), "head")
    flat = every.reshape(-1, part.shape[1])
    chunk = flat.shape[0] // 8
    block = pl.BlockSpec((chunk, part.shape[1]), lambda i: (i, 0))
    return call(narrow_body, (8,), 0, [block], block, shape(flat.shape, bf16))(flat).reshape(every.shape)


def swap(v, axis, mask):
    return lax.ppermute(v, axis, [(i, i ^ mask) for i in range(lax.axis_size(axis))])


def on_device(
    inputs, doc_ids, pad_mask, ln1_gain, ln1_shift, w_query, w_key, w_value, w_out,
    ln2_gain, ln2_shift, w_up, b_up, w_down, b_down, out_grad,
):
    rows, region, width = inputs.shape
    tokens = rows * region
    devices = lax.axis_size("seq")
    groups = lax.axis_size("head")
    here = lax.axis_index("seq")
    group = lax.axis_index("head")
    share = width // groups
    pairs = width // LANES
    spans = region // SPAN
    own_pair = group * share // LANES
    at = jnp.stack([here, own_pair, group]).astype(jnp.int32)
    x = inputs.reshape(tokens, width)
    g = out_grad.reshape(tokens, width)
    by_share = share == LANES and devices == 8 and groups & (groups - 1) == 0

    if by_share:
        others = range(2, devices, 2)
        ks = range(1, groups)
        a_mine = attention_share(at, w_query, w_key, w_value, devices)
        a_came = [swap(a_mine, "head", k) for k in ks]
        up_mine, down_mine = hidden_share(at, w_up, w_out, b_up, w_down, devices, a_came[:1])
        up_came = [swap(up_mine, "head", k) for k in ks]
        down_came = [swap(down_mine, "head", k) for k in ks]
    h1, m, prefix, tiny = first_norm(
        doc_ids, pad_mask, x, ln1_gain, ln1_shift, rows, region, [up_mine] if by_share else []
    )
    tiny = tiny.reshape(rows * 8, LANES)
    if by_share:
        (a_sent,) = cat([[(v, 0, v.shape[0]) for v in a_came + [tiny]]])
        a_moved = [swap(a_sent, "seq", j) for j in others]
        thick = up_mine.shape[0] - 8
        (up_sent,) = cat([[(v, 0, thick) for v in up_came]])
        up_moved = [swap(up_sent, "seq", j) for j in others]
        mine = pile([a_sent] + a_moved, after=[up_sent])
        a_block = (mine, swap(mine, "seq", 1))
        means, misc, every = document_means(at, doc_ids, pad_mask, prefix, a_block, devices, rows, region)
        source = ("came", w_query, w_key, w_value) + a_block
        kept = pair_forward(at, means, misc, h1, source, 0, pairs // 2, region, None)
        deep = down_mine.shape[0] // 2
        upper, lower = cat([[(v, first, deep) for v in down_came] for first in (0, deep)], after=[kept[3]])
        down_moved = [upper, swap(upper, "seq", 2), lower, swap(lower, "seq", 4)]
        kept = pair_forward(at, means, misc, h1, source, pairs // 2, pairs - pairs // 2, region, kept)
        qkv, p, ps, o, bars, w_in = kept
        up_block = pile([up_sent] + up_moved, after=[upper])
        down_block = pile(down_moved, after=[o])
        ffn_source = (
            "came", w_up, w_out, b_up[None], w_down, (up_block, down_block),
            (swap(up_block, "seq", 1), swap(down_block, "seq", 1)), up_came,
        )
    else:
        every = lax.all_gather(tiny, "seq")
        means, misc, every = document_means(at, doc_ids, pad_mask, prefix, [every], devices, rows, region)
        w_in = gathered(jnp.concatenate([w_query, w_key, w_value], axis=1))
        w_in = w_in.reshape(groups, width, 3, share).transpose(1, 2, 0, 3).reshape(width, 3, pairs, LANES)
        w_in = w_in.transpose(0, 2, 1, 3).reshape(width, 3 * width)
        qkv, p, ps, o, bars = pair_forward(at, means, misc, h1, ("all", w_in), 0, pairs, region, None)
        bu = lax.all_gather(b_up, "head")
        bu = jnp.broadcast_to(bu[:, None], (groups, 8, bu.shape[1]))
        ffn_source = ("all", gathered(w_up), gathered(w_out).reshape(width, width), bu, gathered(w_down))

    out, dmid, do, gwu, gwd, gwo, gbu, small = feed_forward(
        at, x, g, o, ln2_gain, ln2_shift, b_down, ffn_source
    )
    back_args = (at, qkv, do, p, ps, bars, misc)
    d, g_back, gw = pair_backward(*back_args, h1, region, 0, 1, None)
    if by_share:
        keep, give = pack(at, gwu, gwd, gwo, gw, devices)
        got = swap(give, "seq", 1)
        d, g_back = pair_backward(*back_args, None, region, 1, 1, (d, g_back))
        folded = fold(at, keep, got, [g_back])
        arrived = [swap(v, "seq", j) for v, j in zip(folded[1:], others)]
        d, g_back = pair_backward(*back_args, None, region, 2, pairs - 2, (d, g_back))
        total = add_up([folded[0]] + arrived, [g_back])
        spread = [swap(total, "seq", j) for j in others]
    else:
        d, g_back = pair_backward(*back_args, None, region, 1, pairs - 1, (d, g_back))
    back = lax.all_gather(g_back, "seq")
    grad_inputs, small, late = input_grads(at, every, back, m, x, ln1_gain, dmid, d, w_in, small, region)
    out = out.reshape(rows, region, width)
    grad_inputs = grad_inputs.reshape(rows, region, width)
    if by_share:
        mine = pile([total] + spread, after=[small])
        gq, gk, gv, gwo, gwu, gwd, *tiny = unpack(
            at, mine, swap(mine, "seq", 1), late, lax.all_gather(small, "seq")
        )
        g1, s1, g2, s2, gbd, gbu = (v[0] for v in tiny)
        return out, grad_inputs, g1, s1, gq, gk, gv, gwo, g2, s2, gwu, gbu, gwd, gbd

    gwu, gwd, gwo, gbu, small, gw = lax.psum((gwu, gwd, gwo, gbu, small, gw), "seq")
    gw = gw + late
    gq, gk, gv = (gw[:, i * LANES : (i + 1) * LANES] for i in range(3))
    if share != LANES:
        inner = group * share - own_pair * LANES
        gq, gk, gv = (lax.dynamic_slice_in_dim(v, inner, share, 1) for v in (gq, gk, gv))
        gwo = lax.dynamic_slice_in_dim(gwo, inner, share, 0)
    return (
        out, grad_inputs, small[0], small[1], gq, gk, gv, gwo, small[2], small[3], gwu, gbu[0], gwd, small[4]
    )


def solution(mesh):
    tok = P(None, "seq", None)
    ids = P(None, "seq")
    cols, lines = P(None, "head"), P("head", None)
    in_specs = (
        tok, ids, ids, P(), P(), cols, cols, cols, lines, P(), P(), cols, P("head"), lines, P(), tok,
    )
    out_specs = (
        tok, tok, P(), P(), cols, cols, cols, lines, P(), P(), cols, P("head"), lines, P(),
    )
    return jax.shard_map(on_device, mesh=mesh, in_specs=in_specs, out_specs=out_specs, check_vma=False)
```

time: 410 us -> 234 us (0.57)
  waiting for transfers between devices: 182 us -> 21.5 us
  blocking collectives: 60.6 us -> 19.4 us
  starting transfers between devices: 0.21 us -> 32.3 us
  Pallas kernels: 131 us -> 145 us
  between operations: 13.9 us -> 1.09 us
  other arithmetic: 7.66 us -> 0.64 us
    all_gather x4 -> x0, waiting for transfers between devices: 162 us -> none  [spread_weights(): return lax.all_gather(mine, ('head', 'seq'), tiled=True)]
    ppermute x0 -> x28, starting transfers between devices: none -> 32.3 us  [swap(): lax.ppermute(v, axis, [(i, i ^ mask) for i in range(lax.axis_size(axis))])]
    psum x1 -> x0, blocking collectives: 25.1 us -> none  [on_device(): small1 = lax.psum(small1, 'seq')]
    ppermute x0 -> x28, waiting for transfers between devices: none -> 21.5 us  [swap(): lax.ppermute(v, axis, [(i, i ^ mask) for i in range(lax.axis_size(axis))])]
    psum x1 -> x0, waiting for transfers between devices: 20.1 us -> none  [on_device(): gw = lax.psum(gw, 'seq')]
    all_gather x2 -> x1, blocking collectives: 25.2 us -> 9.26 us  [on_device(): lax.all_gather(small, 'seq')]
    pallas_call x11 -> x22, Pallas kernels: 131 us -> 145 us  [call(): return lambda *operands: kernel(*operands, *after)]
    unnamed x16 -> x62, local copies, waits for them, and re-layouts: 2.68 us -> 12.7 us
  transfers between devices with their start and end apart: 5 -> 28, of which waited for: 5 -> 7; matrix products, arithmetic and copies ran while one was open for 3% -> 0% of each run, Pallas kernels for 15% -> 32%
where the time goes in v2:
time: 234 us; the launch traced here: 233 us
  Pallas kernels  145 us (62%)
  starting transfers between devices  32.3 us (14%)
  waiting for transfers between devices  21.5 us (9%)
  blocking collectives  19.4 us (8%)
  local copies, waits for them, and re-layouts  12.7 us (5%)
    pallas_call x22, Pallas kernels, call(): return lambda *operands: kernel(*operands, *after)  145 us
    ppermute x28, starting transfers between devices, swap(): lax.ppermute(v, axis, [(i, i ^ mask) for i in range(lax.axis_size(axis))])  32.3 us
    ppermute x28, waiting for transfers between devices, swap(): lax.ppermute(v, axis, [(i, i ^ mask) for i in range(lax.axis_size(axis))])  21.5 us
    unnamed x62, local copies, waits for them, and re-layouts  12.7 us
    all_gather x1, blocking collectives, on_device(): back = lax.all_gather(g_back, 'seq')  10.2 us
    all_gather x1, blocking collectives, on_device(): lax.all_gather(small, 'seq')  9.26 us
  transfers between devices with their start and end apart: 28, of which 7 were waited for; matrix products, arithmetic and copies ran while one was open for 0% of the time, Pallas kernels for 32%

profile of v2, /device:TPU:0, one launch (start us, length us, event | category | flops | bytes accessed | tf_op | source)
XLA Modules:
  0.0 232.6 jit_solution(2663085297854384884)
XLA Ops:
  1.3 2.1 shard_map.263
  3.4 3.0 %collective-permute-start = (f32[192,128]{1,0:T(8,128)}, f32[192,128]{1,0:T(8,128)S(1)}, u32[]{:S(2)}, u32[]{:S(2)}) collective-permute-start(f32[192,128]{1,0:T(8,128)} %shard_map.263), channel_id=1, source_target_pairs={{0,1},{1,0},{2,3},{3,2},{4,5},{5,4},{6,7},{7,6},{8,9},{9,8},{10,11... | collective-permute-start | bytes 294920 | tf_op jit(solution)/shard_map/ppermute | solution.py:953
  6.4 2.6 %collective-permute-start.1 = (f32[192,128]{1,0:T(8,128)}, f32[192,128]{1,0:T(8,128)S(1)}, u32[]{:S(2)}, u32[]{:S(2)}) collective-permute-start(f32[192,128]{1,0:T(8,128)} %shard_map.263), channel_id=1, source_target_pairs={{0,2},{1,3},{2,0},{3,1},{4,6},{5,7},{6,4},{7,5},{8,10},{9,11},{10,... | collective-permute-start | bytes 294920 | tf_op jit(solution)/shard_map/ppermute | solution.py:953
  10.0 2.4 %shard_map.264 = (f32[88,512]{1,0:T(8,128)}, f32[128,512]{1,0:T(8,128)}) custom-call(s32[3]{0:T(128)} %pad_add_fusion.refs_0_, bf16[512,512]{1,0:T(8,128)(2,1)} %refs_8_.1, bf16[128,512]{1,0:T(8,128)(2,1)} %refs_9_.1, f32[1,512]{1,0:T(1,128)} %bitcast.30, bf16[512,512]{1,0:T(8,128)(2,1)} %refs_11_.1, bf16[512,512]{1,0:T(8,128)(2,1)} %refs_11_.1, ...), custom_call_target="tpu_custom_call" | custom-call | flops 2200000000 | bytes 7000000 | tf_op jit(solution)/shard_map/pallas_call | solution.py:91
  12.4 1.8 collective-permute-start.6
  14.2 3.6 %collective-permute-start.7 = (f32[88,512]{1,0:T(8,128)}, f32[88,512]{1,0:T(8,128)S(1)}, u32[]{:S(2)}, u32[]{:S(2)}) collective-permute-start(f32[88,512]{1,0:T(8,128)} %get-tuple-element.72.refs_6_), channel_id=1, source_target_pairs={{0,2},{1,3},{2,0},{3,1},{4,6},{5,7},{6,4},{7,5},{8,10},{9,11},{10,... | collective-permute-start | bytes 540680 | tf_op jit(solution)/shard_map/ppermute | solution.py:953
  17.8 4.4 %shard_map.265 = (bf16[1792,512]{1,0:T(8,128)(2,1)}, f32[2,8,896]{2,1,0:T(8,128)}, f32[2,8,768]{2,1,0:T(8,128)}, f32[2,8,128]{2,1,0:T(8,128)}) custom-call(s32[2,896]{1,0:T(2,128)} %refs_2_.7, s32[2,896]{1,0:T(2,128)} %refs_2_.7, s32[2,896]{1,0:T(2,128)} %refs_3_.3, bf16[1792,512]{1,0:T(8,128)(2,1)} %bitcast.26, f32[1,512]{1,0:T(1,128)} %bitcast.35, ...), custom_call_target="tpu_custom_call" | custom-call | flops 4400000000 | bytes 14000000 | tf_op jit(solution)/shard_map/pallas_call | solution.py:91
  22.9 1.7 shard_map.266.refs_0_
  24.6 1.5 collective-permute-start.3
  26.1 1.5 collective-permute-start.4
  28.1 2.7 %collective-permute-done.7.refs_1_.refs_17_ = f32[88,512]{1,0:T(8,128)S(1)} collective-permute-done((f32[88,512]{1,0:T(8,128)}, f32[88,512]{1,0:T(8,128)S(1)}, u32[]{:S(2)}, u32[]{:S(2)}) %collective-permute-start.7) | collective-permute-done | bytes 180256 | tf_op jit(solution)/shard_map/ppermute | solution.py:953
  32.2 1.9 shard_map.267.refs_4_.refs_0_
  34.6 4.2 %collective-permute-done.4.refs_2_ = f32[592,128]{1,0:T(8,128)S(1)} collective-permute-done((f32[592,128]{1,0:T(8,128)}, f32[592,128]{1,0:T(8,128)S(1)}, u32[]{:S(2)}, u32[]{:S(2)}) %collective-permute-start.4) | collective-permute-done | bytes 303136 | tf_op jit(solution)/shard_map/ppermute | solution.py:953
  40.2 2.3 %shard_map.268.refs_5_.refs_7_ = f32[4,592,128]{2,1,0:T(8,128)} custom-call(f32[592,128]{1,0:T(8,128)} %shard_map.266.refs_0_, f32[592,128]{1,0:T(8,128)} %copy-done.18, f32[592,128]{1,0:T(8,128)} %copy-done.19, f32[592,128]{1,0:T(8,128)} %copy-done.20, f32[240,512]{1,0:T(8,128)} %shard_map.267.refs_4_.refs_0_), custom_call_target="tpu_custom_call" | custom-call | flops 2200000000 | bytes 7000000 | tf_op jit(solution)/shard_map/pallas_call | solution.py:91
  43.2 3.5 %collective-permute-start.14 = (f32[128,512]{1,0:T(8,128)S(1)}, f32[128,512]{1,0:T(8,128)S(1)}, u32[]{:S(2)}, u32[]{:S(2)}) collective-permute-start(f32[128,512]{1,0:T(8,128)S(1)} %copy-done.21), channel_id=1, source_target_pairs={{0,2},{1,3},{2,0},{3,1},{4,6},{5,7},{6,4},{7,5},{8,10},{9,11},{10,... | collective-permute-start | bytes 786440 | tf_op jit(solution)/shard_map/ppermute | solution.py:953
  47.5 1.5 collective-permute-start.11
  49.0 2.4 %shard_map.269 = (f32[2,8,512]{2,1,0:T(8,128)}, f32[14,8,128]{2,1,0:T(8,128)}, f32[8,16,128]{2,1,0:T(8,128)}) custom-call(s32[3]{0:T(128)} %pad_add_fusion.refs_0_, s32[2,896]{1,0:T(2,128)} %refs_2_.7, s32[2,896]{1,0:T(2,128)} %refs_2_.7, s32[2,896]{1,0:T(2,128)} %refs_3_.3, f32[2,8,768]{2,1,0:T(8,128)} %get-tuple-element.73.refs_4_, ...), custom_call_target="tpu_custom_call" | custom-call | flops 2200000000 | bytes 7000000 | tf_op jit(solution)/shard_map/pallas_call | solution.py:91
  51.4 5.2 %collective-permute-done.13.refs_0_.refs_3_ = f32[128,512]{1,0:T(8,128)S(1)} collective-permute-done((f32[128,512]{1,0:T(8,128)S(1)}, f32[128,512]{1,0:T(8,128)S(1)}, u32[]{:S(2)}, u32[]{:S(2)}) %collective-permute-start.13) | collective-permute-done | bytes 262176 | tf_op jit(solution)/shard_map/ppermute | solution.py:953
  56.6 1.5 collective-permute-start.12
  58.1 11.4 %shard_map.270 = (bf16[1792,1536]{1,0:T(8,128)(2,1)}, bf16[4,14,256,128]{3,2,1,0:T(8,128)(2,1)}, f32[4,14,8,128]{3,2,1,0:T(8,128)}, bf16[1792,512]{1,0:T(8,128)(...) custom-call(s32[3]{0:T(128)} %pad_add_fusion.refs_0_, f32[2,8,512]{2,1,0:T(8,128)} %get-tuple-element.75.refs_1_, ...), custom_call_target="tpu_custom_call" | custom-call | flops 11000000512 | bytes 35000000 | tf_op jit(solution)/shard_map/pallas_call | solution.py:91
  70.3 2.4 %shard_map.272 = (f32[192,512]{1,0:T(8,128)}, f32[192,512]{1,0:T(8,128)}) custom-call(f32[128,512]{1,0:T(8,128)} %copy-done.22, f32[128,512]{1,0:T(8,128)} %copy-done.23, f32[128,512]{1,0:T(8,128)} %copy-done.24, f32[128,512]{1,0:T(8,128)} %copy-done.22, f32[128,512]{1,0:T(8,128)} %copy-done.23, f32[128,512]{1,0:T(8,128)} %copy-done.24, ...), custom_call_target="tpu_custom_call" | custom-call | flops 2200000000 | bytes 7000000 | tf_op jit(solution)/shard_map/pallas_call | solution.py:91
  72.7 1.5 collective-permute-start.16
  74.8 0.8 copy-done.7
  75.7 0.8 copy-done.9
  76.5 2.9 %shard_map.273.refs_12_ = f32[4,240,512]{2,1,0:T(8,128)} custom-call(f32[240,512]{1,0:T(8,128)} %shard_map.267.refs_4_.refs_0_, f32[240,512]{1,0:T(8,128)} %copy-done.7, f32[240,512]{1,0:T(8,128)} %copy-done.8, f32[240,512]{1,0:T(8,128)} %copy-done.9, f32[192,512]{1,0:T(8,128)} %get-tuple-element.86.refs_4_.refs_0_), custom_call_target="tpu_custom_call" | custom-call | flops 2200000000 | bytes 7000000 | tf_op jit(solution)/shard_map/pallas_call | solution.py:91
  79.4 11.4 %shard_map.271 = (bf16[1792,1536]{1,0:T(8,128)(2,1)}, bf16[4,14,256,128]{3,2,1,0:T(8,128)(2,1)}, f32[4,14,8,128]{3,2,1,0:T(8,128)}, bf16[1792,512]{1,0:T(8,128)(...) custom-call(s32[3]{0:T(128)} %pad_add_fusion.refs_0_, ...), custom_call_target="tpu_custom_call", output_to_operand_aliasing={{0}: (9, {}), {1}: (10, {}), {2}: (11, {}), {3}: (12, {}), ... | custom-call | flops 11000000512 | bytes 35000000 | tf_op jit(solution)/shard_map/pallas_call | solution.py:91
  91.7 2.6 %shard_map.274.refs_13_ = f32[4,192,512]{2,1,0:T(8,128)} custom-call(f32[192,512]{1,0:T(8,128)} %get-tuple-element.86.refs_4_.refs_0_, f32[192,512]{1,0:T(8,128)} %copy-done.10, f32[192,512]{1,0:T(8,128)} %get-tuple-element.87.refs_2_, f32[192,512]{1,0:T(8,128)} %copy-done.11, bf16[1792,512]{1,0:T(8,128)(2,1)} %get-tuple-element.84.refs_4_.refs_3_), custom_call_target="tpu_custom_call" | custom-call | flops 2200000000 | bytes 7000000 | tf_op jit(solution)/shard_map/pallas_call | solution.py:91
  94.9 3.2 %collective-permute-done.19.refs_15_ = f32[4,192,512]{2,1,0:T(8,128)S(1)} collective-permute-done((f32[4,192,512]{2,1,0:T(8,128)}, f32[4,192,512]{2,1,0:T(8,128)S(1)}, u32[]{:S(2)}, u32[]{:S(2)}) %collective-permute-start.19) | collective-permute-done | bytes 1572896 | tf_op jit(solution)/shard_map/ppermute | solution.py:953
  98.1 1.2 copy-done.2
  99.3 38.7 %shard_map.275 = (bf16[1792,512]{1,0:T(8,128)(2,1)}, f32[1792,512]{1,0:T(8,128)}, bf16[1792,512]{1,0:T(8,128)(2,1)}, f32[512,512]{1,0:T(8,128)}, f32[512,512]{1,...) custom-call(s32[3]{0:T(128)} %pad_add_fusion.refs_0_, bf16[1792,512]{1,0:T(8,128)(2,1)} %bitcast.27, ...), custom_call_target="tpu_custom_call" | custom-call | flops 41799999488 | bytes 133000000 | tf_op jit(solution)/shard_map/pallas_call | solution.py:91
  138.0 9.2 %shard_map.276 = (bf16[1792,1536]{1,0:T(8,128)(2,1)}, f32[2,1,1536]{2,1,0:T(1,128)}, f32[512,384]{1,0:T(8,128)}) custom-call(s32[3]{0:T(128)} %pad_add_fusion.refs_0_, bf16[1792,1536]{1,0:T(8,128)(2,1)} %get-tuple-element.90.refs_1_, bf16[1792,512]{1,0:T(8,128)(2,1)} %get-tuple-element.91.refs_2_, bf16[4,14,256,128]{3,2,1,0:T(8,128)(2,1)} %get-tuple-element.92.refs_3_, ...), custom_call_target="tpu_custom_call" | custom-call | flops 6600000000 | bytes 21000000 | tf_op jit(solution)/shard_map/pallas_call | solution.py:91
  147.2 4.4 %shard_map.280 = (f32[4,192,512]{2,1,0:T(8,128)}, f32[4,192,512]{2,1,0:T(8,128)}) custom-call(s32[3]{0:T(128)} %pad_add_fusion.refs_0_, f32[512,512]{1,0:T(8,128)} %get-tuple-element.106.refs_1_, f32[512,512]{1,0:T(8,128)} %get-tuple-element.107.refs_2_, f32[128,512]{1,0:T(8,128)} %get-tuple-element.108.refs_3_, f32[512,384]{1,0:T(8,128)} %get-tuple-element.109.refs_4_), custom_call_target="tpu_custom_call" | custom-call | flops 2200000000 | bytes 7000000 | tf_op jit(solution)/shard_map/pallas_call | solution.py:91
  151.9 7.3 %shard_map.277 = (bf16[1792,1536]{1,0:T(8,128)(2,1)}, f32[2,1,1536]{2,1,0:T(1,128)}) custom-call(s32[3]{0:T(128)} %pad_add_fusion.refs_0_, bf16[1792,1536]{1,0:T(8,128)(2,1)} %get-tuple-element.90.refs_1_, bf16[1792,512]{1,0:T(8,128)(2,1)} %get-tuple-element.91.refs_2_, ...), custom_call_target="tpu_custom_call", output_to_operand_aliasing={{0}: (7, {}), {1}: (8, {})} | custom-call | flops 6600000000 | bytes 21000000 | tf_op jit(solution)/shard_map/pallas_call | solution.py:91
  159.2 1.1 copy-done.4
  160.4 3.9 %shard_map.281 = (f32[192,512]{1,0:T(8,128)}, f32[192,512]{1,0:T(8,128)}, f32[192,512]{1,0:T(8,128)}, f32[192,512]{1,0:T(8,128)}) custom-call(s32[3]{0:T(128)} %pad_add_fusion.refs_0_, f32[4,192,512]{2,1,0:T(8,128)} %get-tuple-element.110.refs_1_, f32[4,192,512]{2,1,0:T(8,128)} %copy-done.4, f32[2,1,1536]{2,1,0:T(1,128)} %get-tuple-element.98.refs_8_.refs_3_), custom_call_target="tpu_custom_call" | custom-call | flops 2200000000 | bytes 7000000 | tf_op jit(solution)/shard_map/pallas_call | solution.py:91
  164.7 1.5 collective-permute-start.22
  166.3 1.4 collective-permute-start.23
  167.7 11.5 %shard_map.278 = (bf16[1792,1536]{1,0:T(8,128)(2,1)}, f32[2,1,1536]{2,1,0:T(1,128)}) custom-call(s32[3]{0:T(128)} %pad_add_fusion.refs_0_, bf16[1792,1536]{1,0:T(8,128)(2,1)} %get-tuple-element.90.refs_1_, bf16[1792,512]{1,0:T(8,128)(2,1)} %get-tuple-element.91.refs_2_, ...), custom_call_target="tpu_custom_call", output_to_operand_aliasing={{0}: (7, {}), {1}: (8, {})} | custom-call | flops 13200000000 | bytes 42000000 | tf_op jit(solution)/shard_map/pallas_call | solution.py:91
  179.2 10.2 %all-gather = f32[16,1,1536]{2,1,0:T(1,128)} all-gather(f32[2,1,1536]{2,1,0:T(1,128)} %get-tuple-element.99.refs_4_), channel_id=2, replica_groups=mesh['seq'=8,'head'=4] {'seq'}, dimensions={0}, use_global_device_ids=true | all-gather | bytes 110592 | tf_op jit(solution)/shard_map/all_gather | solution.py:1036
  190.5 2.2 shard_map.282.refs_0_
  192.7 1.5 collective-permute-start.24
  194.7 1.5 collective-permute-start.26
  196.2 12.5 %shard_map.279 = (f32[1792,512]{1,0:T(8,128)}, f32[8,512]{1,0:T(8,128)}, f32[512,384]{1,0:T(8,128)}) custom-call(s32[3]{0:T(128)} %pad_add_fusion.refs_0_, f32[8,16,128]{2,1,0:T(8,128)} %get-tuple-element.89.refs_1_, f32[8,2,1,1536]{3,2,1,0:T(1,128)} %bitcast.23, f32[8,2,1,1536]{3,2,1,0:T(1,128)} %bitcast.24, f32[2,8,896]{2,1,0:T(8,128)} %get-tuple-element.100.refs_4_, ...), custom_call_target="tpu_custom_call" | custom-call | flops 13200000000 | bytes 42000000 | tf_op jit(solution)/shard_map/pallas_call | solution.py:91
  208.7 5.2 %collective-permute-done.25.refs_2_ = f32[192,512]{1,0:T(8,128)S(1)} collective-permute-done((f32[192,512]{1,0:T(8,128)}, f32[192,512]{1,0:T(8,128)S(1)}, u32[]{:S(2)}, u32[]{:S(2)}) %collective-permute-start.25) | collective-permute-done | bytes 393248 | tf_op jit(solution)/shard_map/ppermute | solution.py:953
  214.8 2.7 %shard_map.283.refs_1_ = f32[4,192,512]{2,1,0:T(8,128)} custom-call(f32[192,512]{1,0:T(8,128)} %shard_map.282.refs_0_, f32[192,512]{1,0:T(8,128)} %copy-done.13, f32[192,512]{1,0:T(8,128)} %copy-done.15, f32[192,512]{1,0:T(8,128)} %copy-done.17, f32[8,512]{1,0:T(8,128)} %get-tuple-element.116.refs_4_), custom_call_target="tpu_custom_call" | custom-call | flops 2200000000 | bytes 7000000 | tf_op jit(solution)/shard_map/pallas_call | solution.py:91
  217.4 9.3 %all-gather.1 = f32[64,512]{1,0:T(8,128)} all-gather(f32[8,512]{1,0:T(8,128)S(1)} %copy-done), channel_id=3, replica_groups=mesh['seq'=8,'head'=4] {'seq'}, dimensions={0}, use_global_device_ids=true | all-gather | bytes 147456 | tf_op jit(solution)/shard_map/all_gather | solution.py:1043
  226.7 1.1 copy-done.3
  227.8 4.6 %shard_map.284 = (f32[512,128]{1,0:T(8,128)}, f32[512,128]{1,0:T(8,128)}, f32[512,128]{1,0:T(8,128)}, f32[128,512]{1,0:T(8,128)}, f32[512,512]{1,0:T(8,128)}, /*...) custom-call(s32[3]{0:T(128)} %pad_add_fusion.refs_0_, ...), custom_call_target="tpu_custom_call" | custom-call | flops 2200000000 | bytes 7000000 | tf_op jit(solution)/shard_map/pallas_call | solution.py:91
  (95 shorter events, 13.8 us)
Async XLA Ops:
  3.4 6.0 %collective-permute-start = (f32[192,128]{1,0:T(8,128)}, f32[192,128]{1,0:T(8,128)S(1)}, u32[]{:S(2)}, u32[]{:S(2)}) collective-permute-start(f32[192,128]{1,0:T(8,128)} %shard_map.263), channel_id=1, source_target_pairs={{0,1},{1,0},{2,3},{3,2},{4,5},{5,4},{6,7},{7,6},{8,9},{9,8},{10,11... | collective-permute-start | bytes 294920 | tf_op jit(solution)/shard_map/ppermute | solution.py:953
  6.4 15.9 %collective-permute-start.1 = (f32[192,128]{1,0:T(8,128)}, f32[192,128]{1,0:T(8,128)S(1)}, u32[]{:S(2)}, u32[]{:S(2)}) collective-permute-start(f32[192,128]{1,0:T(8,128)} %shard_map.263), channel_id=1, source_target_pairs={{0,2},{1,3},{2,0},{3,1},{4,6},{5,7},{6,4},{7,5},{8,10},{9,11},{10,... | collective-permute-start | bytes 294920 | tf_op jit(solution)/shard_map/ppermute | solution.py:953
  9.0 13.3 %collective-permute-start.2 = (f32[192,128]{1,0:T(8,128)}, f32[192,128]{1,0:T(8,128)S(1)}, u32[]{:S(2)}, u32[]{:S(2)}) collective-permute-start(f32[192,128]{1,0:T(8,128)} %shard_map.263), channel_id=1, source_target_pairs={{0,3},{1,2},{2,1},{3,0},{4,7},{5,6},{6,5},{7,4},{8,11},{9,10},{10,... | collective-permute-start | bytes 294920 | tf_op jit(solution)/shard_map/ppermute | solution.py:953
  12.4 15.3 %collective-permute-start.6 = (f32[88,512]{1,0:T(8,128)}, f32[88,512]{1,0:T(8,128)S(1)}, u32[]{:S(2)}, u32[]{:S(2)}) collective-permute-start(f32[88,512]{1,0:T(8,128)} %get-tuple-element.72.refs_6_), channel_id=1, source_target_pairs={{0,1},{1,0},{2,3},{3,2},{4,5},{5,4},{6,7},{7,6},{8,9},{9,8},{10,11... | collective-permute-start | bytes 540680 | tf_op jit(solution)/shard_map/ppermute | solution.py:953
  14.2 16.6 %collective-permute-start.7 = (f32[88,512]{1,0:T(8,128)}, f32[88,512]{1,0:T(8,128)S(1)}, u32[]{:S(2)}, u32[]{:S(2)}) collective-permute-start(f32[88,512]{1,0:T(8,128)} %get-tuple-element.72.refs_6_), channel_id=1, source_target_pairs={{0,2},{1,3},{2,0},{3,1},{4,6},{5,7},{6,4},{7,5},{8,10},{9,11},{10,... | collective-permute-start | bytes 540680 | tf_op jit(solution)/shard_map/ppermute | solution.py:953
  17.8 13.0 %collective-permute-start.8 = (f32[88,512]{1,0:T(8,128)}, f32[88,512]{1,0:T(8,128)S(1)}, u32[]{:S(2)}, u32[]{:S(2)}) collective-permute-start(f32[88,512]{1,0:T(8,128)} %get-tuple-element.72.refs_6_), channel_id=1, source_target_pairs={{0,3},{1,2},{2,1},{3,0},{4,7},{5,6},{6,5},{7,4},{8,11},{9,10},{10,... | collective-permute-start | bytes 540680 | tf_op jit(solution)/shard_map/ppermute | solution.py:953
  24.6 10.0 %collective-permute-start.3 = (f32[592,128]{1,0:T(8,128)}, f32[592,128]{1,0:T(8,128)S(1)}, u32[]{:S(2)}, u32[]{:S(2)}) collective-permute-start(f32[592,128]{1,0:T(8,128)} %shard_map.266.refs_0_), channel_id=1, source_target_pairs={{0,8},{4,12},{8,0},{12,4},{16,24},{20,28},{24,16},{28,20},{1,9},{5... | collective-permute-start | bytes 909320 | tf_op jit(solution)/shard_map/ppermute | solution.py:953
  26.1 12.7 %collective-permute-start.4 = (f32[592,128]{1,0:T(8,128)}, f32[592,128]{1,0:T(8,128)S(1)}, u32[]{:S(2)}, u32[]{:S(2)}) collective-permute-start(f32[592,128]{1,0:T(8,128)} %shard_map.266.refs_0_), channel_id=1, source_target_pairs={{0,16},{4,20},{8,24},{12,28},{16,0},{20,4},{24,8},{28,12},{1,17},{... | collective-permute-start | bytes 909320 | tf_op jit(solution)/shard_map/ppermute | solution.py:953
  27.7 3.2 %copy-start.25 = (f32[88,512]{1,0:T(8,128)}, f32[88,512]{1,0:T(8,128)S(1)}, u32[]{:S(2)}) copy-start(f32[88,512]{1,0:T(8,128)S(1)} %collective-permute-done.6.refs_0_.refs_16_) | copy-start | bytes 540676
  27.7 11.1 %collective-permute-start.5 = (f32[592,128]{1,0:T(8,128)}, f32[592,128]{1,0:T(8,128)S(1)}, u32[]{:S(2)}, u32[]{:S(2)}) collective-permute-start(f32[592,128]{1,0:T(8,128)} %shard_map.266.refs_0_), channel_id=1, source_target_pairs={{0,24},{4,28},{8,16},{12,20},{16,8},{20,12},{24,0},{28,4},{1,25},{... | collective-permute-start | bytes 909320 | tf_op jit(solution)/shard_map/ppermute | solution.py:953
  34.1 8.5 %copy-start.21 = (f32[128,512]{1,0:T(8,128)S(1)}, f32[128,512]{1,0:T(8,128)}, u32[]{:S(2)}) copy-start(f32[128,512]{1,0:T(8,128)} %get-tuple-element.85) | copy-start | bytes 786436
  34.1 12.9 %copy-start.6 = (f32[240,512]{1,0:T(8,128)S(1)}, f32[240,512]{1,0:T(8,128)}, u32[]{:S(2)}) copy-start(f32[240,512]{1,0:T(8,128)} %shard_map.267.refs_4_.refs_0_) | copy-start | bytes 1474564
  34.6 4.2 %copy-start.18 = (f32[592,128]{1,0:T(8,128)}, f32[592,128]{1,0:T(8,128)S(1)}, u32[]{:S(2)}) copy-start(f32[592,128]{1,0:T(8,128)S(1)} %collective-permute-done.3.refs_1_) | copy-start | bytes 909316
  42.6 4.9 %collective-permute-start.9 = (f32[4,592,128]{2,1,0:T(8,128)}, f32[4,592,128]{2,1,0:T(8,128)S(1)}, u32[]{:S(2)}, u32[]{:S(2)}) collective-permute-start(f32[4,592,128]{2,1,0:T(8,128)} %shard_map.268.refs_5_.refs_7_), channel_id=1, source_target_pairs={{0,4},{4,0},{8,12},{12,8},{16,20},{20,16},{24,28},{28,24},{1,5},{5... | collective-permute-start | bytes 3637256 | tf_op jit(solution)/shard_map/ppermute | solution.py:953
  42.6 14.0 %collective-permute-start.13 = (f32[128,512]{1,0:T(8,128)S(1)}, f32[128,512]{1,0:T(8,128)S(1)}, u32[]{:S(2)}, u32[]{:S(2)}) collective-permute-start(f32[128,512]{1,0:T(8,128)S(1)} %copy-done.21), channel_id=1, source_target_pairs={{0,1},{1,0},{2,3},{3,2},{4,5},{5,4},{6,7},{7,6},{8,9},{9,8},{10,11... | collective-permute-start | bytes 786440 | tf_op jit(solution)/shard_map/ppermute | solution.py:953
  43.2 26.3 %collective-permute-start.14 = (f32[128,512]{1,0:T(8,128)S(1)}, f32[128,512]{1,0:T(8,128)S(1)}, u32[]{:S(2)}, u32[]{:S(2)}) collective-permute-start(f32[128,512]{1,0:T(8,128)S(1)} %copy-done.21), channel_id=1, source_target_pairs={{0,2},{1,3},{2,0},{3,1},{4,6},{5,7},{6,4},{7,5},{8,10},{9,11},{10,... | collective-permute-start | bytes 786440 | tf_op jit(solution)/shard_map/ppermute | solution.py:953
  46.7 22.9 %collective-permute-start.15 = (f32[128,512]{1,0:T(8,128)S(1)}, f32[128,512]{1,0:T(8,128)S(1)}, u32[]{:S(2)}, u32[]{:S(2)}) collective-permute-start(f32[128,512]{1,0:T(8,128)S(1)} %copy-done.21), channel_id=1, source_target_pairs={{0,3},{1,2},{2,1},{3,0},{4,7},{5,6},{6,5},{7,4},{8,11},{9,10},{10,... | collective-permute-start | bytes 786440 | tf_op jit(solution)/shard_map/ppermute | solution.py:953
  47.0 27.8 %collective-permute-start.10 = (f32[240,512]{1,0:T(8,128)S(1)}, f32[240,512]{1,0:T(8,128)S(1)}, u32[]{:S(2)}, u32[]{:S(2)}) collective-permute-start(f32[240,512]{1,0:T(8,128)S(1)} %copy-done.6), channel_id=1, source_target_pairs={{0,8},{4,12},{8,0},{12,4},{16,24},{20,28},{24,16},{28,20},{1,9},{5... | collective-permute-start | bytes 1474568 | tf_op jit(solution)/shard_map/ppermute | solution.py:953
  47.5 1.5 copy-start.5
  47.5 27.2 %collective-permute-start.11 = (f32[240,512]{1,0:T(8,128)S(1)}, f32[240,512]{1,0:T(8,128)S(1)}, u32[]{:S(2)}, u32[]{:S(2)}) collective-permute-start(f32[240,512]{1,0:T(8,128)S(1)} %copy-done.6), channel_id=1, source_target_pairs={{0,16},{4,20},{8,24},{12,28},{16,0},{20,4},{24,8},{28,12},{1,17},{... | collective-permute-start | bytes 1474568 | tf_op jit(solution)/shard_map/ppermute | solution.py:953
  56.6 12.9 %copy-start.22 = (f32[128,512]{1,0:T(8,128)}, f32[128,512]{1,0:T(8,128)S(1)}, u32[]{:S(2)}) copy-start(f32[128,512]{1,0:T(8,128)S(1)} %collective-permute-done.13.refs_0_.refs_3_) | copy-start | bytes 786436
  56.6 18.1 %collective-permute-start.12 = (f32[240,512]{1,0:T(8,128)S(1)}, f32[240,512]{1,0:T(8,128)S(1)}, u32[]{:S(2)}, u32[]{:S(2)}) collective-permute-start(f32[240,512]{1,0:T(8,128)S(1)} %copy-done.6), channel_id=1, source_target_pairs={{0,24},{4,28},{8,16},{12,20},{16,8},{20,12},{24,0},{28,4},{1,25},{... | collective-permute-start | bytes 1474568 | tf_op jit(solution)/shard_map/ppermute | solution.py:953
  69.6 0.8 copy-start.24
  72.7 18.1 %collective-permute-start.16 = (f32[192,512]{1,0:T(8,128)}, f32[192,512]{1,0:T(8,128)S(1)}, u32[]{:S(2)}, u32[]{:S(2)}) collective-permute-start(f32[192,512]{1,0:T(8,128)} %get-tuple-element.86.refs_4_.refs_0_), channel_id=1, source_target_pairs={{0,8},{4,12},{8,0},{12,4},{16,24},{20,28},{24,16},{28,20},{1,9},{5... | collective-permute-start | bytes 1179656 | tf_op jit(solution)/shard_map/ppermute | solution.py:953
  74.2 16.7 %collective-permute-start.17 = (f32[192,512]{1,0:T(8,128)}, f32[192,512]{1,0:T(8,128)S(1)}, u32[]{:S(2)}, u32[]{:S(2)}) collective-permute-start(f32[192,512]{1,0:T(8,128)} %get-tuple-element.87.refs_2_), channel_id=1, source_target_pairs={{0,16},{4,20},{8,24},{12,28},{16,0},{20,4},{24,8},{28,12},{1,17},{... | collective-permute-start | bytes 1179656 | tf_op jit(solution)/shard_map/ppermute | solution.py:953
  74.7 0.8 copy-start.7
  74.7 0.9 copy-start.8
  75.7 0.8 copy-start.9
  79.4 15.4 %collective-permute-start.18 = (f32[4,240,512]{2,1,0:T(8,128)}, f32[4,240,512]{2,1,0:T(8,128)S(1)}, u32[]{:S(2)}, u32[]{:S(2)}) collective-permute-start(f32[4,240,512]{2,1,0:T(8,128)} %shard_map.273.refs_12_), channel_id=1, source_target_pairs={{0,4},{4,0},{8,12},{12,8},{16,20},{20,16},{24,28},{28,24},{1,5},{5... | collective-permute-start | bytes 5898248 | tf_op jit(solution)/shard_map/ppermute | solution.py:953
  90.9 0.9 copy-start.11
  94.4 3.7 %collective-permute-start.19 = (f32[4,192,512]{2,1,0:T(8,128)}, f32[4,192,512]{2,1,0:T(8,128)S(1)}, u32[]{:S(2)}, u32[]{:S(2)}) collective-permute-start(f32[4,192,512]{2,1,0:T(8,128)} %shard_map.274.refs_13_), channel_id=1, source_target_pairs={{0,4},{4,0},{8,12},{12,8},{16,20},{20,16},{24,28},{28,24},{1,5},{5... | collective-permute-start | bytes 4718600 | tf_op jit(solution)/shard_map/ppermute | solution.py:953
  94.9 3.2 %copy-start.1 = (f32[4,240,512]{2,1,0:T(8,128)}, f32[4,240,512]{2,1,0:T(8,128)S(1)}, u32[]{:S(2)}) copy-start(f32[4,240,512]{2,1,0:T(8,128)S(1)} %collective-permute-done.18.refs_14_) | copy-start | bytes 5898244
  98.1 1.2 copy-start.2
  151.5 7.7 %collective-permute-start.20 = (f32[4,192,512]{2,1,0:T(8,128)}, f32[4,192,512]{2,1,0:T(8,128)S(1)}, u32[]{:S(2)}, u32[]{:S(2)}) collective-permute-start(f32[4,192,512]{2,1,0:T(8,128)} %get-tuple-element.111), channel_id=1, source_target_pairs={{0,4},{4,0},{8,12},{12,8},{16,20},{20,16},{24,28},{28,24},{1,5},{5... | collective-permute-start | bytes 4718600 | tf_op jit(solution)/shard_map/ppermute | solution.py:953
  159.2 1.1 copy-start.4
  164.2 25.2 %collective-permute-start.21 = (f32[192,512]{1,0:T(8,128)}, f32[192,512]{1,0:T(8,128)S(1)}, u32[]{:S(2)}, u32[]{:S(2)}) collective-permute-start(f32[192,512]{1,0:T(8,128)} %get-tuple-element.113), channel_id=1, source_target_pairs={{0,8},{4,12},{8,0},{12,4},{16,24},{20,28},{24,16},{28,20},{1,9},{5... | collective-permute-start | bytes 1179656 | tf_op jit(solution)/shard_map/ppermute | solution.py:953
  164.7 24.7 %collective-permute-start.22 = (f32[192,512]{1,0:T(8,128)}, f32[192,512]{1,0:T(8,128)S(1)}, u32[]{:S(2)}, u32[]{:S(2)}) collective-permute-start(f32[192,512]{1,0:T(8,128)} %get-tuple-element.114), channel_id=1, source_target_pairs={{0,16},{4,20},{8,24},{12,28},{16,0},{20,4},{24,8},{28,12},{1,17},{... | collective-permute-start | bytes 1179656 | tf_op jit(solution)/shard_map/ppermute | solution.py:953
  166.3 23.2 %collective-permute-start.23 = (f32[192,512]{1,0:T(8,128)}, f32[192,512]{1,0:T(8,128)S(1)}, u32[]{:S(2)}, u32[]{:S(2)}) collective-permute-start(f32[192,512]{1,0:T(8,128)} %get-tuple-element.115), channel_id=1, source_target_pairs={{0,24},{4,28},{8,16},{12,20},{16,8},{20,12},{24,0},{28,4},{1,25},{... | collective-permute-start | bytes 1179656 | tf_op jit(solution)/shard_map/ppermute | solution.py:953
  189.4 0.9 copy-start.14
  189.5 1.0 copy-start.16
  192.7 16.0 %collective-permute-start.24 = (f32[192,512]{1,0:T(8,128)}, f32[192,512]{1,0:T(8,128)S(1)}, u32[]{:S(2)}, u32[]{:S(2)}) collective-permute-start(f32[192,512]{1,0:T(8,128)} %shard_map.282.refs_0_), channel_id=1, source_target_pairs={{0,8},{4,12},{8,0},{12,4},{16,24},{20,28},{24,16},{28,20},{1,9},{5... | collective-permute-start | bytes 1179656 | tf_op jit(solution)/shard_map/ppermute | solution.py:953
  194.2 19.7 %collective-permute-start.25 = (f32[192,512]{1,0:T(8,128)}, f32[192,512]{1,0:T(8,128)S(1)}, u32[]{:S(2)}, u32[]{:S(2)}) collective-permute-start(f32[192,512]{1,0:T(8,128)} %shard_map.282.refs_0_), channel_id=1, source_target_pairs={{0,16},{4,20},{8,24},{12,28},{16,0},{20,4},{24,8},{28,12},{1,17},{... | collective-permute-start | bytes 1179656 | tf_op jit(solution)/shard_map/ppermute | solution.py:953
  194.7 19.2 %collective-permute-start.26 = (f32[192,512]{1,0:T(8,128)}, f32[192,512]{1,0:T(8,128)S(1)}, u32[]{:S(2)}, u32[]{:S(2)}) collective-permute-start(f32[192,512]{1,0:T(8,128)} %shard_map.282.refs_0_), channel_id=1, source_target_pairs={{0,24},{4,28},{8,16},{12,20},{16,8},{20,12},{24,0},{28,4},{1,25},{... | collective-permute-start | bytes 1179656 | tf_op jit(solution)/shard_map/ppermute | solution.py:953
  208.7 5.2 %copy-start.13 = (f32[192,512]{1,0:T(8,128)}, f32[192,512]{1,0:T(8,128)S(1)}, u32[]{:S(2)}) copy-start(f32[192,512]{1,0:T(8,128)S(1)} %collective-permute-done.24.refs_1_) | copy-start | bytes 1179652
  213.9 0.9 copy-start.17
  214.8 2.7 %copy-start = (f32[8,512]{1,0:T(8,128)S(1)}, f32[8,512]{1,0:T(8,128)}, u32[]{:S(2)}) copy-start(f32[8,512]{1,0:T(8,128)} %get-tuple-element.116.refs_4_) | copy-start | bytes 49156
  217.4 9.3 %collective-permute-start.27 = (f32[4,192,512]{2,1,0:T(8,128)}, f32[4,192,512]{2,1,0:T(8,128)S(1)}, u32[]{:S(2)}, u32[]{:S(2)}) collective-permute-start(f32[4,192,512]{2,1,0:T(8,128)} %shard_map.283.refs_1_), channel_id=1, source_target_pairs={{0,4},{4,0},{8,12},{12,8},{16,20},{20,16},{24,28},{28,24},{1,5},{5... | collective-permute-start | bytes 4718600 | tf_op jit(solution)/shard_map/ppermute | solution.py:953
  226.7 1.1 copy-start.3
  (11 other events, 7.7 us)

commit v3 on v2

v3 whole, which is shorter than its diff:
```python
import math

import jax
import jax.numpy as jnp
from jax import lax
from jax.experimental import pallas as pl
from jax.experimental.pallas import tpu as pltpu
from jax.sharding import PartitionSpec as P

HEAD_DIM = 64
SPAN = 128
LANES = 128
NORM_EPS = 1e-05
MASKED = -1e30
f32, bf16 = jnp.float32, jnp.bfloat16


def nn(a, b):
    return lax.dot_general(a, b, (((1,), (0,)), ((), ())), preferred_element_type=f32)


def nt(a, b):
    return lax.dot_general(a, b, (((1,), (1,)), ((), ())), preferred_element_type=f32)


def tn(a, b):
    return lax.dot_general(a, b, (((0,), (0,)), ((), ())), preferred_element_type=f32)


def hi_lo(v):
    hi = v.astype(bf16).astype(f32)
    return jnp.concatenate([hi, v - hi], axis=0).astype(bf16)


def twice(v):
    return jnp.concatenate([v, v], axis=0).astype(bf16)


def norm_parts(x):
    mean = jnp.mean(x, axis=-1, keepdims=True)
    centred = x - mean
    rstd = lax.rsqrt(jnp.mean(centred * centred, axis=-1, keepdims=True) + NORM_EPS)
    return centred * rstd, rstd


def norm_back(y, xhat, rstd):
    return rstd * (
        y
        - jnp.mean(y, axis=-1, keepdims=True)
        - xhat * jnp.mean(y * xhat, axis=-1, keepdims=True)
    )


def gelu_parts(u):
    z = jnp.abs(u)
    t = 1.0 / (1.0 + (0.3275911 * math.sqrt(0.5)) * z)
    e = jnp.exp(-0.5 * u * u)
    poly = t * (
        0.5 * 0.254829592
        + t
        * (
            0.5 * -0.284496736
            + t * (0.5 * 1.421413741 + t * (0.5 * -1.453152027 + t * (0.5 * 1.061405429)))
        )
    )
    tail = poly * e
    phi = jnp.where(u >= 0.0, 1.0 - tail, tail)
    return phi, phi + u * e * (1.0 / math.sqrt(2.0 * math.pi))


def call(body, grid, prefetch, in_specs, out_specs, out_shape, scratch=(), us=2, mib=6, aliases=None, after=()):
    first, last = prefetch + len(in_specs), prefetch + len(in_specs) + len(after)

    def only(*refs):
        body(*refs[:first], *refs[last:])

    kernel = pl.pallas_call(
        only,
        input_output_aliases=aliases or {},
        grid_spec=pltpu.PrefetchScalarGridSpec(
            num_scalar_prefetch=prefetch,
            grid=grid,
            in_specs=list(in_specs) + [pl.BlockSpec(memory_space=pl.ANY)] * len(after),
            out_specs=out_specs,
            scratch_shapes=list(scratch),
        ),
        out_shape=out_shape,
        compiler_params=pltpu.CompilerParams(vmem_limit_bytes=mib * 2**20),
        cost_estimate=pl.CostEstimate(flops=int(us * 1.1e9), bytes_accessed=int(us * 3.5e6), transcendentals=0),
    )
    return lambda *operands: kernel(*operands, *after)


def whole(shape):
    return pl.BlockSpec(shape, lambda *_: (0,) * len(shape))


def shape(dims, dtype):
    return jax.ShapeDtypeStruct(dims, dtype)


def halves():
    lane = lax.broadcasted_iota(jnp.int32, (1, LANES), 1)
    first = (lane < HEAD_DIM).astype(f32)
    return first.astype(bf16), (1.0 - first).astype(bf16)


def split(v, masks):
    return jnp.concatenate([v * masks[0], v * masks[1]], axis=0)


def head_lines(bars):
    line = lax.broadcasted_iota(jnp.int32, (8, LANES), 0)
    lane = lax.broadcasted_iota(jnp.int32, (8, LANES), 1)
    own = lane // HEAD_DIM == line
    lines = [jnp.where(own, bars[s : s + 1], 0.0) for s in range(bars.shape[0])]
    return jnp.concatenate(lines, axis=0).astype(bf16)


def eight(rows):
    return jnp.concatenate(rows + [jnp.zeros((8 - len(rows), rows[0].shape[1]), f32)], axis=0)


def diagonal(blocks, lines):
    zero = jnp.zeros_like(blocks[0])
    rows = [jnp.concatenate([b if i == j else zero for j in range(len(blocks))], axis=1) for i, b in enumerate(blocks)]
    rows += [jnp.zeros_like(rows[0])] * (lines - len(blocks))
    return jnp.concatenate(rows, axis=0).astype(bf16)


def from_hbm(*arrays):
    return [pltpu.with_memory_space_constraint(v, pltpu.HBM) for v in arrays]


def put_shares(at_s, ins, both_ref, one_ref):
    at = 0
    for ref in ins:
        rows = ref.shape[0] // 2
        both_ref[2 * at : 2 * (at + rows)] = ref[...].astype(f32)
        mine = pl.ds(pl.multiple_of(at_s[0] % 2 * rows, rows), rows)
        one_ref[at : at + rows] = ref[mine].astype(f32)
        at += rows


def shares_body(at_s, *refs):
    put_shares(at_s, refs[:3], *refs[3:])


def attention_share(at, wq, wk, wv, devices):
    width, share = wq.shape
    rows = width // devices
    spec = pl.BlockSpec((2 * rows, share), lambda i, s: (s[0] // 2, 0))
    outs = [shape((6 * rows, share), f32), shape((3 * rows, share), f32)]
    return call(
        shares_body, (1,), 1, [spec] * 3, [whole(v.shape) for v in outs], outs
    )(at, *from_hbm(wq, wk, wv))


def hidden_body(at_s, u_ref, o_ref, b_ref, upper_ref, lower_ref, up_both, up_one, down_both, down_one):
    put_shares(at_s, (u_ref, o_ref), up_both, up_one)
    for ref in (up_both, up_one):
        ref[ref.shape[0] - 8 :] = jnp.broadcast_to(b_ref[...], (8, b_ref.shape[1]))
    put_shares(at_s, (upper_ref, lower_ref), down_both, down_one)


def hidden_share(at, wu, wo, bu, wd, devices, after):
    width, hidden = wu.shape
    rows, lines, deep = width // devices, wo.shape[0] // devices, 2 * hidden // devices
    chip = lambda i, s: (s[0] // 2, 0)
    heights = [2 * (rows + lines) + 8, rows + lines + 8, 2 * deep, deep]
    outs = [shape((n, width), f32) for n in heights]
    return call(
        hidden_body,
        (1,),
        1,
        [
            pl.BlockSpec((2 * rows, hidden), chip),
            pl.BlockSpec((2 * lines, width), chip),
            whole((1, hidden)),
            pl.BlockSpec((deep, width), lambda i, s: (s[0] // 2 % 2, 0)),
            pl.BlockSpec((deep, width), lambda i, s: (2 + s[0] // 4, 0)),
        ],
        [whole(v.shape) for v in outs],
        outs,
        after=after,
    )(at, *from_hbm(wu, wo, bu[None], wd, wd))


def cat(groups, after=()):
    arrays, outs = [], []
    for group in groups:
        arrays += [v for v, _, _ in group]
        outs.append(shape((sum(n for _, _, n in group),) + group[0][0].shape[1:], f32))

    def body(*refs):
        ins, got = refs[: len(arrays)], 0
        for group, out in zip(groups, refs[len(arrays) :]):
            at = 0
            for _, first, n in group:
                out[at : at + n] = ins[got][first : first + n]
                at += n
                got += 1

    return call(body, (1,), 0, [whole(v.shape) for v in arrays], [whole(v.shape) for v in outs], outs, after=after)(*arrays)


def norm_body(spans, doc_s, doc_ref, pad_ref, x_ref, g_ref, b_ref, h_ref, m_ref, p_ref, t_ref):
    row_at = pl.program_id(0)
    width = x_ref.shape[-1]
    xhat, _ = norm_parts(x_ref[...].astype(f32))
    h = (xhat * g_ref[...] + b_ref[...]).astype(bf16)
    h_ref[...] = h
    doc = doc_ref[pl.ds(row_at, 1)]
    alive = pad_ref[pl.ds(row_at, 1)] == 1
    rows, region = m_ref.shape[1:]
    lane = lax.broadcasted_iota(jnp.int32, (rows, region), 1)
    line = lax.broadcasted_iota(jnp.int32, (rows, region), 0)
    tag_line = lax.broadcasted_iota(jnp.int32, (rows, LANES), 0)
    picked = jnp.zeros((rows, region), f32)
    tag = jnp.zeros((rows, LANES), f32)
    for s in range(1, spans + 1):
        last = doc_s[row_at, s * SPAN - 1]
        hit = (line == s) & (lane < s * SPAN) & (doc == last) & alive
        picked = jnp.where(hit, 1.0, picked)
        tag = jnp.where(tag_line == s, last.astype(f32), tag)
    m_ref[0] = picked
    sums = nn(picked.astype(bf16), h)
    count = jnp.broadcast_to(jnp.sum(picked, axis=1, keepdims=True), (rows, LANES))
    p_ref[0, :, :width] = sums
    p_ref[0, :, width : width + LANES] = count
    p_ref[0, :, width + LANES :] = tag
    tiles = width // LANES
    for c in range(tiles):
        t_ref[0, c : c + 1] = sums[spans : spans + 1, c * LANES : (c + 1) * LANES]
    t_ref[0, tiles : tiles + 1] = count[spans : spans + 1]
    t_ref[0, tiles + 1 : tiles + 2] = tag[spans : spans + 1]
    t_ref[0, tiles + 2 :] = jnp.zeros((8 - tiles - 2, LANES), f32)


def first_norm(docs, pads, x, gain, shift, rows, region, after):
    tokens, width = x.shape
    spans = region // SPAN
    lines = -(-(spans + 1) // 8) * 8
    wide = width + 2 * LANES
    tok = pl.BlockSpec((region, width), lambda i, *_: (i, 0))

    def row(n, w):
        return pl.BlockSpec((1, n, w), lambda i, *_: (i, 0, 0))

    def body(*refs):
        norm_body(spans, *refs)

    return call(
        body,
        (rows,),
        1,
        [whole(docs.shape), whole(docs.shape), tok, whole((1, width)), whole((1, width))],
        [tok, row(lines, region), row(lines, wide), row(8, LANES)],
        [
            shape((tokens, width), bf16),
            shape((rows, lines, region), f32),
            shape((rows, lines, wide), f32),
            shape((rows, 8, LANES), f32),
        ],
        after=after,
        us=4,
    )(docs, docs, pads, x, gain[None], shift[None])


def state_of(every_ref, d, row_at, tiles):
    lines = every_ref[d, row_at * 8 : row_at * 8 + 8]
    sums = jnp.concatenate([lines[c : c + 1] for c in range(tiles)], axis=1)
    return sums, lines[tiles : tiles + 1], lines[tiles + 1 : tiles + 2]


def owners(me, refs):
    half = len(refs) // 2
    return [(me ^ (2 * (i % half) + i // half), ref) for i, ref in enumerate(refs)]


def means_body(rows, spans, take, me_s, doc_s, doc_ref, pad_ref, p_ref, mean_ref, misc_ref, every_ref):
    me = me_s[0]
    take(me)
    devices = every_ref.shape[0]
    width = mean_ref.shape[-1]
    tiles = width // LANES
    mean_ref[...] = jnp.zeros_like(mean_ref)
    misc_ref[...] = jnp.zeros_like(misc_ref)
    for row_at in range(rows):
        sums = carry = jnp.zeros((1, width), f32)
        count = carry_count = jnp.zeros((1, LANES), f32)
        tag = tag_in = jnp.full((1, LANES), -1.0, f32)
        for d in range(1, devices):
            new_sums, new_count, new_tag = state_of(every_ref, d - 1, row_at, tiles)
            same = (new_tag == tag).astype(f32)
            sums = new_sums + same[:, :1] * sums
            count = new_count + same * count
            tag = new_tag
            mine = me == d
            carry = jnp.where(mine, sums, carry)
            carry_count = jnp.where(mine, count, carry_count)
            tag_in = jnp.where(mine, tag, tag_in)
        for s in range(spans):
            if s == 0:
                run_doc = tag_in
            else:
                run_doc = jnp.full((1, LANES), doc_s[row_at, s * SPAN - 1].astype(f32))
            flag = (tag_in == run_doc).astype(f32)
            total = p_ref[row_at, s : s + 1, :width] + flag[:, :1] * carry
            count_here = p_ref[row_at, s : s + 1, width : width + LANES] + flag * carry_count
            divisor = jnp.maximum(count_here, 1.0)
            mean_ref[row_at, s : s + 1] = total / divisor[:, :1]
            at = row_at * spans + s
            toks = slice(s * SPAN, (s + 1) * SPAN)
            doc = doc_ref[row_at : row_at + 1, toks].astype(f32)
            misc_ref[at, 0:1] = 1.0 / divisor
            misc_ref[at, 1:2] = flag
            misc_ref[at, 2:3] = run_doc
            misc_ref[at, 3:4] = count_here
            misc_ref[at, 4:5] = doc
            misc_ref[at, 5:6] = jnp.where(pad_ref[row_at : row_at + 1, toks] == 1, doc, -2.0)


def document_means(me, docs, pads, prefix, sent, devices, rows, region):
    spans = region // SPAN
    lines = prefix.shape[1]
    width = prefix.shape[2] - 2 * LANES
    in_order = len(sent) == 1
    tall = rows * 8
    outs = [
        shape((rows, lines, width), f32),
        shape((rows * spans, 8, LANES), f32),
        shape((devices, tall, LANES), f32),
    ]

    def body(me_s, doc_s, doc_ref, pad_ref, p_ref, *refs):
        got, outs = refs[: len(sent)], refs[len(sent) :]

        def take(me):
            if in_order:
                outs[2][...] = got[0][...]
                return
            for owner, ref in owners(me, got):
                outs[2][owner] = ref[...]

        means_body(rows, spans, take, me_s, doc_s, doc_ref, pad_ref, p_ref, *outs)

    def tail(v):
        if in_order:
            return whole(v.shape)
        last = v.shape[0] // tall - 1
        return pl.BlockSpec((tall, LANES), lambda *_: (last, 0))

    return call(
        body,
        (1,),
        2,
        [whole(docs.shape), whole(docs.shape), whole(prefix.shape)] + [tail(v) for v in sent],
        [whole(v.shape) for v in outs],
        outs,
    )(me, docs, docs, pads, prefix, *sent)


def take_pieces(at_s, k, came, w_ref):
    here = at_s[0]
    rows = w_ref.shape[0] // len(came)

    def take(ref, first, owner, n):
        at = pl.ds(pl.multiple_of(owner * n, n), n)
        for i in range(3):
            w_ref[at, i * LANES : (i + 1) * LANES] = ref[first + i * n : first + (i + 1) * n].astype(bf16)

    if k == 3:
        for owner, ref in owners(here, came):
            take(ref, 6 * rows, owner, rows)
        return
    half = len(came) // 2
    for core in range(2):

        @pl.when((here + core) % 2 == k - 1)
        def _():
            for j in range(half):
                take(came[core * half + j], 0, here // 2 ^ j, 2 * rows)


def pair_body(load, mean_ref, misc_ref, h_ref, w_ref, qkv_ref, p_ref, ps_ref, o_ref, bar_ref, mix_s):
    load()
    rows = mean_ref.shape[0]
    region = h_ref.shape[0] // rows
    both = nn(hi_lo(mean_ref[...].reshape(-1, mean_ref.shape[-1])), w_ref[:, LANES:])
    half = both.shape[0] // 2
    bars = both[:half] + both[half:]
    bar_ref[0] = bars.reshape(bar_ref.shape[1:])
    masks = halves()
    u = lax.broadcasted_iota(jnp.int32, (SPAN, SPAN), 0)
    t = lax.broadcasted_iota(jnp.int32, (SPAN, SPAN), 1)
    lines = half // rows
    for row_at in range(rows):
        here = slice(row_at * region, (row_at + 1) * region)
        qkv = nn(h_ref[here], w_ref[...])
        qkv_ref[here, :LANES] = (qkv[:, :LANES] * (1.0 / math.sqrt(HEAD_DIM))).astype(bf16)
        qkv_ref[here, LANES:] = qkv[:, LANES:].astype(bf16)
        bars_here = bars[row_at * lines : (row_at + 1) * lines]
        k_lines, v_lines = head_lines(bars_here[:, :LANES]), head_lines(bars_here[:, LANES:])
        summaries = nt(k_lines, qkv_ref[here, :LANES]) + math.log(SPAN)
        all_weights = []
        for s in range(region // SPAN):
            at = row_at * (region // SPAN) + s
            inside = slice(s * SPAN, (s + 1) * SPAN)
            toks = slice(at * SPAN, (at + 1) * SPAN)
            q, k, v = (qkv_ref[toks, i * LANES : (i + 1) * LANES] for i in range(3))
            doc, code = misc_ref[at, 4:5], misc_ref[at, 5:6]
            ok = ((u < t) & (jnp.broadcast_to(code, (SPAN, SPAN)).T == doc)) | (u == t)
            present = (doc == misc_ref[at, 2:3]) & (misc_ref[at, 3:4] > 0.0)
            scores = nt(split(k, masks), q)
            probs, weights = [], []
            for half_at in range(2):
                score = jnp.where(ok, scores[half_at * SPAN : (half_at + 1) * SPAN], MASKED)
                far = jnp.where(present, summaries[8 * s + half_at : 8 * s + half_at + 1, inside], MASKED)
                top = jnp.maximum(jnp.max(score, axis=0, keepdims=True), far)
                e = jnp.exp(score - top)
                w = jnp.exp(far - top)
                inverse = 1.0 / (jnp.sum(e, axis=0, keepdims=True) + w)
                probs.append((e * inverse).astype(bf16))
                weights.append(w * inverse)
            probs = jnp.concatenate(probs, axis=0)
            weights = eight(weights)
            p_ref[0, at] = probs
            ps_ref[0, at] = weights
            all_weights.append(weights)
            mix_s[toks] = tn(probs, split(v, masks))
        o_ref[here] = (mix_s[here] + tn(diagonal(all_weights, lines), v_lines)).astype(bf16)


def pair_forward(at, means, misc, h, source, first, parts, region, kept):
    tokens, width = h.shape
    rows = tokens // region
    spans = region // SPAN
    pairs = width // LANES
    lines = means.shape[1]
    kind, *weights = source

    def pair(i, s):
        return i if kind == "all" else s[1] ^ (first + i)

    in_specs = [whole(means.shape), whole(misc.shape), whole(h.shape)]
    w_spec = pl.BlockSpec((width, 3 * LANES), lambda i, s: (0, pair(i, s)))
    if kind == "all":
        in_specs.append(w_spec)
    else:
        in_specs += [whole(w.shape) for w in weights]
    out_specs = [
        pl.BlockSpec((tokens, 3 * LANES), lambda i, s: (0, pair(i, s))),
        pl.BlockSpec((1, rows * spans, 2 * SPAN, SPAN), lambda i, s: (pair(i, s), 0, 0, 0)),
        pl.BlockSpec((1, rows * spans, 8, SPAN), lambda i, s: (pair(i, s), 0, 0, 0)),
        pl.BlockSpec((tokens, LANES), lambda i, s: (0, pair(i, s))),
        pl.BlockSpec((1, rows, lines, 2 * LANES), lambda i, s: (pair(i, s), 0, 0, 0)),
    ]
    out_shape = [
        shape((tokens, 3 * width), bf16),
        shape((pairs, tokens // SPAN, 2 * SPAN, SPAN), bf16),
        shape((pairs, tokens // SPAN, 8, SPAN), f32),
        shape((tokens, width), bf16),
        shape((pairs, rows, lines, 2 * LANES), f32),
    ]
    if kind != "all":
        out_specs.append(w_spec)
        out_shape.append(shape((width, 3 * width), bf16))
    n_in = 3 + len(weights)
    kept = list(kept or ())

    def body(at_s, *refs):
        ins, got, outs, mix_s = refs[:3], refs[3:n_in], refs[n_in + len(kept) : -1], refs[-1]
        if kind == "all":
            w_ref = got[0]
            load = lambda: None
        else:
            w_ref = outs[5]

            def load():
                for i in range(parts):

                    @pl.when(pl.program_id(0) == i)
                    def _(i=i):
                        if first + i == 0:
                            for m in range(3):
                                w_ref[:, m * LANES : (m + 1) * LANES] = got[m][...]
                        else:
                            take_pieces(at_s, first + i, got[3:], w_ref)

        pair_body(load, *ins, w_ref, *outs[:5], mix_s)

    return call(
        body,
        (parts,),
        1,
        in_specs + [pl.BlockSpec(memory_space=pl.ANY)] * len(kept),
        out_specs,
        out_shape,
        us=5 * parts,
        mib=12,
        aliases={1 + n_in + i: i for i in range(len(kept))},
        scratch=[pltpu.VMEM((tokens, LANES), f32)],
    )(at, means, misc, h, *weights, *kept)


def take_hidden(at_s, own, ups, downs, wu_s, wo_s, wd_s, bu_s):
    here, group = at_s[0], at_s[2]
    lines = own[1].shape[0]
    wu_s[group] = own[0][...]
    wo_s[pl.ds(pl.multiple_of(group * lines, lines), lines)] = own[1][...]
    bu_s[group] = jnp.broadcast_to(own[2][...], bu_s.shape[1:])
    wd_s[group] = own[3][...]
    rows, thin = wu_s.shape[1] // 8, lines // 8
    thick = 3 * (rows + thin)
    deep = downs[0].shape[0] // 12
    for core in range(2):
        up, down = ups[core], downs[core]
        sender = (here ^ core) % 2
        near = group ^ (1 + sender)
        bu_s[near] = up[4 * thick :]
        for j in range(4):
            owner = here ^ (2 * j + core)
            first = j * thick
            for to, who, n in ((near, owner // 2, 2), (group ^ 3, owner, 1)):
                at = pl.multiple_of(who * n * rows, n * rows)
                wu_s[to, pl.ds(at, n * rows)] = up[first : first + n * rows].astype(bf16)
                first += n * rows
                at = pl.multiple_of(to * lines + who * n * thin, n * thin)
                wo_s[pl.ds(at, n * thin)] = up[first : first + n * thin].astype(bf16)
                first += n * thin
            chip = here ^ (0, 0, 2, 4)[j]
            place = 4 + chip // 4 * 2 if j % 2 else chip // 2 % 2 * 2
            at = pl.multiple_of(place * deep, 2 * deep)
            wd_s[near, pl.ds(at, 2 * deep)] = down[3 * j * deep : (3 * j + 2) * deep].astype(bf16)
            at = pl.multiple_of((place + sender) * deep, deep)
            wd_s[group ^ 3, pl.ds(at, deep)] = down[(3 * j + 2) * deep : (3 * j + 3) * deep].astype(bf16)


def ffn_body(
    at_s, x_ref, g_ref, o_ref, mine_ref, gain_ref, shift_ref, bd_ref, load, wo_ref,
    out_ref, dmid_ref, do_ref, gwo_ref, gbu_ref, small_ref, gwu_ref, gwd_ref, wu_ref, wd_ref, bu_ref, a_s, du_s,
):
    @pl.when(pl.program_id(0) == 0)
    def _():
        load()
        gwu_ref[...] = jnp.zeros_like(gwu_ref)
        gwd_ref[...] = jnp.zeros_like(gwd_ref)
        gwo_ref[...] = jnp.zeros_like(gwo_ref)
        gbu_ref[...] = jnp.zeros_like(gbu_ref)
        small_ref[...] = jnp.zeros_like(small_ref)

    mid = x_ref[...].astype(f32) + nn(o_ref[...], wo_ref[...])
    xhat, rstd = norm_parts(mid)
    h = (xhat * gain_ref[...] + shift_ref[...]).astype(bf16)
    gm = g_ref[...]
    y = dn = None
    n = wu_ref.shape[0]
    for j in range(n):
        up = nn(h, wu_ref[j]) + bu_ref[j, :1]
        da = nt(gm, wd_ref[j])
        if j > 0:
            y_part = nn(a, wd_ref[j - 1])
            dn_part = nt(du, wu_ref[j - 1])
            y = y_part if y is None else y + y_part
            dn = dn_part if dn is None else dn + dn_part
        phi, slope = gelu_parts(up)
        a = (up * phi).astype(bf16)
        du = (da * slope).astype(bf16)
        a_s[j] = a
        du_s[j] = du
    y = y + nn(a, wd_ref[n - 1])
    dn = dn + nt(du, wu_ref[n - 1])
    out_ref[...] = (mid + y + bd_ref[...]).astype(bf16)
    g = gm.astype(f32)
    small_ref[2:3] += jnp.sum(dn * xhat, axis=0, keepdims=True)
    small_ref[3:4] += jnp.sum(dn, axis=0, keepdims=True)
    small_ref[4:5] += jnp.sum(g, axis=0, keepdims=True)
    dmid = g + norm_back(dn * gain_ref[...], xhat, rstd)
    dmid_ref[...] = dmid
    gx = dmid.astype(bf16)
    do_ref[...] = nt(gx, wo_ref[...]).astype(bf16)
    gwo_ref[...] += tn(mine_ref[...], gx)
    group = at_s[2]
    du = du_s[group]
    gwd_ref[...] += tn(a_s[group], gm)
    gwu_ref[...] += tn(h, du)
    gbu = jnp.sum(du.astype(f32), axis=0, keepdims=True)
    gbu_ref[...] += gbu
    if gbu.shape[1] == small_ref.shape[1]:
        small_ref[5:6] += gbu


def by_core(core, keep_ref, give_ref):
    return (keep_ref, core), (give_ref, 1 - core)


def feed_forward(at, x, g, o, gain, shift, bd, source, devices):
    tokens, width = x.shape
    kind, *weights = source
    came = kind == "came"
    if came:
        *own, ups, downs, bias = weights
        hidden, groups = own[0].shape[1], 4
        args = [*own, *ups, *downs, bias]
        n_up, n_down = 4 + len(ups), 4 + len(ups) + len(downs)
        last = bias.shape[0] // 8 - 1
        specs = [whole(w.shape) for w in args[:n_down]] + [pl.BlockSpec((8, width), lambda i, *_: (last, 0))]
    else:
        args = weights
        groups, _, hidden = args[0].shape
        specs = [whole(w.shape) for w in args]
    steps = 4
    chunk = tokens // steps
    tok = pl.BlockSpec((chunk, width), lambda i, *_: (i, 0))
    n_w = len(args)
    scratch = [pltpu.VMEM((groups, chunk, hidden), bf16)] * 2
    grads = [shape((width, hidden), f32), shape((hidden, width), f32)]
    if came:
        scratch += [pltpu.VMEM(v.shape, f32) for v in grads]
        scratch += [
            pltpu.VMEM((groups, width, hidden), bf16),
            pltpu.VMEM((width, width), bf16),
            pltpu.VMEM((groups, 8, hidden), f32),
            pltpu.VMEM((groups, hidden, width), bf16),
        ]
        grads = [shape((devices // 2, (width + hidden) // devices, width), f32)] * 2

    def body(at_s, *refs):
        ins, got = refs[:7], refs[7 : 7 + n_w]
        outs, acts, held = refs[7 + n_w : 15 + n_w], refs[15 + n_w : 17 + n_w], refs[17 + n_w :]
        if not came:
            wu_r, wo_r, bu_r, wd_r = got
            ffn_body(at_s, *ins, lambda: None, wo_r, *outs, wu_r, wd_r, bu_r, *acts)
            return
        gwu_s, gwd_s, wu_s, wo_s, bu_s, wd_s = held

        def load():
            take_hidden(at_s, got[:4], got[4:n_up], got[n_up:n_down], wu_s, wo_s, wd_s, bu_s)
            bu_s[at_s[2] ^ 3] = got[n_down][...]

        ffn_body(at_s, *ins, load, wo_s, *outs[:6], gwu_s, gwd_s, wu_s, wd_s, bu_s, *acts)

        @pl.when(pl.program_id(0) == steps - 1)
        def _():
            rows = width // devices
            for out, c in by_core(at_s[0] % 2, *outs[6:]):
                for j in range(devices // 2):
                    lines = pl.ds(pl.multiple_of((2 * j + c) * rows, rows), rows)
                    out[j, :rows] = gwu_s[lines]
                    out[j, rows:] = gwd_s[lines]

    return call(
        body,
        (steps,),
        1,
        [tok, tok, tok, pl.BlockSpec((chunk, LANES), lambda i, s: (i, s[1])),
         whole((1, width)), whole((1, width)), whole((1, width))] + specs,
        [tok, tok, tok, whole((LANES, width)), whole((1, hidden)), whole((8, width))] + [whole(v.shape) for v in grads],
        [
            shape((tokens, width), bf16),
            shape((tokens, width), f32),
            shape((tokens, width), bf16),
            shape((LANES, width), f32),
            shape((1, hidden), f32),
            shape((8, width), f32),
        ] + grads,
        scratch=scratch,
        us=38,
        mib=26,
    )(at, x, g, o, o, gain[None], shift[None], bd[None], *args)


def pair_back_body(rows, qkv_ref, do_ref, p_ref, ps_ref, bar_ref, misc_ref, d_ref, g_ref, d_s):
    masks = halves()
    wide = 2 * LANES
    region = do_ref.shape[0] // rows
    spans = region // SPAN
    for row_at in range(rows):
        here = slice(row_at * region, (row_at + 1) * region)
        bars = bar_ref[0, row_at]
        lines = bars.shape[0]
        k_lines, v_lines = head_lines(bars[:, :LANES]), head_lines(bars[:, LANES:])
        dp_far = nt(v_lines, do_ref[here])
        all_far, all_weights = [], []
        for s in range(spans):
            at = row_at * spans + s
            inside = slice(s * SPAN, (s + 1) * SPAN)
            toks = slice(at * SPAN, (at + 1) * SPAN)
            q, k, v = (qkv_ref[toks, i * LANES : (i + 1) * LANES] for i in range(3))
            do = do_ref[toks]
            weight = ps_ref[0, at]
            dp = nt(split(v, masks), do)
            probs, grads, far = [], [], []
            for half in range(2):
                p_half = p_ref[0, at, half * SPAN : (half + 1) * SPAN, :]
                p = p_half.astype(f32)
                dp_half = dp[half * SPAN : (half + 1) * SPAN]
                w, dw = weight[half : half + 1], dp_far[8 * s + half : 8 * s + half + 1, inside]
                r = jnp.sum(p * dp_half, axis=0, keepdims=True) + w * dw
                probs.append(p_half)
                grads.append((p * (dp_half - r)).astype(bf16))
                far.append(w * (dw - r))
            all_far.append(eight(far))
            all_weights.append(weight)
            d_s[toks, :LANES] = tn(jnp.concatenate(grads, axis=0), split(k, masks))
            d_s[toks, LANES:wide] = nn(jnp.concatenate(grads, axis=1), split(q, masks))
            d_s[toks, wide:] = nn(jnp.concatenate(probs, axis=1), split(do, masks))
        far = diagonal(all_far, lines)
        dq = d_s[here, :LANES] + tn(far, k_lines)
        d_ref[here, :LANES] = (dq.astype(bf16).astype(f32) * (1.0 / math.sqrt(HEAD_DIM))).astype(bf16)
        line = lax.broadcasted_iota(jnp.int32, (8 * lines, LANES), 0)
        lane = lax.broadcasted_iota(jnp.int32, (8 * lines, LANES), 1)
        own = lane // HEAD_DIM == line % 8
        gk = jnp.where(own, nn(far, qkv_ref[here, :LANES]), 0.0)
        gv = jnp.where(own, nn(diagonal(all_weights, lines), do_ref[here]), 0.0)
        out = jnp.zeros((1, wide), f32)
        after = None
        for s in reversed(range(spans)):
            at = row_at * spans + s
            toks = slice(at * SPAN, (at + 1) * SPAN)
            dkv = d_s[toks, LANES:]
            gkv = [jnp.sum(v[8 * s : 8 * s + 8], axis=0, keepdims=True) for v in (gk, gv)]
            inverse, flag = misc_ref[at, 0:1, :], misc_ref[at, 1:2, :]
            gkv = jnp.concatenate(gkv, axis=1) * jnp.concatenate([inverse, inverse], axis=1)
            out = out + jnp.concatenate([flag, flag], axis=1) * gkv
            if after is None:
                after = gkv
            else:
                reached = jnp.broadcast_to(misc_ref[at, 5:6], (SPAN, SPAN)).T == misc_ref[at + 1, 2:3]
                dkv = dkv + jnp.where(jnp.concatenate([reached, reached], axis=1), after, 0.0)
                same = (misc_ref[at, 2:3] == misc_ref[at + 1, 2:3]).astype(f32)
                after = gkv + jnp.concatenate([same, same], axis=1) * after
            d_ref[toks, LANES:] = dkv.astype(bf16)
        g_ref[row_at, :, :LANES] = jnp.zeros((1, LANES), f32)
        g_ref[row_at, :, LANES:] = out


def pair_backward(at, qkv, do, p, ps, bars, misc, h, gwo, devices, region, first, parts, kept):
    tokens, width = do.shape
    rows = tokens // region
    spans = region // SPAN
    lines = bars.shape[2]
    own = h is not None

    def pair(i, s):
        return s[1] ^ (first + i)

    tok3 = pl.BlockSpec((tokens, 3 * LANES), lambda i, s: (0, pair(i, s)))
    back = pl.BlockSpec((rows, 1, 3 * LANES), lambda i, s: (0, 0, pair(i, s)))
    in_specs = [
        tok3,
        pl.BlockSpec((tokens, LANES), lambda i, s: (0, pair(i, s))),
        pl.BlockSpec((1, rows * spans, 2 * SPAN, SPAN), lambda i, s: (pair(i, s), 0, 0, 0)),
        pl.BlockSpec((1, rows * spans, 8, SPAN), lambda i, s: (pair(i, s), 0, 0, 0)),
        pl.BlockSpec((1, rows, lines, 2 * LANES), lambda i, s: (pair(i, s), 0, 0, 0)),
        whole(misc.shape),
    ]
    args = [qkv, do, p, ps, bars, misc]
    out_specs = [tok3, back]
    out_shape = [shape((tokens, 3 * width), bf16), shape((rows, 1, 3 * width), f32)]
    if own:
        in_specs.append(whole(h.shape))
        args.append(h)
        grads = [shape((width, 3 * LANES), f32)]
        if gwo is not None:
            in_specs.append(whole(gwo.shape))
            args.append(gwo)
            grads = [shape((devices // 2, width // devices, width), f32)] * 2
        out_specs += [whole(v.shape) for v in grads]
        out_shape += grads
    n_in = len(args)
    kept = list(kept or ())

    def body(at_s, *refs):
        outs = refs[n_in + len(kept) : n_in + len(kept) + len(out_shape)]
        held = refs[n_in + len(kept) + len(out_shape) :]
        pair_back_body(rows, *refs[:6], outs[0], outs[1], held[0])
        if own:
            grads = tn(refs[6][...], outs[0][...])
            if gwo is None:
                outs[2][...] = grads
            else:
                held[1][...] = grads
                lines_q, lines_o = width // devices, LANES // devices
                for out, c in by_core(at_s[0] % 2, *outs[2:]):
                    for j in range(devices // 2):
                        owner = 2 * j + c
                        out[j, :, : 3 * LANES] = held[1][pl.ds(pl.multiple_of(owner * lines_q, lines_q), lines_q)]
                        go = refs[7][pl.ds(pl.multiple_of(owner * lines_o, lines_o), lines_o)]
                        for i in range(width // LANES):
                            out[j, i * lines_o : (i + 1) * lines_o, 3 * LANES :] = go[:, i * LANES : (i + 1) * LANES]

    return call(
        body,
        (parts,),
        1,
        in_specs + [pl.BlockSpec(memory_space=pl.ANY)] * len(kept),
        out_specs,
        out_shape,
        us=6 * parts,
        mib=12,
        aliases={1 + n_in + i: i for i in range(len(kept))},
        scratch=[pltpu.VMEM((tokens, 3 * LANES), f32), pltpu.VMEM((width, 3 * LANES), f32)],
    )(at, *args, *kept)


def input_body(
    rows, at_s, every_ref, backs, misc_ref, x_ref, gain_ref, dmid_ref, d_ref, w_ref, so_far_ref,
    gi_ref, small_ref, late_ref, through_s, tag_s, back_s,
):
    me = at_s[0]
    devices = every_ref.shape[0]
    width = x_ref.shape[-1]
    tiles = width // LANES
    wide = w_ref.shape[1]

    @pl.when(pl.program_id(0) == 0)
    def _():
        small_ref[...] = so_far_ref[...]
        if len(backs) == 1:
            for d in range(devices):
                back_s[d] = backs[0][d * rows : (d + 1) * rows]
        else:
            for core, ref in enumerate(backs):
                for j in range(devices // 2):
                    back_s[me ^ (2 * j + core)] = ref[j * rows : (j + 1) * rows]
        mine_lanes = pl.ds(pl.multiple_of(at_s[1] * 3 * LANES, LANES), 3 * LANES)
        heads, tails = [], []
        for r in range(rows):
            run = mine = jnp.zeros((1, wide), f32)
            own_run = jnp.zeros((1, 3 * LANES), f32)
            tag = None
            for d in reversed(range(devices)):
                sums, _, tag_here = state_of(every_ref, d, r, tiles)
                if tag is not None:
                    same = (tag == tag_here).astype(f32)[:, :1]
                    run = back_s[d + 1, r : r + 1] + same * run
                    own_run = back_s[d + 1, r : r + 1, mine_lanes] + same * own_run
                    mine = jnp.where(me == d, run, mine)
                tag = tag_here
                tag_s[r : r + 1] = jnp.where(me == d, tag, tag_s[r : r + 1])
                heads.append(sums)
                tails.append(own_run)
            through = nt(hi_lo(jnp.broadcast_to(mine, (8, wide))), w_ref[...])
            through_s[r : r + 1] = through[0:1] + through[8:9]
        late_ref[...] = lax.dot_general(
            jnp.concatenate(heads, axis=0), jnp.concatenate(tails, axis=0), (((0,), (0,)), ((), ())),
            preferred_element_type=f32, precision=lax.Precision.HIGHEST,
        )

    dn = nt(d_ref[...], w_ref[...])
    spans = misc_ref.shape[0]
    added = []
    for i in range(spans):
        at = pl.program_id(0) * spans + i
        row_at = at // (pl.num_programs(0) * spans // rows)
        reached = jnp.broadcast_to(misc_ref[i, 5:6], (SPAN, SPAN)).T == tag_s[pl.ds(row_at, 1)]
        added.append(jnp.where(jnp.concatenate([reached] * tiles, axis=1), through_s[pl.ds(row_at, 1)], 0.0))
    dn = dn + jnp.concatenate(added, axis=0)
    xhat, rstd = norm_parts(x_ref[...].astype(f32))
    small_ref[0:1] += jnp.sum(dn * xhat, axis=0, keepdims=True)
    small_ref[1:2] += jnp.sum(dn, axis=0, keepdims=True)
    gi_ref[...] = dmid_ref[...] + norm_back(dn * gain_ref[...], xhat, rstd)


def input_grads(at, every, back, misc, x, gain, dmid, d, w, small, rows):
    tokens, width = x.shape
    devices = every.shape[0]
    steps = 7 if tokens // SPAN % 7 == 0 else tokens // SPAN
    chunk = tokens // steps
    tok = pl.BlockSpec((chunk, width), lambda i, *_: (i, 0))

    def body(at_s, every_ref, *refs):
        input_body(rows, at_s, every_ref, refs[: len(back)], *refs[len(back) :])

    return call(
        body,
        (steps,),
        1,
        [
            whole(every.shape),
            *[whole(v.shape) for v in back],
            pl.BlockSpec((chunk // SPAN,) + misc.shape[1:], lambda i, *_: (i, 0, 0)),
            tok, whole((1, width)), tok,
            pl.BlockSpec((chunk, 3 * width), lambda i, *_: (i, 0)),
            whole(w.shape),
            whole(small.shape),
        ],
        [tok, whole((8, width)), whole((width, 3 * LANES))],
        [shape((tokens, width), f32), shape((8, width), f32), shape((width, 3 * LANES), f32)],
        scratch=[
            pltpu.VMEM((rows, width), f32), pltpu.VMEM((rows, LANES), f32), pltpu.VMEM((devices, rows, 3 * width), f32)
        ],
        us=10,
        mib=10,
    )(at, every, *back, misc, x, gain[None], dmid, d, w, small)


def fold_body(count, at_s, *refs):
    chip = at_s[0] // 2
    outs = refs[2 * count :]
    at = 0
    for keep, got in zip(refs[:count], refs[count : 2 * count]):
        rows = keep.shape[1]
        for j, out in enumerate(outs):
            out[at : at + rows] = keep[chip ^ j] + got[chip ^ j]
        at += rows


def fold(at, keeps, gots):
    chips, _, width = keeps[0].shape
    outs = [shape((sum(v.shape[1] for v in keeps), width), f32)] * chips

    def body(*refs):
        fold_body(len(keeps), *refs)

    args = [*keeps, *gots]
    return call(body, (1,), 1, [whole(v.shape) for v in args], [whole(v.shape) for v in outs], outs)(at, *args)


def add_body(*refs):
    total = refs[0][...]
    for ref in refs[1:-1]:
        total = total + ref[...]
    refs[-1][...] = total


def add_up(parts, after):
    spec = whole(parts[0].shape)
    return call(add_body, (1,), 0, [spec] * len(parts), spec, shape(parts[0].shape, f32), after=after)(*parts)


def unpack_body(at_s, *refs):
    *pieces, late_ref, gq_ref, gk_ref, gv_ref, go_ref, gu_ref, gd_ref = refs
    rows = gu_ref.shape[0] // len(pieces)
    lines = go_ref.shape[0] // len(pieces)
    for owner, ref in owners(at_s[0], pieces):
        at = pl.ds(pl.multiple_of(owner * rows, rows), rows)
        gu_ref[at] = ref[:rows]
        gd_ref[at] = ref[rows : 2 * rows]
        for i, out in enumerate((gq_ref, gk_ref, gv_ref)):
            lanes = slice(i * LANES, (i + 1) * LANES)
            out[at] = ref[2 * rows :, lanes] + late_ref[at, lanes]
        at = pl.ds(pl.multiple_of(owner * lines, lines), lines)
        for i in range(go_ref.shape[1] // LANES):
            first = 2 * rows + i * lines
            go_ref[at, i * LANES : (i + 1) * LANES] = ref[first : first + lines, 3 * LANES :]


def unpack(at, pieces, late):
    width = pieces[0].shape[1]
    thin = shape((width, LANES), f32)
    outs = [thin, thin, thin, shape((LANES, width), f32), shape((width, width), f32), shape((width, width), f32)]
    args = [*pieces, late]
    return call(
        unpack_body, (1,), 1, [whole(v.shape) for v in args], [whole(v.shape) for v in outs], outs
    )(at, *args)


def totals_body(small_ref, *outs):
    total = small_ref[0]
    for d in range(1, small_ref.shape[0]):
        total = total + small_ref[d]
    for i, out in enumerate(outs):
        out[...] = total[i : i + 1]


def totals(small):
    outs = [shape((1, small.shape[2]), f32)] * 6
    return call(totals_body, (1,), 0, [whole(small.shape)], [whole(v.shape) for v in outs], outs)(small)


def narrow_body(w_ref, o_ref):
    o_ref[...] = w_ref[...].astype(bf16)


def gathered(part):
    every = lax.all_gather(part.astype(f32), "head")
    flat = every.reshape(-1, part.shape[1])
    chunk = flat.shape[0] // 8
    block = pl.BlockSpec((chunk, part.shape[1]), lambda i: (i, 0))
    return call(narrow_body, (8,), 0, [block], block, shape(flat.shape, bf16))(flat).reshape(every.shape)


def swap(v, axis, mask):
    return lax.ppermute(v, axis, [(i, i ^ mask) for i in range(lax.axis_size(axis))])


def along_z(both, one):
    groups, devices = lax.axis_size("head"), lax.axis_size("seq")
    by_core = [(d * groups + h, d * groups + (h ^ (1 + d % 2))) for d in range(devices) for h in range(groups)]
    return lax.ppermute(both, ("seq", "head"), by_core), swap(one, "head", 3)


def both_cores(pieces, after):
    first, *rest = pieces
    theirs = [swap(first, "seq", 1)]
    held = lax.optimization_barrier((after, *rest))
    return pieces + theirs + [swap(v, "seq", 1) for v in held[1:]]


def on_device(
    inputs, doc_ids, pad_mask, ln1_gain, ln1_shift, w_query, w_key, w_value, w_out,
    ln2_gain, ln2_shift, w_up, b_up, w_down, b_down, out_grad,
):
    rows, region, width = inputs.shape
    tokens = rows * region
    devices = lax.axis_size("seq")
    groups = lax.axis_size("head")
    here = lax.axis_index("seq")
    group = lax.axis_index("head")
    share = width // groups
    pairs = width // LANES
    spans = region // SPAN
    own_pair = group * share // LANES
    at = jnp.stack([here, own_pair, group]).astype(jnp.int32)
    x = inputs.reshape(tokens, width)
    g = out_grad.reshape(tokens, width)
    by_share = share == LANES and devices == 8 and groups == 4

    if by_share:
        others = range(2, devices, 2)
        a_both, a_one = along_z(*attention_share(at, w_query, w_key, w_value, devices))
    h1, m, prefix, tiny = first_norm(
        doc_ids, pad_mask, x, ln1_gain, ln1_shift, rows, region, []
    )
    tiny = tiny.reshape(rows * 8, LANES)
    if by_share:
        (a_sent,) = cat([[(v, 0, v.shape[0]) for v in (a_both, a_one, tiny)]])
        a_moved = [swap(a_sent, "seq", j) for j in others]
        up_both, up_one, down_both, down_one = hidden_share(at, w_up, w_out, b_up, w_down, devices, [h1])
        up_both, up_one = along_z(up_both, up_one)
        down_both, down_one = along_z(down_both, down_one)
        (up_sent,) = cat([[(v, 0, v.shape[0] - 8) for v in (up_both, up_one)]])
        a_pieces = both_cores([a_sent] + a_moved, up_sent)
        up_moved = [swap(up_sent, "seq", j) for j in others]
        means, misc, every = document_means(at, doc_ids, pad_mask, prefix, a_pieces, devices, rows, region)
        source = ("came", w_query, w_key, w_value, *a_pieces)
        qkv, p, ps, o, bars, w_in = pair_forward(at, means, misc, h1, source, 0, pairs, region, None)
        deep = down_one.shape[0] // 2
        upper, lower = cat([[(down_both, 2 * i * deep, 2 * deep), (down_one, i * deep, deep)] for i in range(2)], after=[o])
        down_moved = [upper, lower, swap(upper, "seq", 2), swap(lower, "seq", 4)]
        (up_half,) = cat(
            [[(v, 0, v.shape[0]) for v in [up_sent] + up_moved] + [(up_both, up_both.shape[0] - 8, 8)]], after=[upper]
        )
        (down_half,) = cat([[(v, 0, v.shape[0]) for v in down_moved]], after=[up_half])
        up_pieces = [up_half, swap(up_half, "seq", 1)]
        down_pieces = [down_half, swap(down_half, "seq", 1)]
        ffn_source = ("came", w_up, w_out, b_up[None], w_down, up_pieces, down_pieces, up_one)
    else:
        every = lax.all_gather(tiny, "seq")
        means, misc, every = document_means(at, doc_ids, pad_mask, prefix, [every], devices, rows, region)
        w_in = gathered(jnp.concatenate([w_query, w_key, w_value], axis=1))
        w_in = w_in.reshape(groups, width, 3, share).transpose(1, 2, 0, 3).reshape(width, 3, pairs, LANES)
        w_in = w_in.transpose(0, 2, 1, 3).reshape(width, 3 * width)
        qkv, p, ps, o, bars = pair_forward(at, means, misc, h1, ("all", w_in), 0, pairs, region, None)
        bu = lax.all_gather(b_up, "head")
        bu = jnp.broadcast_to(bu[:, None], (groups, 8, bu.shape[1]))
        ffn_source = ("all", gathered(w_up), gathered(w_out).reshape(width, width), bu, gathered(w_down))

    out, dmid, do, gwo, gbu, small, *hidden_grads = feed_forward(
        at, x, g, o, ln2_gain, ln2_shift, b_down, ffn_source, devices
    )
    back_args = (at, qkv, do, p, ps, bars, misc)
    d, g_back, *pair_grads = pair_backward(
        *back_args, h1, gwo if by_share else None, devices, region, 0, 1, None
    )
    if by_share:
        keeps, gives = zip(hidden_grads, pair_grads)
        folded = fold(at, keeps, [swap(v, "seq", 1) for v in gives])
        arrived = [swap(v, "seq", j) for v, j in zip(folded[1:], others)]
    d, g_back = pair_backward(*back_args, None, None, devices, region, 1, pairs - 1, (d, g_back))
    if by_share:
        g_back = g_back.reshape(rows, 3 * width)
        (back,) = cat([[(v, 0, rows) for v in [g_back] + [swap(g_back, "seq", j) for j in others]]])
        total = add_up([folded[0]] + arrived, [back])
        spread = [swap(total, "seq", j) for j in others]
        back = [back, swap(back, "seq", 1)]
    else:
        back = [lax.all_gather(g_back, "seq").reshape(devices * rows, 3 * width)]
    grad_inputs, small, late = input_grads(at, every, back, misc, x, ln1_gain, dmid, d, w_in, small, rows)
    out = out.reshape(rows, region, width)
    grad_inputs = grad_inputs.reshape(rows, region, width)
    if by_share:
        pieces = both_cores([total] + spread, small)
        gq, gk, gv, gwo, gwu, gwd = unpack(at, pieces, late)
        g1, s1, g2, s2, gbd, gbu = (v[0] for v in totals(lax.all_gather(small, "seq")))
        return out, grad_inputs, g1, s1, gq, gk, gv, gwo, g2, s2, gwu, gbu, gwd, gbd

    gwu, gwd = hidden_grads
    (gw,) = pair_grads
    gwu, gwd, gwo, gbu, small, gw = lax.psum((gwu, gwd, gwo, gbu, small, gw), "seq")
    gw = gw + late
    gq, gk, gv = (gw[:, i * LANES : (i + 1) * LANES] for i in range(3))
    if share != LANES:
        inner = group * share - own_pair * LANES
        gq, gk, gv = (lax.dynamic_slice_in_dim(v, inner, share, 1) for v in (gq, gk, gv))
        gwo = lax.dynamic_slice_in_dim(gwo, inner, share, 0)
    return (
        out, grad_inputs, small[0], small[1], gq, gk, gv, gwo, small[2], small[3], gwu, gbu[0], gwd, small[4]
    )


def solution(mesh):
    tok = P(None, "seq", None)
    ids = P(None, "seq")
    cols, lines = P(None, "head"), P("head", None)
    in_specs = (
        tok, ids, ids, P(), P(), cols, cols, cols, lines, P(), P(), cols, P("head"), lines, P(), tok,
    )
    out_specs = (
        tok, tok, P(), P(), cols, cols, cols, lines, P(), P(), cols, P("head"), lines, P(),
    )
    return jax.shard_map(on_device, mesh=mesh, in_specs=in_specs, out_specs=out_specs, check_vma=False)
```

time: 234 us -> 175 us (0.75)
  Pallas kernels: 145 us -> 85.2 us
  waiting for transfers between devices: 21.5 us -> 39.8 us
  blocking collectives: 19.4 us -> 9.21 us
  local copies, waits for them, and re-layouts: 12.7 us -> 3.22 us
  starting transfers between devices: 32.3 us -> 35.9 us
    pallas_call x22 -> x19, Pallas kernels: 145 us -> 85.2 us  [call(): return lambda *operands: kernel(*operands, *after)]
    ppermute x28 -> x33, waiting for transfers between devices: 21.5 us -> 39.8 us  [swap(): lax.ppermute(v, axis, [(i, i ^ mask) for i in range(lax.axis_size(axis))])]
    all_gather x1 -> x0, blocking collectives: 10.2 us -> none  [on_device(): back = lax.all_gather(g_back, 'seq')]
    unnamed x62 -> x41, local copies, waits for them, and re-layouts: 12.7 us -> 3.22 us
    ppermute x0 -> x3, starting transfers between devices: none -> 6.15 us  [along_z(): return (lax.ppermute(both, ('seq', 'head'), by_core), swap(one, 'head', 3))]
    ppermute x28 -> x33, starting transfers between devices: 32.3 us -> 29.7 us  [swap(): lax.ppermute(v, axis, [(i, i ^ mask) for i in range(lax.axis_size(axis))])]
  transfers between devices with their start and end apart: 28 -> 36, of which waited for: 7 -> 11; matrix products, arithmetic and copies ran while one was open for 0% -> 0% of each run, Pallas kernels for 32% -> 28%
where the time goes in v3:
time: 175 us; the launch traced here: 174 us
  Pallas kernels  85.2 us (49%)
  waiting for transfers between devices  39.8 us (23%)
  starting transfers between devices  35.9 us (21%)
  blocking collectives  9.21 us (5%)
  local copies, waits for them, and re-layouts  3.22 us (2%)
    pallas_call x19, Pallas kernels, call(): return lambda *operands: kernel(*operands, *after)  85.2 us
    ppermute x33, waiting for transfers between devices, swap(): lax.ppermute(v, axis, [(i, i ^ mask) for i in range(lax.axis_size(axis))])  39.8 us
    ppermute x33, starting transfers between devices, swap(): lax.ppermute(v, axis, [(i, i ^ mask) for i in range(lax.axis_size(axis))])  29.7 us
    all_gather x1, blocking collectives, on_device(): lax.all_gather(small, 'seq')  9.21 us
    ppermute x3, starting transfers between devices, along_z(): return (lax.ppermute(both, ('seq', 'head'), by_core), swap(one, 'head', 3))  6.15 us
  transfers between devices with their start and end apart: 36, of which 11 were waited for; matrix products, arithmetic and copies ran while one was open for 0% of the time, Pallas kernels for 28%

profile of v3, /device:TPU:0, one launch (start us, length us, event | category | flops | bytes accessed | tf_op | source)
XLA Modules:
  0.0 174.4 jit_solution(2767179065929914875)
XLA Ops:
  0.8 1.4 shard_map.264
  2.2 3.1 %collective-permute-start = (f32[384,128]{1,0:T(8,128)S(1)}, f32[384,128]{1,0:T(8,128)S(1)}, u32[]{:S(2)}, u32[]{:S(2)}) collective-permute-start(f32[384,128]{1,0:T(8,128)S(1)} %get-tuple-element.73), channel_id=1, source_target_pairs={{0,1},{1,0},{2,3},{3,2},{4,6},{5,7},{6,4},{7,5},{8,9},{9,8},{10,11... | collective-permute-start | bytes 589832 | tf_op jit(solution)/shard_map/ppermute | solution.py:993
  5.3 2.5 %collective-permute-start.1 = (f32[192,128]{1,0:T(8,128)S(1)}, f32[192,128]{1,0:T(8,128)S(1)}, u32[]{:S(2)}, u32[]{:S(2)}) collective-permute-start(f32[192,128]{1,0:T(8,128)S(1)} %get-tuple-element.74), channel_id=1, source_target_pairs={{0,3},{1,2},{2,1},{3,0},{4,7},{5,6},{6,5},{7,4},{8,11},{9,10},{10,... | collective-permute-start | bytes 294920 | tf_op jit(solution)/shard_map/ppermute | solution.py:987
  7.8 2.8 %shard_map.263 = (bf16[1792,512]{1,0:T(8,128)(2,1)S(1)}, f32[2,8,896]{2,1,0:T(8,128)}, f32[2,8,768]{2,1,0:T(8,128)S(1)}, f32[2,8,128]{2,1,0:T(8,128)S(1)}) custom-call(s32[2,896]{1,0:T(2,128)S(1)} %copy-done.8, s32[2,896]{1,0:T(2,128)S(1)} %copy-done.8, s32[2,896]{1,0:T(2,128)S(1)} %copy-done.9, bf16[1792,512]{1,0:T(8,128)(2,1)S(1)} %bitcast.30, ...), custom_call_target="tpu_custom_call" | custom-call | flops 4400000000 | bytes 14000000 | tf_op jit(solution)/shard_map/pallas_call | solution.py:91
  10.6 1.7 shard_map.266
  12.3 0.7 collective-permute-start.6
  13.0 0.9 collective-permute-start.7
  13.9 0.5 collective-permute-done.1.refs_1_
  14.5 1.6 collective-permute-start.2
  16.0 1.5 collective-permute-start.3
  18.0 8.2 %collective-permute-done.7.refs_1_.refs_16_ = f32[88,512]{1,0:T(8,128)S(1)} collective-permute-done((f32[88,512]{1,0:T(8,128)S(1)}, f32[88,512]{1,0:T(8,128)S(1)}, u32[]{:S(2)}, u32[]{:S(2)}) %collective-permute-start.7) | collective-permute-done | bytes 180256 | tf_op jit(solution)/shard_map/ppermute | solution.py:987
  26.2 4.5 %collective-permute-done.3.refs_7_.refs_9_ = f32[592,128]{1,0:T(8,128)S(1)} collective-permute-done((f32[592,128]{1,0:T(8,128)S(1)}, f32[592,128]{1,0:T(8,128)S(1)}, u32[]{:S(2)}, u32[]{:S(2)}) %collective-permute-start.3) | collective-permute-done | bytes 303136 | tf_op jit(solution)/shard_map/ppermute | solution.py:987
  31.2 2.3 %collective-permute-start.14 = (f32[256,512]{1,0:T(8,128)S(1)}, f32[256,512]{1,0:T(8,128)S(1)}, u32[]{:S(2)}, u32[]{:S(2)}) collective-permute-start(f32[256,512]{1,0:T(8,128)S(1)} %get-tuple-element.85), channel_id=1, source_target_pairs={{0,1},{1,0},{2,3},{3,2},{4,6},{5,7},{6,4},{7,5},{8,9},{9,8},{10,11... | collective-permute-start | bytes 1572872 | tf_op jit(solution)/shard_map/ppermute | solution.py:993
  33.5 4.1 %collective-permute-start.15 = (f32[128,512]{1,0:T(8,128)S(1)}, f32[128,512]{1,0:T(8,128)S(1)}, u32[]{:S(2)}, u32[]{:S(2)}) collective-permute-start(f32[128,512]{1,0:T(8,128)S(1)} %get-tuple-element.86), channel_id=1, source_target_pairs={{0,3},{1,2},{2,1},{3,0},{4,7},{5,6},{6,5},{7,4},{8,11},{9,10},{10,... | collective-permute-start | bytes 786440 | tf_op jit(solution)/shard_map/ppermute | solution.py:987
  37.7 1.0 collective-permute-start.11
  38.6 1.1 collective-permute-start.12
  39.7 1.4 collective-permute-start.13
  41.2 0.8 shard_map.268
  42.2 13.9 %shard_map.269 = (bf16[1792,1536]{1,0:T(8,128)(2,1)S(1)}, bf16[4,14,256,128]{3,2,1,0:T(8,128)(2,1)S(1)}, f32[4,14,8,128]{3,2,1,0:T(8,128)S(1)}, bf16[1792,512]{1...) custom-call(s32[3]{0:T(128)S(1)} %pad_add_fusion.refs_0_, ...), custom_call_target="tpu_custom_call" | custom-call | flops 22000001024 | bytes 70000000 | tf_op jit(solution)/shard_map/pallas_call | solution.py:91
  56.3 1.1 copy-done.18
  57.3 0.9 collective-permute-start.17
  58.3 1.1 collective-permute-start.18
  59.4 1.9 %collective-permute-done.13.refs_3_ = f32[240,512]{1,0:T(8,128)S(1)} collective-permute-done((f32[240,512]{1,0:T(8,128)S(1)}, f32[240,512]{1,0:T(8,128)S(1)}, u32[]{:S(2)}, u32[]{:S(2)}) %collective-permute-start.13) | collective-permute-done | bytes 491552 | tf_op jit(solution)/shard_map/ppermute | solution.py:987
  61.6 6.6 %collective-permute-done.17.refs_2_ = f32[192,512]{1,0:T(8,128)S(1)} collective-permute-done((f32[192,512]{1,0:T(8,128)S(1)}, f32[192,512]{1,0:T(8,128)S(1)}, u32[]{:S(2)}, u32[]{:S(2)}) %collective-permute-start.17) | collective-permute-done | bytes 393248 | tf_op jit(solution)/shard_map/ppermute | solution.py:987
  68.1 0.9 collective-permute-done.18.refs_3_
  69.2 3.4 %collective-permute-done.19.refs_15_ = f32[768,512]{1,0:T(8,128)S(1)} collective-permute-done((f32[768,512]{1,0:T(8,128)S(1)}, f32[768,512]{1,0:T(8,128)S(1)}, u32[]{:S(2)}, u32[]{:S(2)}) %collective-permute-start.19) | collective-permute-done | bytes 1572896 | tf_op jit(solution)/shard_map/ppermute | solution.py:987
  72.7 32.0 %shard_map.273 = (bf16[1792,512]{1,0:T(8,128)(2,1)}, f32[1792,512]{1,0:T(8,128)S(1)}, bf16[1792,512]{1,0:T(8,128)(2,1)S(1)}, f32[128,512]{1,0:T(8,128)S(1)}, f32...) custom-call(s32[3]{0:T(128)S(1)} %pad_add_fusion.refs_0_, ...), custom_call_target="tpu_custom_call" | custom-call | flops 41799999488 | bytes 133000000 | tf_op jit(solution)/shard_map/pallas_call | solution.py:91
  104.7 1.8 %copy-done.16 = f32[1792,512]{1,0:T(8,128)} copy-done((f32[1792,512]{1,0:T(8,128)}, f32[1792,512]{1,0:T(8,128)S(1)}, u32[]{:S(2)}) %copy-start.16) | copy-done | bytes 3670040
  106.6 5.8 %shard_map.274 = (bf16[1792,1536]{1,0:T(8,128)(2,1)S(1)}, f32[2,1,1536]{2,1,0:T(1,128)S(1)}, f32[4,64,512]{2,1,0:T(8,128)S(1)}, f32[4,64,512]{2,1,0:T(8,128)S(1)}) custom-call(s32[3]{0:T(128)S(1)} %pad_add_fusion.refs_0_, bf16[1792,1536]{1,0:T(8,128)(2,1)S(1)} %get-tuple-element.91.refs_1_, bf16[1792,512]{1,0:T(8,128)(2,1)S(1)} %get-tuple-element.92.refs_2_, ...), custom_call_target="tpu_custom_call" | custom-call | flops 6600000000 | bytes 21000000 | tf_op jit(solution)/shard_map/pallas_call | solution.py:91
  112.9 1.5 collective-permute-done.25.refs_4_
  114.4 0.7 shard_map.279
  115.1 0.9 collective-permute-start.26
  116.0 1.5 collective-permute-start.27
  117.5 1.2 collective-permute-start.28
  118.7 13.7 %shard_map.275 = (bf16[1792,1536]{1,0:T(8,128)(2,1)S(1)}, f32[2,1,1536]{2,1,0:T(1,128)S(1)}) custom-call(s32[3]{0:T(128)S(1)} %pad_add_fusion.refs_0_, bf16[1792,1536]{1,0:T(8,128)(2,1)S(1)} %get-tuple-element.91.refs_1_, bf16[1792,512]{1,0:T(8,128)(2,1)S(1)} %get-tuple-element.92.refs_2_, ...), custom_call_target="tpu_custom_call", output_to_operand_aliasing={{0}: (7, {}), {1}: (8, {})} | custom-call | flops 19800000512 | bytes 63000000 | tf_op jit(solution)/shard_map/pallas_call | solution.py:91
  132.4 0.9 collective-permute-start.20
  133.3 1.5 collective-permute-start.21
  134.8 1.4 collective-permute-done.20.refs_1_
  136.2 1.8 %collective-permute-start.22 = (f32[2,1536]{1,0:T(2,128)S(1)}, f32[2,1536]{1,0:T(2,128)S(1)}, u32[]{:S(2)}, u32[]{:S(2)}) collective-permute-start(f32[2,1536]{1,0:T(2,128)S(1)} %bitcast.27), channel_id=1, source_target_pairs={{0,24},{4,28},{8,16},{12,20},{16,8},{20,12},{24,0},{28,4},{1,25},{... | collective-permute-start | bytes 36872 | tf_op jit(solution)/shard_map/ppermute | solution.py:987
  137.9 2.8 %collective-permute-done.22.refs_3_ = f32[2,1536]{1,0:T(2,128)S(1)} collective-permute-done((f32[2,1536]{1,0:T(2,128)S(1)}, f32[2,1536]{1,0:T(2,128)S(1)}, u32[]{:S(2)}, u32[]{:S(2)}) %collective-permute-start.22) | collective-permute-done | bytes 12320 | tf_op jit(solution)/shard_map/ppermute | solution.py:987
  141.0 0.9 collective-permute-start.29
  141.9 1.5 collective-permute-start.30
  143.4 1.2 collective-permute-start.31
  144.6 8.9 %shard_map.277 = (f32[1792,512]{1,0:T(8,128)}, f32[8,512]{1,0:T(8,128)S(1)}, f32[512,384]{1,0:T(8,128)S(1)}) custom-call(s32[3]{0:T(128)S(1)} %pad_add_fusion.refs_0_, f32[8,16,128]{2,1,0:T(8,128)S(1)} %get-tuple-element.90.refs_1_, f32[8,1536]{1,0:T(8,128)S(1)} %shard_map.276.refs_2_.refs_4_, f32[8,1536]{1,0:T(8,128)S(1)} %collective-permute-done.23.refs_3_, ...), custom_call_target="tpu_custom_call" | custom-call | flops 11000000512 | bytes 35000000 | tf_op jit(solution)/shard_map/pallas_call | solution.py:91
  153.4 8.1 %collective-permute-done.30.refs_3_ = f32[192,512]{1,0:T(8,128)S(1)} collective-permute-done((f32[192,512]{1,0:T(8,128)S(1)}, f32[192,512]{1,0:T(8,128)S(1)}, u32[]{:S(2)}, u32[]{:S(2)}) %collective-permute-start.30) | collective-permute-done | bytes 393248 | tf_op jit(solution)/shard_map/ppermute | solution.py:987
  162.0 9.2 %all-gather = f32[64,512]{1,0:T(8,128)S(1)} all-gather(f32[8,512]{1,0:T(8,128)S(1)} %get-tuple-element.105), channel_id=2, replica_groups=mesh['seq'=8,'head'=4] {'seq'}, dimensions={0}, use_global_device_ids=true | all-gather | bytes 147456 | tf_op jit(solution)/shard_map/all_gather | solution.py:1088
  171.2 0.6 shard_map.278
  171.9 2.5 %shard_map.281 = (f32[512,128]{1,0:T(8,128)}, f32[512,128]{1,0:T(8,128)}, f32[512,128]{1,0:T(8,128)}, f32[128,512]{1,0:T(8,128)}, f32[512,512]{1,0:T(8,128)}, /*index=5*/f32[512,512]{1,0:T(8,128)}) custom-call(s32[3]{0:T(128)S(1)} %pad_add_fusion.refs_0_, f32[192,512]{1,0:T(8,128)S(1)} %shard_map.280.refs_1_, ...), custom_call_target="tpu_custom_call" | custom-call | flops 2200000000 | bytes 7000000 | tf_op jit(solution)/shard_map/pallas_call | solution.py:91
  (86 shorter events, 3.2 us)
Async XLA Ops:
  0.7 7.0 %copy-start.1 = (bf16[2,896,512]{2,1,0:T(8,128)(2,1)S(1)}, bf16[2,896,512]{2,1,0:T(8,128)(2,1)}, u32[]{:S(2)}) copy-start(bf16[2,896,512]{2,1,0:T(8,128)(2,1)} %param.16) | copy-start | bytes 5505028
  0.7 7.0 %copy-start.8 = (s32[2,896]{1,0:T(2,128)S(1)}, s32[2,896]{1,0:T(2,128)}, u32[]{:S(2)}) copy-start(s32[2,896]{1,0:T(2,128)} %refs_2_.7) | copy-start | bytes 21508
  0.7 7.0 %copy-start.9 = (s32[2,896]{1,0:T(2,128)S(1)}, s32[2,896]{1,0:T(2,128)}, u32[]{:S(2)}) copy-start(s32[2,896]{1,0:T(2,128)} %refs_3_.3) | copy-start | bytes 21508
  0.7 7.0 %copy-start.10 = (f32[512]{0:T(512)S(1)}, f32[512]{0:T(512)}, u32[]{:S(2)}) copy-start(f32[512]{0:T(512)} %param.20) | copy-start | bytes 6148
  2.2 12.3 %collective-permute-start = (f32[384,128]{1,0:T(8,128)S(1)}, f32[384,128]{1,0:T(8,128)S(1)}, u32[]{:S(2)}, u32[]{:S(2)}) collective-permute-start(f32[384,128]{1,0:T(8,128)S(1)} %get-tuple-element.73), channel_id=1, source_target_pairs={{0,1},{1,0},{2,3},{3,2},{4,6},{5,7},{6,4},{7,5},{8,9},{9,8},{10,11... | collective-permute-start | bytes 589832 | tf_op jit(solution)/shard_map/ppermute | solution.py:993
  5.3 9.2 %collective-permute-start.1 = (f32[192,128]{1,0:T(8,128)S(1)}, f32[192,128]{1,0:T(8,128)S(1)}, u32[]{:S(2)}, u32[]{:S(2)}) collective-permute-start(f32[192,128]{1,0:T(8,128)S(1)} %get-tuple-element.74), channel_id=1, source_target_pairs={{0,3},{1,2},{2,1},{3,0},{4,7},{5,6},{6,5},{7,4},{8,11},{9,10},{10,... | collective-permute-start | bytes 294920 | tf_op jit(solution)/shard_map/ppermute | solution.py:987
  12.3 13.9 %collective-permute-start.6 = (f32[168,512]{1,0:T(8,128)S(1)}, f32[168,512]{1,0:T(8,128)S(1)}, u32[]{:S(2)}, u32[]{:S(2)}) collective-permute-start(f32[168,512]{1,0:T(8,128)S(1)} %get-tuple-element.77), channel_id=1, source_target_pairs={{0,1},{1,0},{2,3},{3,2},{4,6},{5,7},{6,4},{7,5},{8,9},{9,8},{10,11... | collective-permute-start | bytes 1032200 | tf_op jit(solution)/shard_map/ppermute | solution.py:993
  13.0 13.2 %collective-permute-start.7 = (f32[88,512]{1,0:T(8,128)S(1)}, f32[88,512]{1,0:T(8,128)S(1)}, u32[]{:S(2)}, u32[]{:S(2)}) collective-permute-start(f32[88,512]{1,0:T(8,128)S(1)} %get-tuple-element.78), channel_id=1, source_target_pairs={{0,3},{1,2},{2,1},{3,0},{4,7},{5,6},{6,5},{7,4},{8,11},{9,10},{10,... | collective-permute-start | bytes 540680 | tf_op jit(solution)/shard_map/ppermute | solution.py:987
  14.5 11.8 %collective-permute-start.2 = (f32[592,128]{1,0:T(8,128)S(1)}, f32[592,128]{1,0:T(8,128)S(1)}, u32[]{:S(2)}, u32[]{:S(2)}) collective-permute-start(f32[592,128]{1,0:T(8,128)S(1)} %shard_map.265.refs_5_.refs_7_), channel_id=1, source_target_pairs={{0,8},{4,12},{8,0},{12,4},{16,24},{20,28},{24,16},{28,20},{1,9},{5... | collective-permute-start | bytes 909320 | tf_op jit(solution)/shard_map/ppermute | solution.py:987
  16.0 14.7 %collective-permute-start.3 = (f32[592,128]{1,0:T(8,128)S(1)}, f32[592,128]{1,0:T(8,128)S(1)}, u32[]{:S(2)}, u32[]{:S(2)}) collective-permute-start(f32[592,128]{1,0:T(8,128)S(1)} %shard_map.265.refs_5_.refs_7_), channel_id=1, source_target_pairs={{0,16},{4,20},{8,24},{12,28},{16,0},{20,4},{24,8},{28,12},{1,17},{... | collective-permute-start | bytes 909320 | tf_op jit(solution)/shard_map/ppermute | solution.py:987
  17.5 13.2 %collective-permute-start.4 = (f32[592,128]{1,0:T(8,128)S(1)}, f32[592,128]{1,0:T(8,128)S(1)}, u32[]{:S(2)}, u32[]{:S(2)}) collective-permute-start(f32[592,128]{1,0:T(8,128)S(1)} %shard_map.265.refs_5_.refs_7_), channel_id=1, source_target_pairs={{0,24},{4,28},{8,16},{12,20},{16,8},{20,12},{24,0},{28,4},{1,25},{... | collective-permute-start | bytes 909320 | tf_op jit(solution)/shard_map/ppermute | solution.py:987
  26.2 7.4 %collective-permute-start.5 = (f32[592,128]{1,0:T(8,128)S(1)}, f32[592,128]{1,0:T(8,128)S(1)}, u32[]{:S(2)}, u32[]{:S(2)}) collective-permute-start(f32[592,128]{1,0:T(8,128)S(1)} %shard_map.265.refs_5_.refs_7_), channel_id=1, source_target_pairs={{0,4},{4,0},{8,12},{12,8},{16,20},{20,16},{24,28},{28,24},{1,5},{5... | collective-permute-start | bytes 909320 | tf_op jit(solution)/shard_map/ppermute | solution.py:987
  30.7 7.0 %collective-permute-start.10 = (f32[592,128]{1,0:T(8,128)S(1)}, f32[592,128]{1,0:T(8,128)S(1)}, u32[]{:S(2)}, u32[]{:S(2)}) collective-permute-start(f32[592,128]{1,0:T(8,128)S(1)} %collective-permute-done.4.refs_8_.refs_10_), channel_id=1, source_target_pairs={{0,4},{4,0},{8,12},{12,8},{16,20},{20,16},{24,28},{28,24},{1,5},{5... | collective-permute-start | bytes 909320 | tf_op jit(solution)/shard_map/ppermute | solution.py:987
  30.7 7.9 %collective-permute-start.8 = (f32[592,128]{1,0:T(8,128)S(1)}, f32[592,128]{1,0:T(8,128)S(1)}, u32[]{:S(2)}, u32[]{:S(2)}) collective-permute-start(f32[592,128]{1,0:T(8,128)S(1)} %collective-permute-done.2.refs_6_.refs_8_), channel_id=1, source_target_pairs={{0,4},{4,0},{8,12},{12,8},{16,20},{20,16},{24,28},{28,24},{1,5},{5... | collective-permute-start | bytes 909320 | tf_op jit(solution)/shard_map/ppermute | solution.py:987
  31.2 8.5 %collective-permute-start.9 = (f32[592,128]{1,0:T(8,128)S(1)}, f32[592,128]{1,0:T(8,128)S(1)}, u32[]{:S(2)}, u32[]{:S(2)}) collective-permute-start(f32[592,128]{1,0:T(8,128)S(1)} %collective-permute-done.3.refs_7_.refs_9_), channel_id=1, source_target_pairs={{0,4},{4,0},{8,12},{12,8},{16,20},{20,16},{24,28},{28,24},{1,5},{5... | collective-permute-start | bytes 909320 | tf_op jit(solution)/shard_map/ppermute | solution.py:987
  31.2 25.0 %collective-permute-start.14 = (f32[256,512]{1,0:T(8,128)S(1)}, f32[256,512]{1,0:T(8,128)S(1)}, u32[]{:S(2)}, u32[]{:S(2)}) collective-permute-start(f32[256,512]{1,0:T(8,128)S(1)} %get-tuple-element.85), channel_id=1, source_target_pairs={{0,1},{1,0},{2,3},{3,2},{4,6},{5,7},{6,4},{7,5},{8,9},{9,8},{10,11... | collective-permute-start | bytes 1572872 | tf_op jit(solution)/shard_map/ppermute | solution.py:993
  33.5 22.6 %collective-permute-start.15 = (f32[128,512]{1,0:T(8,128)S(1)}, f32[128,512]{1,0:T(8,128)S(1)}, u32[]{:S(2)}, u32[]{:S(2)}) collective-permute-start(f32[128,512]{1,0:T(8,128)S(1)} %get-tuple-element.86), channel_id=1, source_target_pairs={{0,3},{1,2},{2,1},{3,0},{4,7},{5,6},{6,5},{7,4},{8,11},{9,10},{10,... | collective-permute-start | bytes 786440 | tf_op jit(solution)/shard_map/ppermute | solution.py:987
  37.7 21.7 %collective-permute-start.11 = (f32[240,512]{1,0:T(8,128)S(1)}, f32[240,512]{1,0:T(8,128)S(1)}, u32[]{:S(2)}, u32[]{:S(2)}) collective-permute-start(f32[240,512]{1,0:T(8,128)S(1)} %shard_map.267.refs_0_), channel_id=1, source_target_pairs={{0,8},{4,12},{8,0},{12,4},{16,24},{20,28},{24,16},{28,20},{1,9},{5... | collective-permute-start | bytes 1474568 | tf_op jit(solution)/shard_map/ppermute | solution.py:987
  38.6 20.8 %collective-permute-start.12 = (f32[240,512]{1,0:T(8,128)S(1)}, f32[240,512]{1,0:T(8,128)S(1)}, u32[]{:S(2)}, u32[]{:S(2)}) collective-permute-start(f32[240,512]{1,0:T(8,128)S(1)} %shard_map.267.refs_0_), channel_id=1, source_target_pairs={{0,16},{4,20},{8,24},{12,28},{16,0},{20,4},{24,8},{28,12},{1,17},{... | collective-permute-start | bytes 1474568 | tf_op jit(solution)/shard_map/ppermute | solution.py:987
  39.7 21.5 %collective-permute-start.13 = (f32[240,512]{1,0:T(8,128)S(1)}, f32[240,512]{1,0:T(8,128)S(1)}, u32[]{:S(2)}, u32[]{:S(2)}) collective-permute-start(f32[240,512]{1,0:T(8,128)S(1)} %shard_map.267.refs_0_), channel_id=1, source_target_pairs={{0,24},{4,28},{8,16},{12,20},{16,8},{20,12},{24,0},{28,4},{1,25},{... | collective-permute-start | bytes 1474568 | tf_op jit(solution)/shard_map/ppermute | solution.py:987
  57.3 10.8 %collective-permute-start.17 = (f32[192,512]{1,0:T(8,128)S(1)}, f32[192,512]{1,0:T(8,128)S(1)}, u32[]{:S(2)}, u32[]{:S(2)}) collective-permute-start(f32[192,512]{1,0:T(8,128)S(1)} %get-tuple-element.87.refs_5_.refs_0_), channel_id=1, source_target_pairs={{0,8},{4,12},{8,0},{12,4},{16,24},{20,28},{24,16},{28,20},{1,9},{5... | collective-permute-start | bytes 1179656 | tf_op jit(solution)/shard_map/ppermute | solution.py:987
  58.3 10.8 %collective-permute-start.18 = (f32[192,512]{1,0:T(8,128)S(1)}, f32[192,512]{1,0:T(8,128)S(1)}, u32[]{:S(2)}, u32[]{:S(2)}) collective-permute-start(f32[192,512]{1,0:T(8,128)S(1)} %get-tuple-element.88.refs_1_), channel_id=1, source_target_pairs={{0,16},{4,20},{8,24},{12,28},{16,0},{20,4},{24,8},{28,12},{1,17},{... | collective-permute-start | bytes 1179656 | tf_op jit(solution)/shard_map/ppermute | solution.py:987
  61.4 11.3 %copy-start = (bf16[2,896,512]{2,1,0:T(8,128)(2,1)S(1)}, bf16[2,896,512]{2,1,0:T(8,128)(2,1)}, u32[]{:S(2)}) copy-start(bf16[2,896,512]{2,1,0:T(8,128)(2,1)} %param.31) | copy-start | bytes 5505028
  61.4 11.2 %copy-start.2 = (bf16[512,512]{1,0:T(8,128)(2,1)S(1)}, bf16[512,512]{1,0:T(8,128)(2,1)}, u32[]{:S(2)}) copy-start(bf16[512,512]{1,0:T(8,128)(2,1)} %refs_8_.1) | copy-start | bytes 1572868
  61.4 11.2 %copy-start.3 = (bf16[512,512]{1,0:T(8,128)(2,1)S(1)}, bf16[512,512]{1,0:T(8,128)(2,1)}, u32[]{:S(2)}) copy-start(bf16[512,512]{1,0:T(8,128)(2,1)} %refs_11_.1) | copy-start | bytes 1572868
  61.4 11.2 %copy-start.7 = (bf16[128,512]{1,0:T(8,128)(2,1)S(1)}, bf16[128,512]{1,0:T(8,128)(2,1)}, u32[]{:S(2)}) copy-start(bf16[128,512]{1,0:T(8,128)(2,1)} %refs_9_.1) | copy-start | bytes 393220
  61.4 11.2 %copy-start.11 = (f32[512]{0:T(512)S(1)}, f32[512]{0:T(512)}, u32[]{:S(2)}) copy-start(f32[512]{0:T(512)} %param.25) | copy-start | bytes 6148
  61.5 11.2 %copy-start.12 = (f32[512]{0:T(512)S(1)}, f32[512]{0:T(512)}, u32[]{:S(2)}) copy-start(f32[512]{0:T(512)} %param.26) | copy-start | bytes 6148
  61.5 11.2 %copy-start.13 = (f32[512]{0:T(512)S(1)}, f32[512]{0:T(512)}, u32[]{:S(2)}) copy-start(f32[512]{0:T(512)} %param.30) | copy-start | bytes 6148
  61.5 11.2 %copy-start.14 = (f32[512]{0:T(512)S(1)}, f32[512]{0:T(512)}, u32[]{:S(2)}) copy-start(f32[512]{0:T(512)} %param.28) | copy-start | bytes 6148
  61.5 11.2 %collective-permute-start.16 = (f32[968,512]{1,0:T(8,128)S(1)}, f32[968,512]{1,0:T(8,128)S(1)}, u32[]{:S(2)}, u32[]{:S(2)}) collective-permute-start(f32[968,512]{1,0:T(8,128)S(1)} %shard_map.271.refs_4_.refs_12_), channel_id=1, source_target_pairs={{0,4},{4,0},{8,12},{12,8},{16,20},{20,16},{24,28},{28,24},{1,5},{5... | collective-permute-start | bytes 5947400 | tf_op jit(solution)/shard_map/ppermute | solution.py:987
  69.2 3.5 %collective-permute-start.19 = (f32[768,512]{1,0:T(8,128)S(1)}, f32[768,512]{1,0:T(8,128)S(1)}, u32[]{:S(2)}, u32[]{:S(2)}) collective-permute-start(f32[768,512]{1,0:T(8,128)S(1)} %shard_map.272.refs_14_), channel_id=1, source_target_pairs={{0,4},{4,0},{8,12},{12,8},{16,20},{20,16},{24,28},{28,24},{1,5},{5... | collective-permute-start | bytes 4718600 | tf_op jit(solution)/shard_map/ppermute | solution.py:987
  106.5 7.9 %collective-permute-start.24 = (f32[4,128,512]{2,1,0:T(8,128)S(1)}, f32[4,128,512]{2,1,0:T(8,128)S(1)}, u32[]{:S(2)}, u32[]{:S(2)}) collective-permute-start(f32[4,128,512]{2,1,0:T(8,128)S(1)} %get-tuple-element.110), channel_id=1, source_target_pairs={{0,4},{4,0},{8,12},{12,8},{16,20},{20,16},{24,28},{28,24},{1,5},{5... | collective-permute-start | bytes 3145736 | tf_op jit(solution)/shard_map/ppermute | solution.py:987
  112.4 2.0 %collective-permute-start.25 = (f32[4,64,512]{2,1,0:T(8,128)S(1)}, f32[4,64,512]{2,1,0:T(8,128)S(1)}, u32[]{:S(2)}, u32[]{:S(2)}) collective-permute-start(f32[4,64,512]{2,1,0:T(8,128)S(1)} %get-tuple-element.111), channel_id=1, source_target_pairs={{0,4},{4,0},{8,12},{12,8},{16,20},{20,16},{24,28},{28,24},{1,5},{5... | collective-permute-start | bytes 1572872 | tf_op jit(solution)/shard_map/ppermute | solution.py:987
  115.1 25.7 %collective-permute-start.26 = (f32[192,512]{1,0:T(8,128)S(1)}, f32[192,512]{1,0:T(8,128)S(1)}, u32[]{:S(2)}, u32[]{:S(2)}) collective-permute-start(f32[192,512]{1,0:T(8,128)S(1)} %get-tuple-element.113), channel_id=1, source_target_pairs={{0,8},{4,12},{8,0},{12,4},{16,24},{20,28},{24,16},{28,20},{1,9},{5... | collective-permute-start | bytes 1179656 | tf_op jit(solution)/shard_map/ppermute | solution.py:987
  116.0 24.8 %collective-permute-start.27 = (f32[192,512]{1,0:T(8,128)S(1)}, f32[192,512]{1,0:T(8,128)S(1)}, u32[]{:S(2)}, u32[]{:S(2)}) collective-permute-start(f32[192,512]{1,0:T(8,128)S(1)} %get-tuple-element.114), channel_id=1, source_target_pairs={{0,16},{4,20},{8,24},{12,28},{16,0},{20,4},{24,8},{28,12},{1,17},{... | collective-permute-start | bytes 1179656 | tf_op jit(solution)/shard_map/ppermute | solution.py:987
  117.5 23.3 %collective-permute-start.28 = (f32[192,512]{1,0:T(8,128)S(1)}, f32[192,512]{1,0:T(8,128)S(1)}, u32[]{:S(2)}, u32[]{:S(2)}) collective-permute-start(f32[192,512]{1,0:T(8,128)S(1)} %get-tuple-element.115), channel_id=1, source_target_pairs={{0,24},{4,28},{8,16},{12,20},{16,8},{20,12},{24,0},{28,4},{1,25},{... | collective-permute-start | bytes 1179656 | tf_op jit(solution)/shard_map/ppermute | solution.py:987
  132.4 3.8 %collective-permute-start.20 = (f32[2,1536]{1,0:T(2,128)S(1)}, f32[2,1536]{1,0:T(2,128)S(1)}, u32[]{:S(2)}, u32[]{:S(2)}) collective-permute-start(f32[2,1536]{1,0:T(2,128)S(1)} %bitcast.25), channel_id=1, source_target_pairs={{0,8},{4,12},{8,0},{12,4},{16,24},{20,28},{24,16},{28,20},{1,9},{5... | collective-permute-start | bytes 36872 | tf_op jit(solution)/shard_map/ppermute | solution.py:987
  133.3 4.7 %collective-permute-start.21 = (f32[2,1536]{1,0:T(2,128)S(1)}, f32[2,1536]{1,0:T(2,128)S(1)}, u32[]{:S(2)}, u32[]{:S(2)}) collective-permute-start(f32[2,1536]{1,0:T(2,128)S(1)} %bitcast.26), channel_id=1, source_target_pairs={{0,16},{4,20},{8,24},{12,28},{16,0},{20,4},{24,8},{28,12},{1,17},{... | collective-permute-start | bytes 36872 | tf_op jit(solution)/shard_map/ppermute | solution.py:987
  136.2 4.6 %collective-permute-start.22 = (f32[2,1536]{1,0:T(2,128)S(1)}, f32[2,1536]{1,0:T(2,128)S(1)}, u32[]{:S(2)}, u32[]{:S(2)}) collective-permute-start(f32[2,1536]{1,0:T(2,128)S(1)} %bitcast.27), channel_id=1, source_target_pairs={{0,24},{4,28},{8,16},{12,20},{16,8},{20,12},{24,0},{28,4},{1,25},{... | collective-permute-start | bytes 36872 | tf_op jit(solution)/shard_map/ppermute | solution.py:987
  140.8 3.8 %collective-permute-start.23 = (f32[8,1536]{1,0:T(8,128)S(1)}, f32[8,1536]{1,0:T(8,128)S(1)}, u32[]{:S(2)}, u32[]{:S(2)}) collective-permute-start(f32[8,1536]{1,0:T(8,128)S(1)} %shard_map.276.refs_2_.refs_4_), channel_id=1, source_target_pairs={{0,4},{4,0},{8,12},{12,8},{16,20},{20,16},{24,28},{28,24},{1,5},{5... | collective-permute-start | bytes 147464 | tf_op jit(solution)/shard_map/ppermute | solution.py:987
  141.0 12.4 %collective-permute-start.29 = (f32[192,512]{1,0:T(8,128)S(1)}, f32[192,512]{1,0:T(8,128)S(1)}, u32[]{:S(2)}, u32[]{:S(2)}) collective-permute-start(f32[192,512]{1,0:T(8,128)S(1)} %shard_map.280.refs_1_), channel_id=1, source_target_pairs={{0,8},{4,12},{8,0},{12,4},{16,24},{20,28},{24,16},{28,20},{1,9},{5... | collective-permute-start | bytes 1179656 | tf_op jit(solution)/shard_map/ppermute | solution.py:987
  141.9 19.6 %collective-permute-start.30 = (f32[192,512]{1,0:T(8,128)S(1)}, f32[192,512]{1,0:T(8,128)S(1)}, u32[]{:S(2)}, u32[]{:S(2)}) collective-permute-start(f32[192,512]{1,0:T(8,128)S(1)} %shard_map.280.refs_1_), channel_id=1, source_target_pairs={{0,16},{4,20},{8,24},{12,28},{16,0},{20,4},{24,8},{28,12},{1,17},{... | collective-permute-start | bytes 1179656 | tf_op jit(solution)/shard_map/ppermute | solution.py:987
  143.4 18.1 %collective-permute-start.31 = (f32[192,512]{1,0:T(8,128)S(1)}, f32[192,512]{1,0:T(8,128)S(1)}, u32[]{:S(2)}, u32[]{:S(2)}) collective-permute-start(f32[192,512]{1,0:T(8,128)S(1)} %shard_map.280.refs_1_), channel_id=1, source_target_pairs={{0,24},{4,28},{8,16},{12,20},{16,8},{20,12},{24,0},{28,4},{1,25},{... | collective-permute-start | bytes 1179656 | tf_op jit(solution)/shard_map/ppermute | solution.py:987
  153.4 18.4 %collective-permute-start.32 = (f32[192,512]{1,0:T(8,128)S(1)}, f32[192,512]{1,0:T(8,128)S(1)}, u32[]{:S(2)}, u32[]{:S(2)}) collective-permute-start(f32[192,512]{1,0:T(8,128)S(1)} %shard_map.280.refs_1_), channel_id=1, source_target_pairs={{0,4},{4,0},{8,12},{12,8},{16,20},{20,16},{24,28},{28,24},{1,5},{5... | collective-permute-start | bytes 1179656 | tf_op jit(solution)/shard_map/ppermute | solution.py:987
  161.5 10.3 %collective-permute-start.33 = (f32[192,512]{1,0:T(8,128)S(1)}, f32[192,512]{1,0:T(8,128)S(1)}, u32[]{:S(2)}, u32[]{:S(2)}) collective-permute-start(f32[192,512]{1,0:T(8,128)S(1)} %collective-permute-done.29.refs_2_), channel_id=1, source_target_pairs={{0,4},{4,0},{8,12},{12,8},{16,20},{20,16},{24,28},{28,24},{1,5},{5... | collective-permute-start | bytes 1179656 | tf_op jit(solution)/shard_map/ppermute | solution.py:987
  161.5 10.3 %collective-permute-start.34 = (f32[192,512]{1,0:T(8,128)S(1)}, f32[192,512]{1,0:T(8,128)S(1)}, u32[]{:S(2)}, u32[]{:S(2)}) collective-permute-start(f32[192,512]{1,0:T(8,128)S(1)} %collective-permute-done.30.refs_3_), channel_id=1, source_target_pairs={{0,4},{4,0},{8,12},{12,8},{16,20},{20,16},{24,28},{28,24},{1,5},{5... | collective-permute-start | bytes 1179656 | tf_op jit(solution)/shard_map/ppermute | solution.py:987
  162.0 9.8 %collective-permute-start.35 = (f32[192,512]{1,0:T(8,128)S(1)}, f32[192,512]{1,0:T(8,128)S(1)}, u32[]{:S(2)}, u32[]{:S(2)}) collective-permute-start(f32[192,512]{1,0:T(8,128)S(1)} %collective-permute-done.31.refs_4_), channel_id=1, source_target_pairs={{0,4},{4,0},{8,12},{12,8},{16,20},{20,16},{24,28},{28,24},{1,5},{5... | collective-permute-start | bytes 1179656 | tf_op jit(solution)/shard_map/ppermute | solution.py:987
  (8 other events, 20.2 us)

commit v4 on v3

--- a/solution.py
+++ b/solution.py
@@ -515,7 +515,7 @@
     thick = 3 * (rows + thin)
     deep = downs[0].shape[0] // 12
     for core in range(2):
-        up, down = ups[core], downs[core]
+        up = ups[core]
         sender = (here ^ core) % 2
         near = group ^ (1 + sender)
         bu_s[near] = up[4 * thick :]
@@ -532,9 +532,11 @@
             chip = here ^ (0, 0, 2, 4)[j]
             place = 4 + chip // 4 * 2 if j % 2 else chip // 2 % 2 * 2
             at = pl.multiple_of(place * deep, 2 * deep)
-            wd_s[near, pl.ds(at, 2 * deep)] = down[3 * j * deep : (3 * j + 2) * deep].astype(bf16)
+            down = downs[core]
+            first = 3 * j * deep
+            wd_s[near, pl.ds(at, 2 * deep)] = down[first : first + 2 * deep].astype(bf16)
             at = pl.multiple_of((place + sender) * deep, deep)
-            wd_s[group ^ 3, pl.ds(at, deep)] = down[(3 * j + 2) * deep : (3 * j + 3) * deep].astype(bf16)
+            wd_s[group ^ 3, pl.ds(at, deep)] = down[first + 2 * deep : first + 3 * deep].astype(bf16)
 
 
 def ffn_body(
@@ -555,22 +557,30 @@
     h = (xhat * gain_ref[...] + shift_ref[...]).astype(bf16)
     gm = g_ref[...]
     y = dn = None
-    n = wu_ref.shape[0]
-    for j in range(n):
-        up = nn(h, wu_ref[j]) + bu_ref[j, :1]
-        da = nt(gm, wd_ref[j])
-        if j > 0:
-            y_part = nn(a, wd_ref[j - 1])
-            dn_part = nt(du, wu_ref[j - 1])
-            y = y_part if y is None else y + y_part
-            dn = dn_part if dn is None else dn + dn_part
+    halves_of = 2 * wu_ref.shape[0]
+    half = wu_ref.shape[2] // 2
+
+    def cut(i):
+        return i // 2, slice(i % 2 * half, (i % 2 + 1) * half)
+
+    def finish(i, a, du, y, dn):
+        j, c = cut(i)
+        y_part = nn(a, wd_ref[j, c, :])
+        dn_part = nt(du, wu_ref[j, :, c])
+        return (y_part if y is None else y + y_part), (dn_part if dn is None else dn + dn_part)
+
+    for i in range(halves_of):
+        j, c = cut(i)
+        up = nn(h, wu_ref[j, :, c]) + bu_ref[j, :1, c]
+        da = nt(gm, wd_ref[j, c, :])
+        if i > 0:
+            y, dn = finish(i - 1, a, du, y, dn)
         phi, slope = gelu_parts(up)
         a = (up * phi).astype(bf16)
         du = (da * slope).astype(bf16)
-        a_s[j] = a
-        du_s[j] = du
-    y = y + nn(a, wd_ref[n - 1])
-    dn = dn + nt(du, wu_ref[n - 1])
+        a_s[j, :, c] = a
+        du_s[j, :, c] = du
+    y, dn = finish(halves_of - 1, a, du, y, dn)
     out_ref[...] = (mid + y + bd_ref[...]).astype(bf16)
     g = gm.astype(f32)
     small_ref[2:3] += jnp.sum(dn * xhat, axis=0, keepdims=True)
@@ -659,7 +669,7 @@
         [tok, tok, tok, whole((LANES, width)), whole((1, hidden)), whole((8, width))] + [whole(v.shape) for v in grads],
         [
             shape((tokens, width), bf16),
-            shape((tokens, width), f32),
+            pltpu.HBM((tokens, width), f32),
             shape((tokens, width), bf16),
             shape((LANES, width), f32),
             shape((1, hidden), f32),
@@ -892,7 +902,7 @@
         scratch=[
             pltpu.VMEM((rows, width), f32), pltpu.VMEM((rows, LANES), f32), pltpu.VMEM((devices, rows, 3 * width), f32)
         ],
-        us=10,
+        us=1,
         mib=10,
     )(at, every, *back, misc, x, gain[None], dmid, d, w, small)
 
@@ -1073,9 +1083,12 @@
     d, g_back = pair_backward(*back_args, None, None, devices, region, 1, pairs - 1, (d, g_back))
     if by_share:
         g_back = g_back.reshape(rows, 3 * width)
-        (back,) = cat([[(v, 0, rows) for v in [g_back] + [swap(g_back, "seq", j) for j in others]]])
-        total = add_up([folded[0]] + arrived, [back])
+        total = add_up([folded[0]] + arrived, [g_back])
+        near = [swap(g_back, "seq", j) for j in others[:-1]]
+        held, _ = lax.optimization_barrier((g_back, total))
+        far = swap(held, "seq", others[-1])
         spread = [swap(total, "seq", j) for j in others]
+        (back,) = cat([[(v, 0, rows) for v in [g_back] + near + [far]]])
         back = [back, swap(back, "seq", 1)]
     else:
         back = [lax.all_gather(g_back, "seq").reshape(devices * rows, 3 * width)]
@@ -1083,9 +1096,10 @@
     out = out.reshape(rows, region, width)
     grad_inputs = grad_inputs.reshape(rows, region, width)
     if by_share:
+        small = lax.all_gather(small, "seq")
         pieces = both_cores([total] + spread, small)
         gq, gk, gv, gwo, gwu, gwd = unpack(at, pieces, late)
-        g1, s1, g2, s2, gbd, gbu = (v[0] for v in totals(lax.all_gather(small, "seq")))
+        g1, s1, g2, s2, gbd, gbu = (v[0] for v in totals(small))
         return out, grad_inputs, g1, s1, gq, gk, gv, gwo, g2, s2, gwu, gbu, gwd, gbd
 
     gwu, gwd = hidden_grads

time: 175 us -> 164 us (0.937)
  waiting for transfers between devices: 39.8 us -> 31.7 us
  local copies, waits for them, and re-layouts: 3.22 us -> 1.01 us
    ppermute x33, waiting for transfers between devices: 39.8 us -> 31.7 us  [swap(): lax.ppermute(v, axis, [(i, i ^ mask) for i in range(lax.axis_size(axis))])]
    unnamed x41 -> x35, local copies, waits for them, and re-layouts: 3.22 us -> 1.01 us
  transfers between devices with their start and end apart: 36 -> 36, of which waited for: 11 -> 14; matrix products, arithmetic and copies ran while one was open for 0% -> 0% of each run, Pallas kernels for 28% -> 30%
where the time goes in v4:
time: 164 us
  Pallas kernels  84 us (51%)
  starting transfers between devices  36.6 us (22%)
  waiting for transfers between devices  31.7 us (19%)
  blocking collectives  9.21 us (6%)
    pallas_call x19, Pallas kernels, call(): return lambda *operands: kernel(*operands, *after)  84 us
    ppermute x33, waiting for transfers between devices, swap(): lax.ppermute(v, axis, [(i, i ^ mask) for i in range(lax.axis_size(axis))])  31.7 us
    ppermute x33, starting transfers between devices, swap(): lax.ppermute(v, axis, [(i, i ^ mask) for i in range(lax.axis_size(axis))])  30.5 us
    all_gather x1, blocking collectives, on_device(): small = lax.all_gather(small, 'seq')  9.21 us
    ppermute x3, starting transfers between devices, along_z(): return (lax.ppermute(both, ('seq', 'head'), by_core), swap(one, 'head', 3))  6.15 us
  transfers between devices with their start and end apart: 36, of which 14 were waited for; matrix products, arithmetic and copies ran while one was open for 0% of the time, Pallas kernels for 30%

profile of v4, /device:TPU:0, one launch (start us, length us, event | category | flops | bytes accessed | tf_op | source)
XLA Modules:
  0.0 163.5 jit_solution(14576689603699343087)
XLA Ops:
  0.8 1.4 shard_map.264
  2.2 3.1 %collective-permute-start = (f32[384,128]{1,0:T(8,128)S(1)}, f32[384,128]{1,0:T(8,128)S(1)}, u32[]{:S(2)}, u32[]{:S(2)}) collective-permute-start(f32[384,128]{1,0:T(8,128)S(1)} %get-tuple-element.74), channel_id=1, source_target_pairs={{0,1},{1,0},{2,3},{3,2},{4,6},{5,7},{6,4},{7,5},{8,9},{9,8},{10,11... | collective-permute-start | bytes 589832 | tf_op jit(solution)/shard_map/ppermute | solution.py:1003
  5.3 2.5 %collective-permute-start.1 = (f32[192,128]{1,0:T(8,128)S(1)}, f32[192,128]{1,0:T(8,128)S(1)}, u32[]{:S(2)}, u32[]{:S(2)}) collective-permute-start(f32[192,128]{1,0:T(8,128)S(1)} %get-tuple-element.75), channel_id=1, source_target_pairs={{0,3},{1,2},{2,1},{3,0},{4,7},{5,6},{6,5},{7,4},{8,11},{9,10},{10,... | collective-permute-start | bytes 294920 | tf_op jit(solution)/shard_map/ppermute | solution.py:997
  7.8 2.8 %shard_map.263 = (bf16[1792,512]{1,0:T(8,128)(2,1)S(1)}, f32[2,8,896]{2,1,0:T(8,128)}, f32[2,8,768]{2,1,0:T(8,128)S(1)}, f32[2,8,128]{2,1,0:T(8,128)S(1)}) custom-call(s32[2,896]{1,0:T(2,128)S(1)} %copy-done.10, s32[2,896]{1,0:T(2,128)S(1)} %copy-done.10, s32[2,896]{1,0:T(2,128)S(1)} %copy-done.11, bf16[1792,512]{1,0:T(8,128)(2,1)S(1)} %bitcast.24, ...), custom_call_target="tpu_custom_call" | custom-call | flops 4400000000 | bytes 14000000 | tf_op jit(solution)/shard_map/pallas_call | solution.py:91
  10.6 1.7 %shard_map.266 = (f32[168,512]{1,0:T(8,128)S(1)}, f32[88,512]{1,0:T(8,128)S(1)}, f32[256,512]{1,0:T(8,128)S(1)}, f32[128,512]{1,0:T(8,128)S(1)}) custom-call(s32[3]{0:T(128)S(1)} %pad_add_fusion.refs_0_, bf16[512,512]{1,0:T(8,128)(2,1)} %refs_8_.1, bf16[128,512]{1,0:T(8,128)(2,1)} %refs_9_.1, f32[1,512]{1,0:T(1,128)} %bitcast.40, bf16[512,512]{1,0:T(8,128)(2,1)} %refs_11_.1, ...), custom_call_target="tpu_custom_call" | custom-call | flops 2200000000 | bytes 7000000 | tf_op jit(solution)/shard_map/pallas_call | solution.py:91
  12.3 0.7 collective-permute-start.6
  13.0 0.9 collective-permute-start.7
  13.9 0.5 collective-permute-done.1.refs_1_
  14.5 1.6 collective-permute-start.2
  16.0 1.5 collective-permute-start.3
  18.0 8.2 %collective-permute-done.7.refs_1_.refs_16_ = f32[88,512]{1,0:T(8,128)S(1)} collective-permute-done((f32[88,512]{1,0:T(8,128)S(1)}, f32[88,512]{1,0:T(8,128)S(1)}, u32[]{:S(2)}, u32[]{:S(2)}) %collective-permute-start.7) | collective-permute-done | bytes 180256 | tf_op jit(solution)/shard_map/ppermute | solution.py:997
  26.2 4.5 %collective-permute-done.3.refs_7_.refs_9_ = f32[592,128]{1,0:T(8,128)S(1)} collective-permute-done((f32[592,128]{1,0:T(8,128)S(1)}, f32[592,128]{1,0:T(8,128)S(1)}, u32[]{:S(2)}, u32[]{:S(2)}) %collective-permute-start.3) | collective-permute-done | bytes 303136 | tf_op jit(solution)/shard_map/ppermute | solution.py:997
  30.7 0.5 collective-permute-start.8
  31.2 2.3 %collective-permute-start.14 = (f32[256,512]{1,0:T(8,128)S(1)}, f32[256,512]{1,0:T(8,128)S(1)}, u32[]{:S(2)}, u32[]{:S(2)}) collective-permute-start(f32[256,512]{1,0:T(8,128)S(1)} %get-tuple-element.86), channel_id=1, source_target_pairs={{0,1},{1,0},{2,3},{3,2},{4,6},{5,7},{6,4},{7,5},{8,9},{9,8},{10,11... | collective-permute-start | bytes 1572872 | tf_op jit(solution)/shard_map/ppermute | solution.py:1003
  33.5 4.1 %collective-permute-start.15 = (f32[128,512]{1,0:T(8,128)S(1)}, f32[128,512]{1,0:T(8,128)S(1)}, u32[]{:S(2)}, u32[]{:S(2)}) collective-permute-start(f32[128,512]{1,0:T(8,128)S(1)} %get-tuple-element.87), channel_id=1, source_target_pairs={{0,3},{1,2},{2,1},{3,0},{4,7},{5,6},{6,5},{7,4},{8,11},{9,10},{10,... | collective-permute-start | bytes 786440 | tf_op jit(solution)/shard_map/ppermute | solution.py:997
  37.7 1.0 collective-permute-start.11
  38.6 1.1 collective-permute-start.12
  39.7 1.4 collective-permute-start.13
  41.2 0.8 shard_map.268
  42.2 13.9 %shard_map.269 = (bf16[1792,1536]{1,0:T(8,128)(2,1)S(1)}, bf16[4,14,256,128]{3,2,1,0:T(8,128)(2,1)S(1)}, f32[4,14,8,128]{3,2,1,0:T(8,128)S(1)}, bf16[1792,512]{1...) custom-call(s32[3]{0:T(128)S(1)} %pad_add_fusion.refs_0_, ...), custom_call_target="tpu_custom_call" | custom-call | flops 22000001024 | bytes 70000000 | tf_op jit(solution)/shard_map/pallas_call | solution.py:91
  56.2 1.0 collective-permute-start.17
  57.2 1.1 collective-permute-start.18
  58.4 2.9 %collective-permute-done.13.refs_3_ = f32[240,512]{1,0:T(8,128)S(1)} collective-permute-done((f32[240,512]{1,0:T(8,128)S(1)}, f32[240,512]{1,0:T(8,128)S(1)}, u32[]{:S(2)}, u32[]{:S(2)}) %collective-permute-start.13) | collective-permute-done | bytes 491552 | tf_op jit(solution)/shard_map/ppermute | solution.py:997
  61.6 6.6 %collective-permute-done.17.refs_2_ = f32[192,512]{1,0:T(8,128)S(1)} collective-permute-done((f32[192,512]{1,0:T(8,128)S(1)}, f32[192,512]{1,0:T(8,128)S(1)}, u32[]{:S(2)}, u32[]{:S(2)}) %collective-permute-start.17) | collective-permute-done | bytes 393248 | tf_op jit(solution)/shard_map/ppermute | solution.py:997
  68.1 0.9 collective-permute-done.18.refs_3_
  69.2 3.4 %collective-permute-done.19.refs_15_ = f32[768,512]{1,0:T(8,128)S(1)} collective-permute-done((f32[768,512]{1,0:T(8,128)S(1)}, f32[768,512]{1,0:T(8,128)S(1)}, u32[]{:S(2)}, u32[]{:S(2)}) %collective-permute-start.19) | collective-permute-done | bytes 1572896 | tf_op jit(solution)/shard_map/ppermute | solution.py:997
  72.7 31.1 %shard_map.273 = (bf16[1792,512]{1,0:T(8,128)(2,1)}, f32[1792,512]{1,0:T(8,128)}, bf16[1792,512]{1,0:T(8,128)(2,1)S(1)}, f32[128,512]{1,0:T(8,128)S(1)}, f32[1,5...) custom-call(s32[3]{0:T(128)S(1)} %pad_add_fusion.refs_0_, ...), custom_call_target="tpu_custom_call" | custom-call | flops 41799999488 | bytes 133000000 | tf_op jit(solution)/shard_map/pallas_call | solution.py:91
  103.9 5.7 %shard_map.274 = (bf16[1792,1536]{1,0:T(8,128)(2,1)S(1)}, f32[2,1,1536]{2,1,0:T(1,128)S(1)}, f32[4,64,512]{2,1,0:T(8,128)S(1)}, f32[4,64,512]{2,1,0:T(8,128)S(1)}) custom-call(s32[3]{0:T(128)S(1)} %pad_add_fusion.refs_0_, bf16[1792,1536]{1,0:T(8,128)(2,1)S(1)} %get-tuple-element.92.refs_1_, bf16[1792,512]{1,0:T(8,128)(2,1)S(1)} %get-tuple-element.93.refs_2_, ...), custom_call_target="tpu_custom_call" | custom-call | flops 6600000000 | bytes 21000000 | tf_op jit(solution)/shard_map/pallas_call | solution.py:91
  110.1 1.5 collective-permute-done.23.refs_4_
  111.7 0.8 shard_map.276
  112.4 0.9 collective-permute-start.24
  113.3 1.5 collective-permute-start.25
  114.8 1.2 collective-permute-start.26
  116.0 13.5 %shard_map.275 = (bf16[1792,1536]{1,0:T(8,128)(2,1)S(1)}, f32[2,1,1536]{2,1,0:T(1,128)S(1)}) custom-call(s32[3]{0:T(128)S(1)} %pad_add_fusion.refs_0_, bf16[1792,1536]{1,0:T(8,128)(2,1)S(1)} %get-tuple-element.92.refs_1_, bf16[1792,512]{1,0:T(8,128)(2,1)S(1)} %get-tuple-element.93.refs_2_, ...), custom_call_target="tpu_custom_call", output_to_operand_aliasing={{0}: (7, {}), {1}: (8, {})} | custom-call | flops 19800000512 | bytes 63000000 | tf_op jit(solution)/shard_map/pallas_call | solution.py:91
  129.5 0.9 collective-permute-start.20
  130.3 1.5 collective-permute-start.21
  131.9 1.0 collective-permute-done.25.refs_2_
  133.0 1.6 collective-permute-start.27
  134.6 1.5 collective-permute-start.29
  136.5 1.5 collective-permute-start.31
  138.7 0.7 collective-permute-done.28.refs_3_
  139.4 0.7 copy-done
  140.1 8.8 %shard_map.279 = (f32[1792,512]{1,0:T(8,128)}, f32[8,512]{1,0:T(8,128)S(1)}, f32[512,384]{1,0:T(8,128)S(1)}) custom-call(s32[3]{0:T(128)S(1)} %pad_add_fusion.refs_0_, f32[8,16,128]{2,1,0:T(8,128)S(1)} %get-tuple-element.91.refs_1_, f32[8,1536]{1,0:T(8,128)S(1)} %shard_map.278.refs_2_, f32[8,1536]{1,0:T(8,128)S(1)} %collective-permute-done.28.refs_3_, ...), custom_call_target="tpu_custom_call" | custom-call | flops 1100000000 | bytes 3500000 | tf_op jit(solution)/shard_map/pallas_call | solution.py:91
  148.9 9.2 %all-gather = f32[64,512]{1,0:T(8,128)S(1)} all-gather(f32[8,512]{1,0:T(8,128)S(1)} %get-tuple-element.115), channel_id=2, replica_groups=mesh['seq'=8,'head'=4] {'seq'}, dimensions={0}, use_global_device_ids=true | all-gather | bytes 147456 | tf_op jit(solution)/shard_map/all_gather | solution.py:1099
  159.1 0.6 shard_map.280
  159.9 0.6 collective-permute-done.34.refs_7_
  160.5 0.6 collective-permute-done.35.refs_8_
  161.1 2.5 %shard_map.281 = (f32[512,128]{1,0:T(8,128)}, f32[512,128]{1,0:T(8,128)}, f32[512,128]{1,0:T(8,128)}, f32[128,512]{1,0:T(8,128)}, f32[512,512]{1,0:T(8,128)}, /*index=5*/f32[512,512]{1,0:T(8,128)}) custom-call(s32[3]{0:T(128)S(1)} %pad_add_fusion.refs_0_, f32[192,512]{1,0:T(8,128)S(1)} %shard_map.277.refs_1_, ...), custom_call_target="tpu_custom_call" | custom-call | flops 2200000000 | bytes 7000000 | tf_op jit(solution)/shard_map/pallas_call | solution.py:91
  (80 shorter events, 4.3 us)
Async XLA Ops:
  0.7 7.0 %copy-start.1 = (bf16[2,896,512]{2,1,0:T(8,128)(2,1)S(1)}, bf16[2,896,512]{2,1,0:T(8,128)(2,1)}, u32[]{:S(2)}) copy-start(bf16[2,896,512]{2,1,0:T(8,128)(2,1)} %param.16) | copy-start | bytes 5505028
  0.7 7.0 %copy-start.2 = (f32[512]{0:T(512)S(1)}, f32[512]{0:T(512)}, u32[]{:S(2)}) copy-start(f32[512]{0:T(512)} %param.19) | copy-start | bytes 6148
  0.7 7.0 %copy-start.10 = (s32[2,896]{1,0:T(2,128)S(1)}, s32[2,896]{1,0:T(2,128)}, u32[]{:S(2)}) copy-start(s32[2,896]{1,0:T(2,128)} %refs_2_.7) | copy-start | bytes 21508
  0.7 7.0 %copy-start.11 = (s32[2,896]{1,0:T(2,128)S(1)}, s32[2,896]{1,0:T(2,128)}, u32[]{:S(2)}) copy-start(s32[2,896]{1,0:T(2,128)} %refs_3_.3) | copy-start | bytes 21508
  2.2 12.3 %collective-permute-start = (f32[384,128]{1,0:T(8,128)S(1)}, f32[384,128]{1,0:T(8,128)S(1)}, u32[]{:S(2)}, u32[]{:S(2)}) collective-permute-start(f32[384,128]{1,0:T(8,128)S(1)} %get-tuple-element.74), channel_id=1, source_target_pairs={{0,1},{1,0},{2,3},{3,2},{4,6},{5,7},{6,4},{7,5},{8,9},{9,8},{10,11... | collective-permute-start | bytes 589832 | tf_op jit(solution)/shard_map/ppermute | solution.py:1003
  5.3 9.2 %collective-permute-start.1 = (f32[192,128]{1,0:T(8,128)S(1)}, f32[192,128]{1,0:T(8,128)S(1)}, u32[]{:S(2)}, u32[]{:S(2)}) collective-permute-start(f32[192,128]{1,0:T(8,128)S(1)} %get-tuple-element.75), channel_id=1, source_target_pairs={{0,3},{1,2},{2,1},{3,0},{4,7},{5,6},{6,5},{7,4},{8,11},{9,10},{10,... | collective-permute-start | bytes 294920 | tf_op jit(solution)/shard_map/ppermute | solution.py:997
  12.3 13.9 %collective-permute-start.6 = (f32[168,512]{1,0:T(8,128)S(1)}, f32[168,512]{1,0:T(8,128)S(1)}, u32[]{:S(2)}, u32[]{:S(2)}) collective-permute-start(f32[168,512]{1,0:T(8,128)S(1)} %get-tuple-element.78), channel_id=1, source_target_pairs={{0,1},{1,0},{2,3},{3,2},{4,6},{5,7},{6,4},{7,5},{8,9},{9,8},{10,11... | collective-permute-start | bytes 1032200 | tf_op jit(solution)/shard_map/ppermute | solution.py:1003
  13.0 13.2 %collective-permute-start.7 = (f32[88,512]{1,0:T(8,128)S(1)}, f32[88,512]{1,0:T(8,128)S(1)}, u32[]{:S(2)}, u32[]{:S(2)}) collective-permute-start(f32[88,512]{1,0:T(8,128)S(1)} %get-tuple-element.79), channel_id=1, source_target_pairs={{0,3},{1,2},{2,1},{3,0},{4,7},{5,6},{6,5},{7,4},{8,11},{9,10},{10,... | collective-permute-start | bytes 540680 | tf_op jit(solution)/shard_map/ppermute | solution.py:997
  14.5 11.8 %collective-permute-start.2 = (f32[592,128]{1,0:T(8,128)S(1)}, f32[592,128]{1,0:T(8,128)S(1)}, u32[]{:S(2)}, u32[]{:S(2)}) collective-permute-start(f32[592,128]{1,0:T(8,128)S(1)} %shard_map.265.refs_5_.refs_7_), channel_id=1, source_target_pairs={{0,8},{4,12},{8,0},{12,4},{16,24},{20,28},{24,16},{28,20},{1,9},{5... | collective-permute-start | bytes 909320 | tf_op jit(solution)/shard_map/ppermute | solution.py:997
  16.0 14.7 %collective-permute-start.3 = (f32[592,128]{1,0:T(8,128)S(1)}, f32[592,128]{1,0:T(8,128)S(1)}, u32[]{:S(2)}, u32[]{:S(2)}) collective-permute-start(f32[592,128]{1,0:T(8,128)S(1)} %shard_map.265.refs_5_.refs_7_), channel_id=1, source_target_pairs={{0,16},{4,20},{8,24},{12,28},{16,0},{20,4},{24,8},{28,12},{1,17},{... | collective-permute-start | bytes 909320 | tf_op jit(solution)/shard_map/ppermute | solution.py:997
  17.5 13.2 %collective-permute-start.4 = (f32[592,128]{1,0:T(8,128)S(1)}, f32[592,128]{1,0:T(8,128)S(1)}, u32[]{:S(2)}, u32[]{:S(2)}) collective-permute-start(f32[592,128]{1,0:T(8,128)S(1)} %shard_map.265.refs_5_.refs_7_), channel_id=1, source_target_pairs={{0,24},{4,28},{8,16},{12,20},{16,8},{20,12},{24,0},{28,4},{1,25},{... | collective-permute-start | bytes 909320 | tf_op jit(solution)/shard_map/ppermute | solution.py:997
  26.2 7.4 %collective-permute-start.5 = (f32[592,128]{1,0:T(8,128)S(1)}, f32[592,128]{1,0:T(8,128)S(1)}, u32[]{:S(2)}, u32[]{:S(2)}) collective-permute-start(f32[592,128]{1,0:T(8,128)S(1)} %shard_map.265.refs_5_.refs_7_), channel_id=1, source_target_pairs={{0,4},{4,0},{8,12},{12,8},{16,20},{20,16},{24,28},{28,24},{1,5},{5... | collective-permute-start | bytes 909320 | tf_op jit(solution)/shard_map/ppermute | solution.py:997
  30.7 7.0 %collective-permute-start.10 = (f32[592,128]{1,0:T(8,128)S(1)}, f32[592,128]{1,0:T(8,128)S(1)}, u32[]{:S(2)}, u32[]{:S(2)}) collective-permute-start(f32[592,128]{1,0:T(8,128)S(1)} %collective-permute-done.4.refs_8_.refs_10_), channel_id=1, source_target_pairs={{0,4},{4,0},{8,12},{12,8},{16,20},{20,16},{24,28},{28,24},{1,5},{5... | collective-permute-start | bytes 909320 | tf_op jit(solution)/shard_map/ppermute | solution.py:997
  30.7 7.9 %collective-permute-start.8 = (f32[592,128]{1,0:T(8,128)S(1)}, f32[592,128]{1,0:T(8,128)S(1)}, u32[]{:S(2)}, u32[]{:S(2)}) collective-permute-start(f32[592,128]{1,0:T(8,128)S(1)} %collective-permute-done.2.refs_6_.refs_8_), channel_id=1, source_target_pairs={{0,4},{4,0},{8,12},{12,8},{16,20},{20,16},{24,28},{28,24},{1,5},{5... | collective-permute-start | bytes 909320 | tf_op jit(solution)/shard_map/ppermute | solution.py:997
  31.2 8.5 %collective-permute-start.9 = (f32[592,128]{1,0:T(8,128)S(1)}, f32[592,128]{1,0:T(8,128)S(1)}, u32[]{:S(2)}, u32[]{:S(2)}) collective-permute-start(f32[592,128]{1,0:T(8,128)S(1)} %collective-permute-done.3.refs_7_.refs_9_), channel_id=1, source_target_pairs={{0,4},{4,0},{8,12},{12,8},{16,20},{20,16},{24,28},{28,24},{1,5},{5... | collective-permute-start | bytes 909320 | tf_op jit(solution)/shard_map/ppermute | solution.py:997
  31.2 24.9 %collective-permute-start.14 = (f32[256,512]{1,0:T(8,128)S(1)}, f32[256,512]{1,0:T(8,128)S(1)}, u32[]{:S(2)}, u32[]{:S(2)}) collective-permute-start(f32[256,512]{1,0:T(8,128)S(1)} %get-tuple-element.86), channel_id=1, source_target_pairs={{0,1},{1,0},{2,3},{3,2},{4,6},{5,7},{6,4},{7,5},{8,9},{9,8},{10,11... | collective-permute-start | bytes 1572872 | tf_op jit(solution)/shard_map/ppermute | solution.py:1003
  33.5 22.6 %collective-permute-start.15 = (f32[128,512]{1,0:T(8,128)S(1)}, f32[128,512]{1,0:T(8,128)S(1)}, u32[]{:S(2)}, u32[]{:S(2)}) collective-permute-start(f32[128,512]{1,0:T(8,128)S(1)} %get-tuple-element.87), channel_id=1, source_target_pairs={{0,3},{1,2},{2,1},{3,0},{4,7},{5,6},{6,5},{7,4},{8,11},{9,10},{10,... | collective-permute-start | bytes 786440 | tf_op jit(solution)/shard_map/ppermute | solution.py:997
  37.7 20.6 %collective-permute-start.11 = (f32[240,512]{1,0:T(8,128)S(1)}, f32[240,512]{1,0:T(8,128)S(1)}, u32[]{:S(2)}, u32[]{:S(2)}) collective-permute-start(f32[240,512]{1,0:T(8,128)S(1)} %shard_map.267.refs_0_), channel_id=1, source_target_pairs={{0,8},{4,12},{8,0},{12,4},{16,24},{20,28},{24,16},{28,20},{1,9},{5... | collective-permute-start | bytes 1474568 | tf_op jit(solution)/shard_map/ppermute | solution.py:997
  38.6 19.8 %collective-permute-start.12 = (f32[240,512]{1,0:T(8,128)S(1)}, f32[240,512]{1,0:T(8,128)S(1)}, u32[]{:S(2)}, u32[]{:S(2)}) collective-permute-start(f32[240,512]{1,0:T(8,128)S(1)} %shard_map.267.refs_0_), channel_id=1, source_target_pairs={{0,16},{4,20},{8,24},{12,28},{16,0},{20,4},{24,8},{28,12},{1,17},{... | collective-permute-start | bytes 1474568 | tf_op jit(solution)/shard_map/ppermute | solution.py:997
  39.7 21.5 %collective-permute-start.13 = (f32[240,512]{1,0:T(8,128)S(1)}, f32[240,512]{1,0:T(8,128)S(1)}, u32[]{:S(2)}, u32[]{:S(2)}) collective-permute-start(f32[240,512]{1,0:T(8,128)S(1)} %shard_map.267.refs_0_), channel_id=1, source_target_pairs={{0,24},{4,28},{8,16},{12,20},{16,8},{20,12},{24,0},{28,4},{1,25},{... | collective-permute-start | bytes 1474568 | tf_op jit(solution)/shard_map/ppermute | solution.py:997
  56.2 12.0 %collective-permute-start.17 = (f32[192,512]{1,0:T(8,128)S(1)}, f32[192,512]{1,0:T(8,128)S(1)}, u32[]{:S(2)}, u32[]{:S(2)}) collective-permute-start(f32[192,512]{1,0:T(8,128)S(1)} %get-tuple-element.88.refs_5_.refs_0_), channel_id=1, source_target_pairs={{0,8},{4,12},{8,0},{12,4},{16,24},{20,28},{24,16},{28,20},{1,9},{5... | collective-permute-start | bytes 1179656 | tf_op jit(solution)/shard_map/ppermute | solution.py:997
  57.2 11.8 %collective-permute-start.18 = (f32[192,512]{1,0:T(8,128)S(1)}, f32[192,512]{1,0:T(8,128)S(1)}, u32[]{:S(2)}, u32[]{:S(2)}) collective-permute-start(f32[192,512]{1,0:T(8,128)S(1)} %get-tuple-element.89.refs_1_), channel_id=1, source_target_pairs={{0,16},{4,20},{8,24},{12,28},{16,0},{20,4},{24,8},{28,12},{1,17},{... | collective-permute-start | bytes 1179656 | tf_op jit(solution)/shard_map/ppermute | solution.py:997
  61.4 11.2 %copy-start.3 = (bf16[2,896,512]{2,1,0:T(8,128)(2,1)S(1)}, bf16[2,896,512]{2,1,0:T(8,128)(2,1)}, u32[]{:S(2)}) copy-start(bf16[2,896,512]{2,1,0:T(8,128)(2,1)} %param.31) | copy-start | bytes 5505028
  61.4 11.2 %copy-start.4 = (bf16[512,512]{1,0:T(8,128)(2,1)S(1)}, bf16[512,512]{1,0:T(8,128)(2,1)}, u32[]{:S(2)}) copy-start(bf16[512,512]{1,0:T(8,128)(2,1)} %refs_8_.1) | copy-start | bytes 1572868
  61.4 11.2 %copy-start.5 = (bf16[512,512]{1,0:T(8,128)(2,1)S(1)}, bf16[512,512]{1,0:T(8,128)(2,1)}, u32[]{:S(2)}) copy-start(bf16[512,512]{1,0:T(8,128)(2,1)} %refs_11_.1) | copy-start | bytes 1572868
  61.4 11.2 %copy-start.9 = (bf16[128,512]{1,0:T(8,128)(2,1)S(1)}, bf16[128,512]{1,0:T(8,128)(2,1)}, u32[]{:S(2)}) copy-start(bf16[128,512]{1,0:T(8,128)(2,1)} %refs_9_.1) | copy-start | bytes 393220
  61.5 11.2 %copy-start.13 = (f32[512]{0:T(512)S(1)}, f32[512]{0:T(512)}, u32[]{:S(2)}) copy-start(f32[512]{0:T(512)} %param.25) | copy-start | bytes 6148
  61.5 11.2 %copy-start.14 = (f32[512]{0:T(512)S(1)}, f32[512]{0:T(512)}, u32[]{:S(2)}) copy-start(f32[512]{0:T(512)} %param.26) | copy-start | bytes 6148
  61.5 11.2 %copy-start.15 = (f32[512]{0:T(512)S(1)}, f32[512]{0:T(512)}, u32[]{:S(2)}) copy-start(f32[512]{0:T(512)} %param.30) | copy-start | bytes 6148
  61.5 11.2 %copy-start.16 = (f32[512]{0:T(512)S(1)}, f32[512]{0:T(512)}, u32[]{:S(2)}) copy-start(f32[512]{0:T(512)} %param.28) | copy-start | bytes 6148
  61.5 11.1 %collective-permute-start.16 = (f32[968,512]{1,0:T(8,128)S(1)}, f32[968,512]{1,0:T(8,128)S(1)}, u32[]{:S(2)}, u32[]{:S(2)}) collective-permute-start(f32[968,512]{1,0:T(8,128)S(1)} %shard_map.271.refs_4_.refs_12_), channel_id=1, source_target_pairs={{0,4},{4,0},{8,12},{12,8},{16,20},{20,16},{24,28},{28,24},{1,5},{5... | collective-permute-start | bytes 5947400 | tf_op jit(solution)/shard_map/ppermute | solution.py:997
  69.2 3.5 %collective-permute-start.19 = (f32[768,512]{1,0:T(8,128)S(1)}, f32[768,512]{1,0:T(8,128)S(1)}, u32[]{:S(2)}, u32[]{:S(2)}) collective-permute-start(f32[768,512]{1,0:T(8,128)S(1)} %shard_map.272.refs_14_), channel_id=1, source_target_pairs={{0,4},{4,0},{8,12},{12,8},{16,20},{20,16},{24,28},{28,24},{1,5},{5... | collective-permute-start | bytes 4718600 | tf_op jit(solution)/shard_map/ppermute | solution.py:997
  103.8 7.9 %collective-permute-start.22 = (f32[4,128,512]{2,1,0:T(8,128)S(1)}, f32[4,128,512]{2,1,0:T(8,128)S(1)}, u32[]{:S(2)}, u32[]{:S(2)}) collective-permute-start(f32[4,128,512]{2,1,0:T(8,128)S(1)} %get-tuple-element.103), channel_id=1, source_target_pairs={{0,4},{4,0},{8,12},{12,8},{16,20},{20,16},{24,28},{28,24},{1,5},{5... | collective-permute-start | bytes 3145736 | tf_op jit(solution)/shard_map/ppermute | solution.py:997
  109.7 2.0 %collective-permute-start.23 = (f32[4,64,512]{2,1,0:T(8,128)S(1)}, f32[4,64,512]{2,1,0:T(8,128)S(1)}, u32[]{:S(2)}, u32[]{:S(2)}) collective-permute-start(f32[4,64,512]{2,1,0:T(8,128)S(1)} %get-tuple-element.104), channel_id=1, source_target_pairs={{0,4},{4,0},{8,12},{12,8},{16,20},{20,16},{24,28},{28,24},{1,5},{5... | collective-permute-start | bytes 1572872 | tf_op jit(solution)/shard_map/ppermute | solution.py:997
  112.4 19.4 %collective-permute-start.24 = (f32[192,512]{1,0:T(8,128)S(1)}, f32[192,512]{1,0:T(8,128)S(1)}, u32[]{:S(2)}, u32[]{:S(2)}) collective-permute-start(f32[192,512]{1,0:T(8,128)S(1)} %get-tuple-element.106), channel_id=1, source_target_pairs={{0,8},{4,12},{8,0},{12,4},{16,24},{20,28},{24,16},{28,20},{1,9},{5... | collective-permute-start | bytes 1179656 | tf_op jit(solution)/shard_map/ppermute | solution.py:997
  113.3 19.6 %collective-permute-start.25 = (f32[192,512]{1,0:T(8,128)S(1)}, f32[192,512]{1,0:T(8,128)S(1)}, u32[]{:S(2)}, u32[]{:S(2)}) collective-permute-start(f32[192,512]{1,0:T(8,128)S(1)} %get-tuple-element.107), channel_id=1, source_target_pairs={{0,16},{4,20},{8,24},{12,28},{16,0},{20,4},{24,8},{28,12},{1,17},{... | collective-permute-start | bytes 1179656 | tf_op jit(solution)/shard_map/ppermute | solution.py:997
  114.8 18.1 %collective-permute-start.26 = (f32[192,512]{1,0:T(8,128)S(1)}, f32[192,512]{1,0:T(8,128)S(1)}, u32[]{:S(2)}, u32[]{:S(2)}) collective-permute-start(f32[192,512]{1,0:T(8,128)S(1)} %get-tuple-element.108), channel_id=1, source_target_pairs={{0,24},{4,28},{8,16},{12,20},{16,8},{20,12},{24,0},{28,4},{1,25},{... | collective-permute-start | bytes 1179656 | tf_op jit(solution)/shard_map/ppermute | solution.py:997
  129.5 7.1 %collective-permute-start.20 = (f32[2,1536]{1,0:T(2,128)S(1)}, f32[2,1536]{1,0:T(2,128)S(1)}, u32[]{:S(2)}, u32[]{:S(2)}) collective-permute-start(f32[2,1536]{1,0:T(2,128)S(1)} %bitcast.28), channel_id=1, source_target_pairs={{0,8},{4,12},{8,0},{12,4},{16,24},{20,28},{24,16},{28,20},{1,9},{5... | collective-permute-start | bytes 36872 | tf_op jit(solution)/shard_map/ppermute | solution.py:997
  130.3 7.7 %collective-permute-start.21 = (f32[2,1536]{1,0:T(2,128)S(1)}, f32[2,1536]{1,0:T(2,128)S(1)}, u32[]{:S(2)}, u32[]{:S(2)}) collective-permute-start(f32[2,1536]{1,0:T(2,128)S(1)} %bitcast.29), channel_id=1, source_target_pairs={{0,16},{4,20},{8,24},{12,28},{16,0},{20,4},{24,8},{28,12},{1,17},{... | collective-permute-start | bytes 36872 | tf_op jit(solution)/shard_map/ppermute | solution.py:997
  133.0 5.1 %collective-permute-start.27 = (f32[2,1536]{1,0:T(2,128)S(1)}, f32[2,1536]{1,0:T(2,128)S(1)}, u32[]{:S(2)}, u32[]{:S(2)}) collective-permute-start(f32[2,1536]{1,0:T(2,128)S(1)} %bitcast.31), channel_id=1, source_target_pairs={{0,24},{4,28},{8,16},{12,20},{16,8},{20,12},{24,0},{28,4},{1,25},{... | collective-permute-start | bytes 36872 | tf_op jit(solution)/shard_map/ppermute | solution.py:997
  134.6 23.6 %collective-permute-start.29 = (f32[192,512]{1,0:T(8,128)S(1)}, f32[192,512]{1,0:T(8,128)S(1)}, u32[]{:S(2)}, u32[]{:S(2)}) collective-permute-start(f32[192,512]{1,0:T(8,128)S(1)} %shard_map.277.refs_1_), channel_id=1, source_target_pairs={{0,8},{4,12},{8,0},{12,4},{16,24},{20,28},{24,16},{28,20},{1,9},{5... | collective-permute-start | bytes 1179656 | tf_op jit(solution)/shard_map/ppermute | solution.py:997
  136.1 22.0 %collective-permute-start.30 = (f32[192,512]{1,0:T(8,128)S(1)}, f32[192,512]{1,0:T(8,128)S(1)}, u32[]{:S(2)}, u32[]{:S(2)}) collective-permute-start(f32[192,512]{1,0:T(8,128)S(1)} %shard_map.277.refs_1_), channel_id=1, source_target_pairs={{0,16},{4,20},{8,24},{12,28},{16,0},{20,4},{24,8},{28,12},{1,17},{... | collective-permute-start | bytes 1179656 | tf_op jit(solution)/shard_map/ppermute | solution.py:997
  136.5 21.6 %collective-permute-start.31 = (f32[192,512]{1,0:T(8,128)S(1)}, f32[192,512]{1,0:T(8,128)S(1)}, u32[]{:S(2)}, u32[]{:S(2)}) collective-permute-start(f32[192,512]{1,0:T(8,128)S(1)} %shard_map.277.refs_1_), channel_id=1, source_target_pairs={{0,24},{4,28},{8,16},{12,20},{16,8},{20,12},{24,0},{28,4},{1,25},{... | collective-permute-start | bytes 1179656 | tf_op jit(solution)/shard_map/ppermute | solution.py:997
  138.1 1.3 collective-permute-start.28
  138.2 21.5 %collective-permute-start.32 = (f32[192,512]{1,0:T(8,128)S(1)}, f32[192,512]{1,0:T(8,128)S(1)}, u32[]{:S(2)}, u32[]{:S(2)}) collective-permute-start(f32[192,512]{1,0:T(8,128)S(1)} %shard_map.277.refs_1_), channel_id=1, source_target_pairs={{0,4},{4,0},{8,12},{12,8},{16,20},{20,16},{24,28},{28,24},{1,5},{5... | collective-permute-start | bytes 1179656 | tf_op jit(solution)/shard_map/ppermute | solution.py:997
  158.1 1.8 %collective-permute-start.33 = (f32[192,512]{1,0:T(8,128)S(1)}, f32[192,512]{1,0:T(8,128)S(1)}, u32[]{:S(2)}, u32[]{:S(2)}) collective-permute-start(f32[192,512]{1,0:T(8,128)S(1)} %collective-permute-done.29.refs_2_), channel_id=1, source_target_pairs={{0,4},{4,0},{8,12},{12,8},{16,20},{20,16},{24,28},{28,24},{1,5},{5... | collective-permute-start | bytes 1179656 | tf_op jit(solution)/shard_map/ppermute | solution.py:997
  158.6 1.9 %collective-permute-start.34 = (f32[192,512]{1,0:T(8,128)S(1)}, f32[192,512]{1,0:T(8,128)S(1)}, u32[]{:S(2)}, u32[]{:S(2)}) collective-permute-start(f32[192,512]{1,0:T(8,128)S(1)} %collective-permute-done.30.refs_3_), channel_id=1, source_target_pairs={{0,4},{4,0},{8,12},{12,8},{16,20},{20,16},{24,28},{28,24},{1,5},{5... | collective-permute-start | bytes 1179656 | tf_op jit(solution)/shard_map/ppermute | solution.py:997
  158.7 2.3 %collective-permute-start.35 = (f32[192,512]{1,0:T(8,128)S(1)}, f32[192,512]{1,0:T(8,128)S(1)}, u32[]{:S(2)}, u32[]{:S(2)}) collective-permute-start(f32[192,512]{1,0:T(8,128)S(1)} %collective-permute-done.31.refs_4_), channel_id=1, source_target_pairs={{0,4},{4,0},{8,12},{12,8},{16,20},{20,16},{24,28},{28,24},{1,5},{5... | collective-permute-start | bytes 1179656 | tf_op jit(solution)/shard_map/ppermute | solution.py:997
  (5 other events, 11.9 us)

commit v5 on v4

--- a/solution.py
+++ b/solution.py
@@ -902,7 +902,7 @@
         scratch=[
             pltpu.VMEM((rows, width), f32), pltpu.VMEM((rows, LANES), f32), pltpu.VMEM((devices, rows, 3 * width), f32)
         ],
-        us=1,
+        us=2,
         mib=10,
     )(at, every, *back, misc, x, gain[None], dmid, d, w, small)
 
@@ -968,17 +968,25 @@
     )(at, *args)
 
 
-def totals_body(small_ref, *outs):
-    total = small_ref[0]
-    for d in range(1, small_ref.shape[0]):
-        total = total + small_ref[d]
+def totals_body(at_s, mine_ref, theirs_ref, *refs):
+    *outs, lines_s = refs
+    for core, ref in enumerate((mine_ref, theirs_ref)):
+        for j in range(lines_s.shape[0] // 2):
+            lines_s[at_s[0] ^ (2 * j + core)] = ref[8 * j : 8 * j + 8]
+    total = lines_s[0]
+    for d in range(1, lines_s.shape[0]):
+        total = total + lines_s[d]
     for i, out in enumerate(outs):
         out[...] = total[i : i + 1]
 
 
-def totals(small):
-    outs = [shape((1, small.shape[2]), f32)] * 6
-    return call(totals_body, (1,), 0, [whole(small.shape)], [whole(v.shape) for v in outs], outs)(small)
+def totals(at, mine, theirs):
+    width = mine.shape[1]
+    outs = [shape((1, width), f32)] * 6
+    return call(
+        totals_body, (1,), 1, [whole(mine.shape)] * 2, [whole(v.shape) for v in outs], outs,
+        scratch=[pltpu.VMEM((mine.shape[0] // 4, 8, width), f32)],
+    )(at, mine, theirs)
 
 
 def narrow_body(w_ref, o_ref):
@@ -1096,10 +1104,10 @@
     out = out.reshape(rows, region, width)
     grad_inputs = grad_inputs.reshape(rows, region, width)
     if by_share:
-        small = lax.all_gather(small, "seq")
         pieces = both_cores([total] + spread, small)
+        (mine,) = cat([[(v, 0, 8) for v in [small] + [swap(small, "seq", j) for j in others]]], after=[])
         gq, gk, gv, gwo, gwu, gwd = unpack(at, pieces, late)
-        g1, s1, g2, s2, gbd, gbu = (v[0] for v in totals(small))
+        g1, s1, g2, s2, gbd, gbu = (v[0] for v in totals(at, mine, swap(mine, "seq", 1)))
         return out, grad_inputs, g1, s1, gq, gk, gv, gwo, g2, s2, gwu, gbu, gwd, gbd
 
     gwu, gwd = hidden_grads

time: 164 us -> 161 us (0.982)
  blocking collectives: 9.21 us -> 0 us
  waiting for transfers between devices: 31.7 us -> 35.1 us
  starting transfers between devices: 36.6 us -> 39.3 us
    all_gather x1 -> x0, blocking collectives: 9.21 us -> none  [on_device(): small = lax.all_gather(small, 'seq')]
    ppermute x33 -> x37, waiting for transfers between devices: 31.7 us -> 35.1 us  [swap(): lax.ppermute(v, axis, [(i, i ^ mask) for i in range(lax.axis_size(axis))])]
    ppermute x33 -> x37, starting transfers between devices: 30.5 us -> 33.1 us  [swap(): lax.ppermute(v, axis, [(i, i ^ mask) for i in range(lax.axis_size(axis))])]
    pallas_call x19 -> x20, Pallas kernels: 84 us -> 84.5 us  [call(): return lambda *operands: kernel(*operands, *after)]
  transfers between devices with their start and end apart: 36 -> 40, of which waited for: 14 -> 14; matrix products, arithmetic and copies ran while one was open for 0% -> 0% of each run, Pallas kernels for 30% -> 30%
where the time goes in v5:
time: 161 us
  Pallas kernels  84.5 us (52%)
  starting transfers between devices  39.3 us (24%)
  waiting for transfers between devices  35.1 us (22%)
    pallas_call x20, Pallas kernels, call(): return lambda *operands: kernel(*operands, *after)  84.5 us
    ppermute x37, waiting for transfers between devices, swap(): lax.ppermute(v, axis, [(i, i ^ mask) for i in range(lax.axis_size(axis))])  35.1 us
    ppermute x37, starting transfers between devices, swap(): lax.ppermute(v, axis, [(i, i ^ mask) for i in range(lax.axis_size(axis))])  33.1 us
    ppermute x3, starting transfers between devices, along_z(): return (lax.ppermute(both, ('seq', 'head'), by_core), swap(one, 'head', 3))  6.15 us
  transfers between devices with their start and end apart: 40, of which 14 were waited for; matrix products, arithmetic and copies ran while one was open for 0% of the time, Pallas kernels for 30%

profile of v5, /device:TPU:0, one launch (start us, length us, event | category | flops | bytes accessed | tf_op | source)
XLA Modules:
  0.0 161.0 jit_solution(7859908208232478754)
XLA Ops:
  0.8 1.4 shard_map.264
  2.2 3.1 %collective-permute-start = (f32[384,128]{1,0:T(8,128)S(1)}, f32[384,128]{1,0:T(8,128)S(1)}, u32[]{:S(2)}, u32[]{:S(2)}) collective-permute-start(f32[384,128]{1,0:T(8,128)S(1)} %get-tuple-element.74), channel_id=1, source_target_pairs={{0,1},{1,0},{2,3},{3,2},{4,6},{5,7},{6,4},{7,5},{8,9},{9,8},{10,11... | collective-permute-start | bytes 589832 | tf_op jit(solution)/shard_map/ppermute | solution.py:1011
  5.3 2.5 %collective-permute-start.1 = (f32[192,128]{1,0:T(8,128)S(1)}, f32[192,128]{1,0:T(8,128)S(1)}, u32[]{:S(2)}, u32[]{:S(2)}) collective-permute-start(f32[192,128]{1,0:T(8,128)S(1)} %get-tuple-element.75), channel_id=1, source_target_pairs={{0,3},{1,2},{2,1},{3,0},{4,7},{5,6},{6,5},{7,4},{8,11},{9,10},{10,... | collective-permute-start | bytes 294920 | tf_op jit(solution)/shard_map/ppermute | solution.py:1005
  7.8 2.8 %shard_map.263 = (bf16[1792,512]{1,0:T(8,128)(2,1)S(1)}, f32[2,8,896]{2,1,0:T(8,128)}, f32[2,8,768]{2,1,0:T(8,128)S(1)}, f32[2,8,128]{2,1,0:T(8,128)S(1)}) custom-call(s32[2,896]{1,0:T(2,128)S(1)} %copy-done.10, s32[2,896]{1,0:T(2,128)S(1)} %copy-done.10, s32[2,896]{1,0:T(2,128)S(1)} %copy-done.11, bf16[1792,512]{1,0:T(8,128)(2,1)S(1)} %bitcast.23, ...), custom_call_target="tpu_custom_call" | custom-call | flops 4400000000 | bytes 14000000 | tf_op jit(solution)/shard_map/pallas_call | solution.py:91
  10.6 1.7 %shard_map.266 = (f32[168,512]{1,0:T(8,128)S(1)}, f32[88,512]{1,0:T(8,128)S(1)}, f32[256,512]{1,0:T(8,128)S(1)}, f32[128,512]{1,0:T(8,128)S(1)}) custom-call(s32[3]{0:T(128)S(1)} %pad_add_fusion.refs_0_, bf16[512,512]{1,0:T(8,128)(2,1)} %refs_8_.1, bf16[128,512]{1,0:T(8,128)(2,1)} %refs_9_.1, f32[1,512]{1,0:T(1,128)} %bitcast.38, bf16[512,512]{1,0:T(8,128)(2,1)} %refs_11_.1, ...), custom_call_target="tpu_custom_call" | custom-call | flops 2200000000 | bytes 7000000 | tf_op jit(solution)/shard_map/pallas_call | solution.py:91
  12.3 0.7 collective-permute-start.6
  13.0 0.9 collective-permute-start.7
  14.5 1.6 collective-permute-start.2
  16.0 1.5 collective-permute-start.3
  18.0 8.2 %collective-permute-done.7.refs_1_.refs_16_ = f32[88,512]{1,0:T(8,128)S(1)} collective-permute-done((f32[88,512]{1,0:T(8,128)S(1)}, f32[88,512]{1,0:T(8,128)S(1)}, u32[]{:S(2)}, u32[]{:S(2)}) %collective-permute-start.7) | collective-permute-done | bytes 180256 | tf_op jit(solution)/shard_map/ppermute | solution.py:1005
  26.2 4.5 %collective-permute-done.3.refs_7_.refs_9_ = f32[592,128]{1,0:T(8,128)S(1)} collective-permute-done((f32[592,128]{1,0:T(8,128)S(1)}, f32[592,128]{1,0:T(8,128)S(1)}, u32[]{:S(2)}, u32[]{:S(2)}) %collective-permute-start.3) | collective-permute-done | bytes 303136 | tf_op jit(solution)/shard_map/ppermute | solution.py:1005
  31.2 2.3 %collective-permute-start.14 = (f32[256,512]{1,0:T(8,128)S(1)}, f32[256,512]{1,0:T(8,128)S(1)}, u32[]{:S(2)}, u32[]{:S(2)}) collective-permute-start(f32[256,512]{1,0:T(8,128)S(1)} %get-tuple-element.86), channel_id=1, source_target_pairs={{0,1},{1,0},{2,3},{3,2},{4,6},{5,7},{6,4},{7,5},{8,9},{9,8},{10,11... | collective-permute-start | bytes 1572872 | tf_op jit(solution)/shard_map/ppermute | solution.py:1011
  33.5 4.1 %collective-permute-start.15 = (f32[128,512]{1,0:T(8,128)S(1)}, f32[128,512]{1,0:T(8,128)S(1)}, u32[]{:S(2)}, u32[]{:S(2)}) collective-permute-start(f32[128,512]{1,0:T(8,128)S(1)} %get-tuple-element.87), channel_id=1, source_target_pairs={{0,3},{1,2},{2,1},{3,0},{4,7},{5,6},{6,5},{7,4},{8,11},{9,10},{10,... | collective-permute-start | bytes 786440 | tf_op jit(solution)/shard_map/ppermute | solution.py:1005
  37.7 1.0 collective-permute-start.11
  38.6 1.1 collective-permute-start.12
  39.7 1.4 collective-permute-start.13
  41.2 0.8 shard_map.268
  42.2 13.9 %shard_map.269 = (bf16[1792,1536]{1,0:T(8,128)(2,1)S(1)}, bf16[4,14,256,128]{3,2,1,0:T(8,128)(2,1)S(1)}, f32[4,14,8,128]{3,2,1,0:T(8,128)S(1)}, bf16[1792,512]{1...) custom-call(s32[3]{0:T(128)S(1)} %pad_add_fusion.refs_0_, ...), custom_call_target="tpu_custom_call" | custom-call | flops 22000001024 | bytes 70000000 | tf_op jit(solution)/shard_map/pallas_call | solution.py:91
  56.2 1.0 collective-permute-start.17
  57.2 1.1 collective-permute-start.18
  58.4 2.9 %collective-permute-done.13.refs_3_ = f32[240,512]{1,0:T(8,128)S(1)} collective-permute-done((f32[240,512]{1,0:T(8,128)S(1)}, f32[240,512]{1,0:T(8,128)S(1)}, u32[]{:S(2)}, u32[]{:S(2)}) %collective-permute-start.13) | collective-permute-done | bytes 491552 | tf_op jit(solution)/shard_map/ppermute | solution.py:1005
  61.6 6.6 %collective-permute-done.17.refs_2_ = f32[192,512]{1,0:T(8,128)S(1)} collective-permute-done((f32[192,512]{1,0:T(8,128)S(1)}, f32[192,512]{1,0:T(8,128)S(1)}, u32[]{:S(2)}, u32[]{:S(2)}) %collective-permute-start.17) | collective-permute-done | bytes 393248 | tf_op jit(solution)/shard_map/ppermute | solution.py:1005
  68.1 0.9 collective-permute-done.18.refs_3_
  69.2 3.4 %collective-permute-done.19.refs_15_ = f32[768,512]{1,0:T(8,128)S(1)} collective-permute-done((f32[768,512]{1,0:T(8,128)S(1)}, f32[768,512]{1,0:T(8,128)S(1)}, u32[]{:S(2)}, u32[]{:S(2)}) %collective-permute-start.19) | collective-permute-done | bytes 1572896 | tf_op jit(solution)/shard_map/ppermute | solution.py:1005
  72.7 31.1 %shard_map.273 = (bf16[1792,512]{1,0:T(8,128)(2,1)}, f32[1792,512]{1,0:T(8,128)}, bf16[1792,512]{1,0:T(8,128)(2,1)S(1)}, f32[128,512]{1,0:T(8,128)S(1)}, f32[1,5...) custom-call(s32[3]{0:T(128)S(1)} %pad_add_fusion.refs_0_, ...), custom_call_target="tpu_custom_call" | custom-call | flops 41799999488 | bytes 133000000 | tf_op jit(solution)/shard_map/pallas_call | solution.py:91
  103.9 5.7 %shard_map.274 = (bf16[1792,1536]{1,0:T(8,128)(2,1)S(1)}, f32[2,1,1536]{2,1,0:T(1,128)S(1)}, f32[4,64,512]{2,1,0:T(8,128)S(1)}, f32[4,64,512]{2,1,0:T(8,128)S(1)}) custom-call(s32[3]{0:T(128)S(1)} %pad_add_fusion.refs_0_, bf16[1792,1536]{1,0:T(8,128)(2,1)S(1)} %get-tuple-element.92.refs_1_, bf16[1792,512]{1,0:T(8,128)(2,1)S(1)} %get-tuple-element.93.refs_2_, ...), custom_call_target="tpu_custom_call" | custom-call | flops 6600000000 | bytes 21000000 | tf_op jit(solution)/shard_map/pallas_call | solution.py:91
  110.1 1.5 collective-permute-done.23.refs_4_
  111.7 0.8 shard_map.276
  112.4 0.9 collective-permute-start.24
  113.3 1.5 collective-permute-start.25
  114.8 1.2 collective-permute-start.26
  116.0 13.5 %shard_map.275 = (bf16[1792,1536]{1,0:T(8,128)(2,1)S(1)}, f32[2,1,1536]{2,1,0:T(1,128)S(1)}) custom-call(s32[3]{0:T(128)S(1)} %pad_add_fusion.refs_0_, bf16[1792,1536]{1,0:T(8,128)(2,1)S(1)} %get-tuple-element.92.refs_1_, bf16[1792,512]{1,0:T(8,128)(2,1)S(1)} %get-tuple-element.93.refs_2_, ...), custom_call_target="tpu_custom_call", output_to_operand_aliasing={{0}: (7, {}), {1}: (8, {})} | custom-call | flops 19800000512 | bytes 63000000 | tf_op jit(solution)/shard_map/pallas_call | solution.py:91
  129.5 0.9 collective-permute-start.20
  130.3 1.5 collective-permute-start.21
  131.9 1.0 collective-permute-done.25.refs_2_
  133.0 1.6 collective-permute-start.27
  134.6 1.5 collective-permute-start.33
  136.5 1.5 collective-permute-start.35
  138.2 1.2 collective-permute-done.28.refs_3_
  139.4 0.7 copy-done
  140.1 8.8 %shard_map.279 = (f32[1792,512]{1,0:T(8,128)}, f32[8,512]{1,0:T(8,128)S(1)}, f32[512,384]{1,0:T(8,128)S(1)}) custom-call(s32[3]{0:T(128)S(1)} %pad_add_fusion.refs_0_, f32[8,16,128]{2,1,0:T(8,128)S(1)} %get-tuple-element.91.refs_1_, f32[8,1536]{1,0:T(8,128)S(1)} %shard_map.278.refs_2_, f32[8,1536]{1,0:T(8,128)S(1)} %collective-permute-done.28.refs_3_, ...), custom_call_target="tpu_custom_call" | custom-call | flops 2200000000 | bytes 7000000 | tf_op jit(solution)/shard_map/pallas_call | solution.py:91
  148.9 1.5 collective-permute-start.29
  150.9 1.5 collective-permute-start.31
  152.4 2.0 %collective-permute-done.35.refs_4_ = f32[192,512]{1,0:T(8,128)S(1)} collective-permute-done((f32[192,512]{1,0:T(8,128)S(1)}, f32[192,512]{1,0:T(8,128)S(1)}, u32[]{:S(2)}, u32[]{:S(2)}) %collective-permute-start.35) | collective-permute-done | bytes 393248 | tf_op jit(solution)/shard_map/ppermute | solution.py:1005
  155.0 0.6 collective-permute-done.31.refs_3_
  155.5 1.8 %collective-permute-done.32.refs_2_ = f32[32,512]{1,0:T(8,128)S(1)} collective-permute-done((f32[32,512]{1,0:T(8,128)S(1)}, f32[32,512]{1,0:T(8,128)S(1)}, u32[]{:S(2)}, u32[]{:S(2)}) %collective-permute-start.32) | collective-permute-done | bytes 65568 | tf_op jit(solution)/shard_map/ppermute | solution.py:1005
  157.3 1.2 shard_map.281
  158.5 2.5 %shard_map.282 = (f32[512,128]{1,0:T(8,128)}, f32[512,128]{1,0:T(8,128)}, f32[512,128]{1,0:T(8,128)}, f32[128,512]{1,0:T(8,128)}, f32[512,512]{1,0:T(8,128)}, /*index=5*/f32[512,512]{1,0:T(8,128)}) custom-call(s32[3]{0:T(128)S(1)} %pad_add_fusion.refs_0_, f32[192,512]{1,0:T(8,128)S(1)} %shard_map.277.refs_1_, ...), custom_call_target="tpu_custom_call" | custom-call | flops 2200000000 | bytes 7000000 | tf_op jit(solution)/shard_map/pallas_call | solution.py:91
  (88 shorter events, 4.8 us)
Async XLA Ops:
  2.2 12.3 %collective-permute-start = (f32[384,128]{1,0:T(8,128)S(1)}, f32[384,128]{1,0:T(8,128)S(1)}, u32[]{:S(2)}, u32[]{:S(2)}) collective-permute-start(f32[384,128]{1,0:T(8,128)S(1)} %get-tuple-element.74), channel_id=1, source_target_pairs={{0,1},{1,0},{2,3},{3,2},{4,6},{5,7},{6,4},{7,5},{8,9},{9,8},{10,11... | collective-permute-start | bytes 589832 | tf_op jit(solution)/shard_map/ppermute | solution.py:1011
  5.3 9.2 %collective-permute-start.1 = (f32[192,128]{1,0:T(8,128)S(1)}, f32[192,128]{1,0:T(8,128)S(1)}, u32[]{:S(2)}, u32[]{:S(2)}) collective-permute-start(f32[192,128]{1,0:T(8,128)S(1)} %get-tuple-element.75), channel_id=1, source_target_pairs={{0,3},{1,2},{2,1},{3,0},{4,7},{5,6},{6,5},{7,4},{8,11},{9,10},{10,... | collective-permute-start | bytes 294920 | tf_op jit(solution)/shard_map/ppermute | solution.py:1005
  12.3 13.9 %collective-permute-start.6 = (f32[168,512]{1,0:T(8,128)S(1)}, f32[168,512]{1,0:T(8,128)S(1)}, u32[]{:S(2)}, u32[]{:S(2)}) collective-permute-start(f32[168,512]{1,0:T(8,128)S(1)} %get-tuple-element.78), channel_id=1, source_target_pairs={{0,1},{1,0},{2,3},{3,2},{4,6},{5,7},{6,4},{7,5},{8,9},{9,8},{10,11... | collective-permute-start | bytes 1032200 | tf_op jit(solution)/shard_map/ppermute | solution.py:1011
  13.0 13.2 %collective-permute-start.7 = (f32[88,512]{1,0:T(8,128)S(1)}, f32[88,512]{1,0:T(8,128)S(1)}, u32[]{:S(2)}, u32[]{:S(2)}) collective-permute-start(f32[88,512]{1,0:T(8,128)S(1)} %get-tuple-element.79), channel_id=1, source_target_pairs={{0,3},{1,2},{2,1},{3,0},{4,7},{5,6},{6,5},{7,4},{8,11},{9,10},{10,... | collective-permute-start | bytes 540680 | tf_op jit(solution)/shard_map/ppermute | solution.py:1005
  14.5 11.8 %collective-permute-start.2 = (f32[592,128]{1,0:T(8,128)S(1)}, f32[592,128]{1,0:T(8,128)S(1)}, u32[]{:S(2)}, u32[]{:S(2)}) collective-permute-start(f32[592,128]{1,0:T(8,128)S(1)} %shard_map.265.refs_5_.refs_7_), channel_id=1, source_target_pairs={{0,8},{4,12},{8,0},{12,4},{16,24},{20,28},{24,16},{28,20},{1,9},{5... | collective-permute-start | bytes 909320 | tf_op jit(solution)/shard_map/ppermute | solution.py:1005
  16.0 14.7 %collective-permute-start.3 = (f32[592,128]{1,0:T(8,128)S(1)}, f32[592,128]{1,0:T(8,128)S(1)}, u32[]{:S(2)}, u32[]{:S(2)}) collective-permute-start(f32[592,128]{1,0:T(8,128)S(1)} %shard_map.265.refs_5_.refs_7_), channel_id=1, source_target_pairs={{0,16},{4,20},{8,24},{12,28},{16,0},{20,4},{24,8},{28,12},{1,17},{... | collective-permute-start | bytes 909320 | tf_op jit(solution)/shard_map/ppermute | solution.py:1005
  17.5 13.2 %collective-permute-start.4 = (f32[592,128]{1,0:T(8,128)S(1)}, f32[592,128]{1,0:T(8,128)S(1)}, u32[]{:S(2)}, u32[]{:S(2)}) collective-permute-start(f32[592,128]{1,0:T(8,128)S(1)} %shard_map.265.refs_5_.refs_7_), channel_id=1, source_target_pairs={{0,24},{4,28},{8,16},{12,20},{16,8},{20,12},{24,0},{28,4},{1,25},{... | collective-permute-start | bytes 909320 | tf_op jit(solution)/shard_map/ppermute | solution.py:1005
  26.2 7.4 %collective-permute-start.5 = (f32[592,128]{1,0:T(8,128)S(1)}, f32[592,128]{1,0:T(8,128)S(1)}, u32[]{:S(2)}, u32[]{:S(2)}) collective-permute-start(f32[592,128]{1,0:T(8,128)S(1)} %shard_map.265.refs_5_.refs_7_), channel_id=1, source_target_pairs={{0,4},{4,0},{8,12},{12,8},{16,20},{20,16},{24,28},{28,24},{1,5},{5... | collective-permute-start | bytes 909320 | tf_op jit(solution)/shard_map/ppermute | solution.py:1005
  30.7 7.0 %collective-permute-start.10 = (f32[592,128]{1,0:T(8,128)S(1)}, f32[592,128]{1,0:T(8,128)S(1)}, u32[]{:S(2)}, u32[]{:S(2)}) collective-permute-start(f32[592,128]{1,0:T(8,128)S(1)} %collective-permute-done.4.refs_8_.refs_10_), channel_id=1, source_target_pairs={{0,4},{4,0},{8,12},{12,8},{16,20},{20,16},{24,28},{28,24},{1,5},{5... | collective-permute-start | bytes 909320 | tf_op jit(solution)/shard_map/ppermute | solution.py:1005
  30.7 7.9 %collective-permute-start.8 = (f32[592,128]{1,0:T(8,128)S(1)}, f32[592,128]{1,0:T(8,128)S(1)}, u32[]{:S(2)}, u32[]{:S(2)}) collective-permute-start(f32[592,128]{1,0:T(8,128)S(1)} %collective-permute-done.2.refs_6_.refs_8_), channel_id=1, source_target_pairs={{0,4},{4,0},{8,12},{12,8},{16,20},{20,16},{24,28},{28,24},{1,5},{5... | collective-permute-start | bytes 909320 | tf_op jit(solution)/shard_map/ppermute | solution.py:1005
  31.2 8.5 %collective-permute-start.9 = (f32[592,128]{1,0:T(8,128)S(1)}, f32[592,128]{1,0:T(8,128)S(1)}, u32[]{:S(2)}, u32[]{:S(2)}) collective-permute-start(f32[592,128]{1,0:T(8,128)S(1)} %collective-permute-done.3.refs_7_.refs_9_), channel_id=1, source_target_pairs={{0,4},{4,0},{8,12},{12,8},{16,20},{20,16},{24,28},{28,24},{1,5},{5... | collective-permute-start | bytes 909320 | tf_op jit(solution)/shard_map/ppermute | solution.py:1005
  31.2 24.9 %collective-permute-start.14 = (f32[256,512]{1,0:T(8,128)S(1)}, f32[256,512]{1,0:T(8,128)S(1)}, u32[]{:S(2)}, u32[]{:S(2)}) collective-permute-start(f32[256,512]{1,0:T(8,128)S(1)} %get-tuple-element.86), channel_id=1, source_target_pairs={{0,1},{1,0},{2,3},{3,2},{4,6},{5,7},{6,4},{7,5},{8,9},{9,8},{10,11... | collective-permute-start | bytes 1572872 | tf_op jit(solution)/shard_map/ppermute | solution.py:1011
  33.5 22.6 %collective-permute-start.15 = (f32[128,512]{1,0:T(8,128)S(1)}, f32[128,512]{1,0:T(8,128)S(1)}, u32[]{:S(2)}, u32[]{:S(2)}) collective-permute-start(f32[128,512]{1,0:T(8,128)S(1)} %get-tuple-element.87), channel_id=1, source_target_pairs={{0,3},{1,2},{2,1},{3,0},{4,7},{5,6},{6,5},{7,4},{8,11},{9,10},{10,... | collective-permute-start | bytes 786440 | tf_op jit(solution)/shard_map/ppermute | solution.py:1005
  37.7 20.6 %collective-permute-start.11 = (f32[240,512]{1,0:T(8,128)S(1)}, f32[240,512]{1,0:T(8,128)S(1)}, u32[]{:S(2)}, u32[]{:S(2)}) collective-permute-start(f32[240,512]{1,0:T(8,128)S(1)} %shard_map.267.refs_0_), channel_id=1, source_target_pairs={{0,8},{4,12},{8,0},{12,4},{16,24},{20,28},{24,16},{28,20},{1,9},{5... | collective-permute-start | bytes 1474568 | tf_op jit(solution)/shard_map/ppermute | solution.py:1005
  38.6 19.8 %collective-permute-start.12 = (f32[240,512]{1,0:T(8,128)S(1)}, f32[240,512]{1,0:T(8,128)S(1)}, u32[]{:S(2)}, u32[]{:S(2)}) collective-permute-start(f32[240,512]{1,0:T(8,128)S(1)} %shard_map.267.refs_0_), channel_id=1, source_target_pairs={{0,16},{4,20},{8,24},{12,28},{16,0},{20,4},{24,8},{28,12},{1,17},{... | collective-permute-start | bytes 1474568 | tf_op jit(solution)/shard_map/ppermute | solution.py:1005
  39.7 21.5 %collective-permute-start.13 = (f32[240,512]{1,0:T(8,128)S(1)}, f32[240,512]{1,0:T(8,128)S(1)}, u32[]{:S(2)}, u32[]{:S(2)}) collective-permute-start(f32[240,512]{1,0:T(8,128)S(1)} %shard_map.267.refs_0_), channel_id=1, source_target_pairs={{0,24},{4,28},{8,16},{12,20},{16,8},{20,12},{24,0},{28,4},{1,25},{... | collective-permute-start | bytes 1474568 | tf_op jit(solution)/shard_map/ppermute | solution.py:1005
  56.2 12.0 %collective-permute-start.17 = (f32[192,512]{1,0:T(8,128)S(1)}, f32[192,512]{1,0:T(8,128)S(1)}, u32[]{:S(2)}, u32[]{:S(2)}) collective-permute-start(f32[192,512]{1,0:T(8,128)S(1)} %get-tuple-element.88.refs_5_.refs_0_), channel_id=1, source_target_pairs={{0,8},{4,12},{8,0},{12,4},{16,24},{20,28},{24,16},{28,20},{1,9},{5... | collective-permute-start | bytes 1179656 | tf_op jit(solution)/shard_map/ppermute | solution.py:1005
  57.2 11.8 %collective-permute-start.18 = (f32[192,512]{1,0:T(8,128)S(1)}, f32[192,512]{1,0:T(8,128)S(1)}, u32[]{:S(2)}, u32[]{:S(2)}) collective-permute-start(f32[192,512]{1,0:T(8,128)S(1)} %get-tuple-element.89.refs_1_), channel_id=1, source_target_pairs={{0,16},{4,20},{8,24},{12,28},{16,0},{20,4},{24,8},{28,12},{1,17},{... | collective-permute-start | bytes 1179656 | tf_op jit(solution)/shard_map/ppermute | solution.py:1005
  61.4 11.2 %copy-start.3 = (bf16[2,896,512]{2,1,0:T(8,128)(2,1)S(1)}, bf16[2,896,512]{2,1,0:T(8,128)(2,1)}, u32[]{:S(2)}) copy-start(bf16[2,896,512]{2,1,0:T(8,128)(2,1)} %param.31) | copy-start | bytes 5505028
  61.4 11.2 %copy-start.4 = (bf16[512,512]{1,0:T(8,128)(2,1)S(1)}, bf16[512,512]{1,0:T(8,128)(2,1)}, u32[]{:S(2)}) copy-start(bf16[512,512]{1,0:T(8,128)(2,1)} %refs_8_.1) | copy-start | bytes 1572868
  61.4 11.2 %copy-start.5 = (bf16[512,512]{1,0:T(8,128)(2,1)S(1)}, bf16[512,512]{1,0:T(8,128)(2,1)}, u32[]{:S(2)}) copy-start(bf16[512,512]{1,0:T(8,128)(2,1)} %refs_11_.1) | copy-start | bytes 1572868
  61.4 11.2 %copy-start.9 = (bf16[128,512]{1,0:T(8,128)(2,1)S(1)}, bf16[128,512]{1,0:T(8,128)(2,1)}, u32[]{:S(2)}) copy-start(bf16[128,512]{1,0:T(8,128)(2,1)} %refs_9_.1) | copy-start | bytes 393220
  61.5 11.2 %copy-start.13 = (f32[512]{0:T(512)S(1)}, f32[512]{0:T(512)}, u32[]{:S(2)}) copy-start(f32[512]{0:T(512)} %param.25) | copy-start | bytes 6148
  61.5 11.2 %copy-start.14 = (f32[512]{0:T(512)S(1)}, f32[512]{0:T(512)}, u32[]{:S(2)}) copy-start(f32[512]{0:T(512)} %param.26) | copy-start | bytes 6148
  61.5 11.2 %copy-start.15 = (f32[512]{0:T(512)S(1)}, f32[512]{0:T(512)}, u32[]{:S(2)}) copy-start(f32[512]{0:T(512)} %param.30) | copy-start | bytes 6148
  61.5 11.2 %copy-start.16 = (f32[512]{0:T(512)S(1)}, f32[512]{0:T(512)}, u32[]{:S(2)}) copy-start(f32[512]{0:T(512)} %param.28) | copy-start | bytes 6148
  61.5 11.1 %collective-permute-start.16 = (f32[968,512]{1,0:T(8,128)S(1)}, f32[968,512]{1,0:T(8,128)S(1)}, u32[]{:S(2)}, u32[]{:S(2)}) collective-permute-start(f32[968,512]{1,0:T(8,128)S(1)} %shard_map.271.refs_4_.refs_12_), channel_id=1, source_target_pairs={{0,4},{4,0},{8,12},{12,8},{16,20},{20,16},{24,28},{28,24},{1,5},{5... | collective-permute-start | bytes 5947400 | tf_op jit(solution)/shard_map/ppermute | solution.py:1005
  69.2 3.5 %collective-permute-start.19 = (f32[768,512]{1,0:T(8,128)S(1)}, f32[768,512]{1,0:T(8,128)S(1)}, u32[]{:S(2)}, u32[]{:S(2)}) collective-permute-start(f32[768,512]{1,0:T(8,128)S(1)} %shard_map.272.refs_14_), channel_id=1, source_target_pairs={{0,4},{4,0},{8,12},{12,8},{16,20},{20,16},{24,28},{28,24},{1,5},{5... | collective-permute-start | bytes 4718600 | tf_op jit(solution)/shard_map/ppermute | solution.py:1005
  103.8 7.9 %collective-permute-start.22 = (f32[4,128,512]{2,1,0:T(8,128)S(1)}, f32[4,128,512]{2,1,0:T(8,128)S(1)}, u32[]{:S(2)}, u32[]{:S(2)}) collective-permute-start(f32[4,128,512]{2,1,0:T(8,128)S(1)} %get-tuple-element.103), channel_id=1, source_target_pairs={{0,4},{4,0},{8,12},{12,8},{16,20},{20,16},{24,28},{28,24},{1,5},{5... | collective-permute-start | bytes 3145736 | tf_op jit(solution)/shard_map/ppermute | solution.py:1005
  109.7 2.0 %collective-permute-start.23 = (f32[4,64,512]{2,1,0:T(8,128)S(1)}, f32[4,64,512]{2,1,0:T(8,128)S(1)}, u32[]{:S(2)}, u32[]{:S(2)}) collective-permute-start(f32[4,64,512]{2,1,0:T(8,128)S(1)} %get-tuple-element.104), channel_id=1, source_target_pairs={{0,4},{4,0},{8,12},{12,8},{16,20},{20,16},{24,28},{28,24},{1,5},{5... | collective-permute-start | bytes 1572872 | tf_op jit(solution)/shard_map/ppermute | solution.py:1005
  112.4 19.4 %collective-permute-start.24 = (f32[192,512]{1,0:T(8,128)S(1)}, f32[192,512]{1,0:T(8,128)S(1)}, u32[]{:S(2)}, u32[]{:S(2)}) collective-permute-start(f32[192,512]{1,0:T(8,128)S(1)} %get-tuple-element.106), channel_id=1, source_target_pairs={{0,8},{4,12},{8,0},{12,4},{16,24},{20,28},{24,16},{28,20},{1,9},{5... | collective-permute-start | bytes 1179656 | tf_op jit(solution)/shard_map/ppermute | solution.py:1005
  113.3 19.6 %collective-permute-start.25 = (f32[192,512]{1,0:T(8,128)S(1)}, f32[192,512]{1,0:T(8,128)S(1)}, u32[]{:S(2)}, u32[]{:S(2)}) collective-permute-start(f32[192,512]{1,0:T(8,128)S(1)} %get-tuple-element.107), channel_id=1, source_target_pairs={{0,16},{4,20},{8,24},{12,28},{16,0},{20,4},{24,8},{28,12},{1,17},{... | collective-permute-start | bytes 1179656 | tf_op jit(solution)/shard_map/ppermute | solution.py:1005
  114.8 18.1 %collective-permute-start.26 = (f32[192,512]{1,0:T(8,128)S(1)}, f32[192,512]{1,0:T(8,128)S(1)}, u32[]{:S(2)}, u32[]{:S(2)}) collective-permute-start(f32[192,512]{1,0:T(8,128)S(1)} %get-tuple-element.108), channel_id=1, source_target_pairs={{0,24},{4,28},{8,16},{12,20},{16,8},{20,12},{24,0},{28,4},{1,25},{... | collective-permute-start | bytes 1179656 | tf_op jit(solution)/shard_map/ppermute | solution.py:1005
  129.5 7.1 %collective-permute-start.20 = (f32[2,1536]{1,0:T(2,128)S(1)}, f32[2,1536]{1,0:T(2,128)S(1)}, u32[]{:S(2)}, u32[]{:S(2)}) collective-permute-start(f32[2,1536]{1,0:T(2,128)S(1)} %bitcast.26), channel_id=1, source_target_pairs={{0,8},{4,12},{8,0},{12,4},{16,24},{20,28},{24,16},{28,20},{1,9},{5... | collective-permute-start | bytes 36872 | tf_op jit(solution)/shard_map/ppermute | solution.py:1005
  130.3 7.7 %collective-permute-start.21 = (f32[2,1536]{1,0:T(2,128)S(1)}, f32[2,1536]{1,0:T(2,128)S(1)}, u32[]{:S(2)}, u32[]{:S(2)}) collective-permute-start(f32[2,1536]{1,0:T(2,128)S(1)} %bitcast.27), channel_id=1, source_target_pairs={{0,16},{4,20},{8,24},{12,28},{16,0},{20,4},{24,8},{28,12},{1,17},{... | collective-permute-start | bytes 36872 | tf_op jit(solution)/shard_map/ppermute | solution.py:1005
  133.0 5.1 %collective-permute-start.27 = (f32[2,1536]{1,0:T(2,128)S(1)}, f32[2,1536]{1,0:T(2,128)S(1)}, u32[]{:S(2)}, u32[]{:S(2)}) collective-permute-start(f32[2,1536]{1,0:T(2,128)S(1)} %bitcast.29), channel_id=1, source_target_pairs={{0,24},{4,28},{8,16},{12,20},{16,8},{20,12},{24,0},{28,4},{1,25},{... | collective-permute-start | bytes 36872 | tf_op jit(solution)/shard_map/ppermute | solution.py:1005
  134.6 16.3 %collective-permute-start.33 = (f32[192,512]{1,0:T(8,128)S(1)}, f32[192,512]{1,0:T(8,128)S(1)}, u32[]{:S(2)}, u32[]{:S(2)}) collective-permute-start(f32[192,512]{1,0:T(8,128)S(1)} %shard_map.277.refs_1_), channel_id=1, source_target_pairs={{0,8},{4,12},{8,0},{12,4},{16,24},{20,28},{24,16},{28,20},{1,9},{5... | collective-permute-start | bytes 1179656 | tf_op jit(solution)/shard_map/ppermute | solution.py:1005
  136.1 16.3 %collective-permute-start.34 = (f32[192,512]{1,0:T(8,128)S(1)}, f32[192,512]{1,0:T(8,128)S(1)}, u32[]{:S(2)}, u32[]{:S(2)}) collective-permute-start(f32[192,512]{1,0:T(8,128)S(1)} %shard_map.277.refs_1_), channel_id=1, source_target_pairs={{0,16},{4,20},{8,24},{12,28},{16,0},{20,4},{24,8},{28,12},{1,17},{... | collective-permute-start | bytes 1179656 | tf_op jit(solution)/shard_map/ppermute | solution.py:1005
  136.5 17.8 %collective-permute-start.35 = (f32[192,512]{1,0:T(8,128)S(1)}, f32[192,512]{1,0:T(8,128)S(1)}, u32[]{:S(2)}, u32[]{:S(2)}) collective-permute-start(f32[192,512]{1,0:T(8,128)S(1)} %shard_map.277.refs_1_), channel_id=1, source_target_pairs={{0,24},{4,28},{8,16},{12,20},{16,8},{20,12},{24,0},{28,4},{1,25},{... | collective-permute-start | bytes 1179656 | tf_op jit(solution)/shard_map/ppermute | solution.py:1005
  138.1 1.3 collective-permute-start.28
  148.9 5.5 %collective-permute-start.29 = (f32[8,512]{1,0:T(8,128)S(1)}, f32[8,512]{1,0:T(8,128)S(1)}, u32[]{:S(2)}, u32[]{:S(2)}) collective-permute-start(f32[8,512]{1,0:T(8,128)S(1)} %get-tuple-element.115.refs_0_), channel_id=1, source_target_pairs={{0,8},{4,12},{8,0},{12,4},{16,24},{20,28},{24,16},{28,20},{1,9},{5... | collective-permute-start | bytes 49160 | tf_op jit(solution)/shard_map/ppermute | solution.py:1005
  150.4 4.4 %collective-permute-start.30 = (f32[8,512]{1,0:T(8,128)S(1)}, f32[8,512]{1,0:T(8,128)S(1)}, u32[]{:S(2)}, u32[]{:S(2)}) collective-permute-start(f32[8,512]{1,0:T(8,128)S(1)} %get-tuple-element.115.refs_0_), channel_id=1, source_target_pairs={{0,16},{4,20},{8,24},{12,28},{16,0},{20,4},{24,8},{28,12},{1,17},{... | collective-permute-start | bytes 49160 | tf_op jit(solution)/shard_map/ppermute | solution.py:1005
  150.9 4.6 %collective-permute-start.31 = (f32[8,512]{1,0:T(8,128)S(1)}, f32[8,512]{1,0:T(8,128)S(1)}, u32[]{:S(2)}, u32[]{:S(2)}) collective-permute-start(f32[8,512]{1,0:T(8,128)S(1)} %get-tuple-element.115.refs_0_), channel_id=1, source_target_pairs={{0,24},{4,28},{8,16},{12,20},{16,8},{20,12},{24,0},{28,4},{1,25},{... | collective-permute-start | bytes 49160 | tf_op jit(solution)/shard_map/ppermute | solution.py:1005
  152.4 6.1 %collective-permute-start.36 = (f32[192,512]{1,0:T(8,128)S(1)}, f32[192,512]{1,0:T(8,128)S(1)}, u32[]{:S(2)}, u32[]{:S(2)}) collective-permute-start(f32[192,512]{1,0:T(8,128)S(1)} %shard_map.277.refs_1_), channel_id=1, source_target_pairs={{0,4},{4,0},{8,12},{12,8},{16,20},{20,16},{24,28},{28,24},{1,5},{5... | collective-permute-start | bytes 1179656 | tf_op jit(solution)/shard_map/ppermute | solution.py:1005
  154.4 4.1 %collective-permute-start.37 = (f32[192,512]{1,0:T(8,128)S(1)}, f32[192,512]{1,0:T(8,128)S(1)}, u32[]{:S(2)}, u32[]{:S(2)}) collective-permute-start(f32[192,512]{1,0:T(8,128)S(1)} %collective-permute-done.33.refs_2_), channel_id=1, source_target_pairs={{0,4},{4,0},{8,12},{12,8},{16,20},{20,16},{24,28},{28,24},{1,5},{5... | collective-permute-start | bytes 1179656 | tf_op jit(solution)/shard_map/ppermute | solution.py:1005
  154.4 4.1 %collective-permute-start.38 = (f32[192,512]{1,0:T(8,128)S(1)}, f32[192,512]{1,0:T(8,128)S(1)}, u32[]{:S(2)}, u32[]{:S(2)}) collective-permute-start(f32[192,512]{1,0:T(8,128)S(1)} %collective-permute-done.34.refs_3_), channel_id=1, source_target_pairs={{0,4},{4,0},{8,12},{12,8},{16,20},{20,16},{24,28},{28,24},{1,5},{5... | collective-permute-start | bytes 1179656 | tf_op jit(solution)/shard_map/ppermute | solution.py:1005
  154.9 3.6 %collective-permute-start.39 = (f32[192,512]{1,0:T(8,128)S(1)}, f32[192,512]{1,0:T(8,128)S(1)}, u32[]{:S(2)}, u32[]{:S(2)}) collective-permute-start(f32[192,512]{1,0:T(8,128)S(1)} %collective-permute-done.35.refs_4_), channel_id=1, source_target_pairs={{0,4},{4,0},{8,12},{12,8},{16,20},{20,16},{24,28},{28,24},{1,5},{5... | collective-permute-start | bytes 1179656 | tf_op jit(solution)/shard_map/ppermute | solution.py:1005
  155.5 1.8 %collective-permute-start.32 = (f32[32,512]{1,0:T(8,128)S(1)}, f32[32,512]{1,0:T(8,128)S(1)}, u32[]{:S(2)}, u32[]{:S(2)}) collective-permute-start(f32[32,512]{1,0:T(8,128)S(1)} %shard_map.280.refs_1_), channel_id=1, source_target_pairs={{0,4},{4,0},{8,12},{12,8},{16,20},{20,16},{24,28},{28,24},{1,5},{5... | collective-permute-start | bytes 196616 | tf_op jit(solution)/shard_map/ppermute | solution.py:1005
  (9 other events, 39.9 us)

commit v6 on v5

--- a/solution.py
+++ b/solution.py
@@ -581,6 +581,14 @@
         a_s[j, :, c] = a
         du_s[j, :, c] = du
     y, dn = finish(halves_of - 1, a, du, y, dn)
+    group = at_s[2]
+    du = du_s[group]
+    gwd_ref[...] += tn(a_s[group], gm)
+    gwu_ref[...] += tn(h, du)
+    gbu = jnp.sum(du.astype(f32), axis=0, keepdims=True)
+    gbu_ref[...] += gbu
+    if gbu.shape[1] == small_ref.shape[1]:
+        small_ref[5:6] += gbu
     out_ref[...] = (mid + y + bd_ref[...]).astype(bf16)
     g = gm.astype(f32)
     small_ref[2:3] += jnp.sum(dn * xhat, axis=0, keepdims=True)
@@ -591,14 +599,6 @@
     gx = dmid.astype(bf16)
     do_ref[...] = nt(gx, wo_ref[...]).astype(bf16)
     gwo_ref[...] += tn(mine_ref[...], gx)
-    group = at_s[2]
-    du = du_s[group]
-    gwd_ref[...] += tn(a_s[group], gm)
-    gwu_ref[...] += tn(h, du)
-    gbu = jnp.sum(du.astype(f32), axis=0, keepdims=True)
-    gbu_ref[...] += gbu
-    if gbu.shape[1] == small_ref.shape[1]:
-        small_ref[5:6] += gbu
 
 
 def by_core(core, keep_ref, give_ref):

time: 161 us -> 161 us (level)
  no operation moved by 1% of the time
where the time goes in v6:
time: 161 us
  Pallas kernels  84.4 us (52%)
  starting transfers between devices  39.3 us (24%)
  waiting for transfers between devices  35.1 us (22%)
    pallas_call x20, Pallas kernels, call(): return lambda *operands: kernel(*operands, *after)  84.4 us
    ppermute x37, waiting for transfers between devices, swap(): lax.ppermute(v, axis, [(i, i ^ mask) for i in range(lax.axis_size(axis))])  35.1 us
    ppermute x37, starting transfers between devices, swap(): lax.ppermute(v, axis, [(i, i ^ mask) for i in range(lax.axis_size(axis))])  33.1 us
    ppermute x3, starting transfers between devices, along_z(): return (lax.ppermute(both, ('seq', 'head'), by_core), swap(one, 'head', 3))  6.15 us
  transfers between devices with their start and end apart: 40, of which 14 were waited for; matrix products, arithmetic and copies ran while one was open for 0% of the time, Pallas kernels for 30%

profile of v6, /device:TPU:0, one launch (start us, length us, event | category | flops | bytes accessed | tf_op | source)
XLA Modules:
  0.0 160.9 jit_solution(1238501881556209290)
XLA Ops:
  0.8 1.4 shard_map.264
  2.2 3.1 %collective-permute-start = (f32[384,128]{1,0:T(8,128)S(1)}, f32[384,128]{1,0:T(8,128)S(1)}, u32[]{:S(2)}, u32[]{:S(2)}) collective-permute-start(f32[384,128]{1,0:T(8,128)S(1)} %get-tuple-element.74), channel_id=1, source_target_pairs={{0,1},{1,0},{2,3},{3,2},{4,6},{5,7},{6,4},{7,5},{8,9},{9,8},{10,11... | collective-permute-start | bytes 589832 | tf_op jit(solution)/shard_map/ppermute | solution.py:1011
  5.3 2.5 %collective-permute-start.1 = (f32[192,128]{1,0:T(8,128)S(1)}, f32[192,128]{1,0:T(8,128)S(1)}, u32[]{:S(2)}, u32[]{:S(2)}) collective-permute-start(f32[192,128]{1,0:T(8,128)S(1)} %get-tuple-element.75), channel_id=1, source_target_pairs={{0,3},{1,2},{2,1},{3,0},{4,7},{5,6},{6,5},{7,4},{8,11},{9,10},{10,... | collective-permute-start | bytes 294920 | tf_op jit(solution)/shard_map/ppermute | solution.py:1005
  7.8 2.8 %shard_map.263 = (bf16[1792,512]{1,0:T(8,128)(2,1)S(1)}, f32[2,8,896]{2,1,0:T(8,128)}, f32[2,8,768]{2,1,0:T(8,128)S(1)}, f32[2,8,128]{2,1,0:T(8,128)S(1)}) custom-call(s32[2,896]{1,0:T(2,128)S(1)} %copy-done.10, s32[2,896]{1,0:T(2,128)S(1)} %copy-done.10, s32[2,896]{1,0:T(2,128)S(1)} %copy-done.11, bf16[1792,512]{1,0:T(8,128)(2,1)S(1)} %bitcast.23, ...), custom_call_target="tpu_custom_call" | custom-call | flops 4400000000 | bytes 14000000 | tf_op jit(solution)/shard_map/pallas_call | solution.py:91
  10.6 1.7 %shard_map.266 = (f32[168,512]{1,0:T(8,128)S(1)}, f32[88,512]{1,0:T(8,128)S(1)}, f32[256,512]{1,0:T(8,128)S(1)}, f32[128,512]{1,0:T(8,128)S(1)}) custom-call(s32[3]{0:T(128)S(1)} %pad_add_fusion.refs_0_, bf16[512,512]{1,0:T(8,128)(2,1)} %refs_8_.1, bf16[128,512]{1,0:T(8,128)(2,1)} %refs_9_.1, f32[1,512]{1,0:T(1,128)} %bitcast.38, bf16[512,512]{1,0:T(8,128)(2,1)} %refs_11_.1, ...), custom_call_target="tpu_custom_call" | custom-call | flops 2200000000 | bytes 7000000 | tf_op jit(solution)/shard_map/pallas_call | solution.py:91
  12.3 0.7 collective-permute-start.6
  13.0 0.9 collective-permute-start.7
  14.5 1.6 collective-permute-start.2
  16.0 1.5 collective-permute-start.3
  18.0 8.2 %collective-permute-done.7.refs_1_.refs_16_ = f32[88,512]{1,0:T(8,128)S(1)} collective-permute-done((f32[88,512]{1,0:T(8,128)S(1)}, f32[88,512]{1,0:T(8,128)S(1)}, u32[]{:S(2)}, u32[]{:S(2)}) %collective-permute-start.7) | collective-permute-done | bytes 180256 | tf_op jit(solution)/shard_map/ppermute | solution.py:1005
  26.2 4.5 %collective-permute-done.3.refs_7_.refs_9_ = f32[592,128]{1,0:T(8,128)S(1)} collective-permute-done((f32[592,128]{1,0:T(8,128)S(1)}, f32[592,128]{1,0:T(8,128)S(1)}, u32[]{:S(2)}, u32[]{:S(2)}) %collective-permute-start.3) | collective-permute-done | bytes 303136 | tf_op jit(solution)/shard_map/ppermute | solution.py:1005
  31.2 2.3 %collective-permute-start.14 = (f32[256,512]{1,0:T(8,128)S(1)}, f32[256,512]{1,0:T(8,128)S(1)}, u32[]{:S(2)}, u32[]{:S(2)}) collective-permute-start(f32[256,512]{1,0:T(8,128)S(1)} %get-tuple-element.86), channel_id=1, source_target_pairs={{0,1},{1,0},{2,3},{3,2},{4,6},{5,7},{6,4},{7,5},{8,9},{9,8},{10,11... | collective-permute-start | bytes 1572872 | tf_op jit(solution)/shard_map/ppermute | solution.py:1011
  33.5 4.1 %collective-permute-start.15 = (f32[128,512]{1,0:T(8,128)S(1)}, f32[128,512]{1,0:T(8,128)S(1)}, u32[]{:S(2)}, u32[]{:S(2)}) collective-permute-start(f32[128,512]{1,0:T(8,128)S(1)} %get-tuple-element.87), channel_id=1, source_target_pairs={{0,3},{1,2},{2,1},{3,0},{4,7},{5,6},{6,5},{7,4},{8,11},{9,10},{10,... | collective-permute-start | bytes 786440 | tf_op jit(solution)/shard_map/ppermute | solution.py:1005
  37.7 1.0 collective-permute-start.11
  38.6 1.1 collective-permute-start.12
  39.7 1.4 collective-permute-start.13
  41.2 0.8 shard_map.268
  42.2 13.9 %shard_map.269 = (bf16[1792,1536]{1,0:T(8,128)(2,1)S(1)}, bf16[4,14,256,128]{3,2,1,0:T(8,128)(2,1)S(1)}, f32[4,14,8,128]{3,2,1,0:T(8,128)S(1)}, bf16[1792,512]{1...) custom-call(s32[3]{0:T(128)S(1)} %pad_add_fusion.refs_0_, ...), custom_call_target="tpu_custom_call" | custom-call | flops 22000001024 | bytes 70000000 | tf_op jit(solution)/shard_map/pallas_call | solution.py:91
  56.2 1.0 collective-permute-start.17
  57.2 1.1 collective-permute-start.18
  58.4 2.9 %collective-permute-done.13.refs_3_ = f32[240,512]{1,0:T(8,128)S(1)} collective-permute-done((f32[240,512]{1,0:T(8,128)S(1)}, f32[240,512]{1,0:T(8,128)S(1)}, u32[]{:S(2)}, u32[]{:S(2)}) %collective-permute-start.13) | collective-permute-done | bytes 491552 | tf_op jit(solution)/shard_map/ppermute | solution.py:1005
  61.6 6.6 %collective-permute-done.17.refs_2_ = f32[192,512]{1,0:T(8,128)S(1)} collective-permute-done((f32[192,512]{1,0:T(8,128)S(1)}, f32[192,512]{1,0:T(8,128)S(1)}, u32[]{:S(2)}, u32[]{:S(2)}) %collective-permute-start.17) | collective-permute-done | bytes 393248 | tf_op jit(solution)/shard_map/ppermute | solution.py:1005
  68.1 0.9 collective-permute-done.18.refs_3_
  69.2 3.4 %collective-permute-done.19.refs_15_ = f32[768,512]{1,0:T(8,128)S(1)} collective-permute-done((f32[768,512]{1,0:T(8,128)S(1)}, f32[768,512]{1,0:T(8,128)S(1)}, u32[]{:S(2)}, u32[]{:S(2)}) %collective-permute-start.19) | collective-permute-done | bytes 1572896 | tf_op jit(solution)/shard_map/ppermute | solution.py:1005
  72.7 31.0 %shard_map.273 = (bf16[1792,512]{1,0:T(8,128)(2,1)}, f32[1792,512]{1,0:T(8,128)}, bf16[1792,512]{1,0:T(8,128)(2,1)S(1)}, f32[128,512]{1,0:T(8,128)S(1)}, f32[1,5...) custom-call(s32[3]{0:T(128)S(1)} %pad_add_fusion.refs_0_, ...), custom_call_target="tpu_custom_call" | custom-call | flops 41799999488 | bytes 133000000 | tf_op jit(solution)/shard_map/pallas_call | solution.py:91
  103.8 5.8 %shard_map.274 = (bf16[1792,1536]{1,0:T(8,128)(2,1)S(1)}, f32[2,1,1536]{2,1,0:T(1,128)S(1)}, f32[4,64,512]{2,1,0:T(8,128)S(1)}, f32[4,64,512]{2,1,0:T(8,128)S(1)}) custom-call(s32[3]{0:T(128)S(1)} %pad_add_fusion.refs_0_, bf16[1792,1536]{1,0:T(8,128)(2,1)S(1)} %get-tuple-element.92.refs_1_, bf16[1792,512]{1,0:T(8,128)(2,1)S(1)} %get-tuple-element.93.refs_2_, ...), custom_call_target="tpu_custom_call" | custom-call | flops 6600000000 | bytes 21000000 | tf_op jit(solution)/shard_map/pallas_call | solution.py:91
  110.0 1.5 collective-permute-done.23.refs_4_
  111.5 0.8 shard_map.276
  112.3 0.9 collective-permute-start.24
  113.2 1.5 collective-permute-start.25
  114.7 1.2 collective-permute-start.26
  115.9 13.5 %shard_map.275 = (bf16[1792,1536]{1,0:T(8,128)(2,1)S(1)}, f32[2,1,1536]{2,1,0:T(1,128)S(1)}) custom-call(s32[3]{0:T(128)S(1)} %pad_add_fusion.refs_0_, bf16[1792,1536]{1,0:T(8,128)(2,1)S(1)} %get-tuple-element.92.refs_1_, bf16[1792,512]{1,0:T(8,128)(2,1)S(1)} %get-tuple-element.93.refs_2_, ...), custom_call_target="tpu_custom_call", output_to_operand_aliasing={{0}: (7, {}), {1}: (8, {})} | custom-call | flops 19800000512 | bytes 63000000 | tf_op jit(solution)/shard_map/pallas_call | solution.py:91
  129.4 0.9 collective-permute-start.20
  130.2 1.5 collective-permute-start.21
  131.7 1.0 collective-permute-done.25.refs_2_
  132.9 1.6 collective-permute-start.27
  134.5 1.5 collective-permute-start.33
  136.4 1.5 collective-permute-start.35
  138.1 1.2 collective-permute-done.28.refs_3_
  139.3 0.7 copy-done
  140.0 8.8 %shard_map.279 = (f32[1792,512]{1,0:T(8,128)}, f32[8,512]{1,0:T(8,128)S(1)}, f32[512,384]{1,0:T(8,128)S(1)}) custom-call(s32[3]{0:T(128)S(1)} %pad_add_fusion.refs_0_, f32[8,16,128]{2,1,0:T(8,128)S(1)} %get-tuple-element.91.refs_1_, f32[8,1536]{1,0:T(8,128)S(1)} %shard_map.278.refs_2_, f32[8,1536]{1,0:T(8,128)S(1)} %collective-permute-done.28.refs_3_, ...), custom_call_target="tpu_custom_call" | custom-call | flops 2200000000 | bytes 7000000 | tf_op jit(solution)/shard_map/pallas_call | solution.py:91
  148.8 1.5 collective-permute-start.29
  150.8 1.5 collective-permute-start.31
  152.3 2.0 %collective-permute-done.35.refs_4_ = f32[192,512]{1,0:T(8,128)S(1)} collective-permute-done((f32[192,512]{1,0:T(8,128)S(1)}, f32[192,512]{1,0:T(8,128)S(1)}, u32[]{:S(2)}, u32[]{:S(2)}) %collective-permute-start.35) | collective-permute-done | bytes 393248 | tf_op jit(solution)/shard_map/ppermute | solution.py:1005
  154.8 0.6 collective-permute-done.31.refs_3_
  155.4 1.8 %collective-permute-done.32.refs_2_ = f32[32,512]{1,0:T(8,128)S(1)} collective-permute-done((f32[32,512]{1,0:T(8,128)S(1)}, f32[32,512]{1,0:T(8,128)S(1)}, u32[]{:S(2)}, u32[]{:S(2)}) %collective-permute-start.32) | collective-permute-done | bytes 65568 | tf_op jit(solution)/shard_map/ppermute | solution.py:1005
  157.2 1.2 shard_map.281
  158.4 2.5 %shard_map.282 = (f32[512,128]{1,0:T(8,128)}, f32[512,128]{1,0:T(8,128)}, f32[512,128]{1,0:T(8,128)}, f32[128,512]{1,0:T(8,128)}, f32[512,512]{1,0:T(8,128)}, /*index=5*/f32[512,512]{1,0:T(8,128)}) custom-call(s32[3]{0:T(128)S(1)} %pad_add_fusion.refs_0_, f32[192,512]{1,0:T(8,128)S(1)} %shard_map.277.refs_1_, ...), custom_call_target="tpu_custom_call" | custom-call | flops 2200000000 | bytes 7000000 | tf_op jit(solution)/shard_map/pallas_call | solution.py:91
  (88 shorter events, 4.8 us)
Async XLA Ops:
  2.2 12.3 %collective-permute-start = (f32[384,128]{1,0:T(8,128)S(1)}, f32[384,128]{1,0:T(8,128)S(1)}, u32[]{:S(2)}, u32[]{:S(2)}) collective-permute-start(f32[384,128]{1,0:T(8,128)S(1)} %get-tuple-element.74), channel_id=1, source_target_pairs={{0,1},{1,0},{2,3},{3,2},{4,6},{5,7},{6,4},{7,5},{8,9},{9,8},{10,11... | collective-permute-start | bytes 589832 | tf_op jit(solution)/shard_map/ppermute | solution.py:1011
  5.3 9.2 %collective-permute-start.1 = (f32[192,128]{1,0:T(8,128)S(1)}, f32[192,128]{1,0:T(8,128)S(1)}, u32[]{:S(2)}, u32[]{:S(2)}) collective-permute-start(f32[192,128]{1,0:T(8,128)S(1)} %get-tuple-element.75), channel_id=1, source_target_pairs={{0,3},{1,2},{2,1},{3,0},{4,7},{5,6},{6,5},{7,4},{8,11},{9,10},{10,... | collective-permute-start | bytes 294920 | tf_op jit(solution)/shard_map/ppermute | solution.py:1005
  12.3 13.9 %collective-permute-start.6 = (f32[168,512]{1,0:T(8,128)S(1)}, f32[168,512]{1,0:T(8,128)S(1)}, u32[]{:S(2)}, u32[]{:S(2)}) collective-permute-start(f32[168,512]{1,0:T(8,128)S(1)} %get-tuple-element.78), channel_id=1, source_target_pairs={{0,1},{1,0},{2,3},{3,2},{4,6},{5,7},{6,4},{7,5},{8,9},{9,8},{10,11... | collective-permute-start | bytes 1032200 | tf_op jit(solution)/shard_map/ppermute | solution.py:1011
  13.0 13.2 %collective-permute-start.7 = (f32[88,512]{1,0:T(8,128)S(1)}, f32[88,512]{1,0:T(8,128)S(1)}, u32[]{:S(2)}, u32[]{:S(2)}) collective-permute-start(f32[88,512]{1,0:T(8,128)S(1)} %get-tuple-element.79), channel_id=1, source_target_pairs={{0,3},{1,2},{2,1},{3,0},{4,7},{5,6},{6,5},{7,4},{8,11},{9,10},{10,... | collective-permute-start | bytes 540680 | tf_op jit(solution)/shard_map/ppermute | solution.py:1005
  14.5 11.8 %collective-permute-start.2 = (f32[592,128]{1,0:T(8,128)S(1)}, f32[592,128]{1,0:T(8,128)S(1)}, u32[]{:S(2)}, u32[]{:S(2)}) collective-permute-start(f32[592,128]{1,0:T(8,128)S(1)} %shard_map.265.refs_5_.refs_7_), channel_id=1, source_target_pairs={{0,8},{4,12},{8,0},{12,4},{16,24},{20,28},{24,16},{28,20},{1,9},{5... | collective-permute-start | bytes 909320 | tf_op jit(solution)/shard_map/ppermute | solution.py:1005
  16.0 14.7 %collective-permute-start.3 = (f32[592,128]{1,0:T(8,128)S(1)}, f32[592,128]{1,0:T(8,128)S(1)}, u32[]{:S(2)}, u32[]{:S(2)}) collective-permute-start(f32[592,128]{1,0:T(8,128)S(1)} %shard_map.265.refs_5_.refs_7_), channel_id=1, source_target_pairs={{0,16},{4,20},{8,24},{12,28},{16,0},{20,4},{24,8},{28,12},{1,17},{... | collective-permute-start | bytes 909320 | tf_op jit(solution)/shard_map/ppermute | solution.py:1005
  17.5 13.2 %collective-permute-start.4 = (f32[592,128]{1,0:T(8,128)S(1)}, f32[592,128]{1,0:T(8,128)S(1)}, u32[]{:S(2)}, u32[]{:S(2)}) collective-permute-start(f32[592,128]{1,0:T(8,128)S(1)} %shard_map.265.refs_5_.refs_7_), channel_id=1, source_target_pairs={{0,24},{4,28},{8,16},{12,20},{16,8},{20,12},{24,0},{28,4},{1,25},{... | collective-permute-start | bytes 909320 | tf_op jit(solution)/shard_map/ppermute | solution.py:1005
  26.2 7.4 %collective-permute-start.5 = (f32[592,128]{1,0:T(8,128)S(1)}, f32[592,128]{1,0:T(8,128)S(1)}, u32[]{:S(2)}, u32[]{:S(2)}) collective-permute-start(f32[592,128]{1,0:T(8,128)S(1)} %shard_map.265.refs_5_.refs_7_), channel_id=1, source_target_pairs={{0,4},{4,0},{8,12},{12,8},{16,20},{20,16},{24,28},{28,24},{1,5},{5... | collective-permute-start | bytes 909320 | tf_op jit(solution)/shard_map/ppermute | solution.py:1005
  30.7 7.0 %collective-permute-start.10 = (f32[592,128]{1,0:T(8,128)S(1)}, f32[592,128]{1,0:T(8,128)S(1)}, u32[]{:S(2)}, u32[]{:S(2)}) collective-permute-start(f32[592,128]{1,0:T(8,128)S(1)} %collective-permute-done.4.refs_8_.refs_10_), channel_id=1, source_target_pairs={{0,4},{4,0},{8,12},{12,8},{16,20},{20,16},{24,28},{28,24},{1,5},{5... | collective-permute-start | bytes 909320 | tf_op jit(solution)/shard_map/ppermute | solution.py:1005
  30.7 7.9 %collective-permute-start.8 = (f32[592,128]{1,0:T(8,128)S(1)}, f32[592,128]{1,0:T(8,128)S(1)}, u32[]{:S(2)}, u32[]{:S(2)}) collective-permute-start(f32[592,128]{1,0:T(8,128)S(1)} %collective-permute-done.2.refs_6_.refs_8_), channel_id=1, source_target_pairs={{0,4},{4,0},{8,12},{12,8},{16,20},{20,16},{24,28},{28,24},{1,5},{5... | collective-permute-start | bytes 909320 | tf_op jit(solution)/shard_map/ppermute | solution.py:1005
  31.2 8.5 %collective-permute-start.9 = (f32[592,128]{1,0:T(8,128)S(1)}, f32[592,128]{1,0:T(8,128)S(1)}, u32[]{:S(2)}, u32[]{:S(2)}) collective-permute-start(f32[592,128]{1,0:T(8,128)S(1)} %collective-permute-done.3.refs_7_.refs_9_), channel_id=1, source_target_pairs={{0,4},{4,0},{8,12},{12,8},{16,20},{20,16},{24,28},{28,24},{1,5},{5... | collective-permute-start | bytes 909320 | tf_op jit(solution)/shard_map/ppermute | solution.py:1005
  31.2 24.9 %collective-permute-start.14 = (f32[256,512]{1,0:T(8,128)S(1)}, f32[256,512]{1,0:T(8,128)S(1)}, u32[]{:S(2)}, u32[]{:S(2)}) collective-permute-start(f32[256,512]{1,0:T(8,128)S(1)} %get-tuple-element.86), channel_id=1, source_target_pairs={{0,1},{1,0},{2,3},{3,2},{4,6},{5,7},{6,4},{7,5},{8,9},{9,8},{10,11... | collective-permute-start | bytes 1572872 | tf_op jit(solution)/shard_map/ppermute | solution.py:1011
  33.5 22.6 %collective-permute-start.15 = (f32[128,512]{1,0:T(8,128)S(1)}, f32[128,512]{1,0:T(8,128)S(1)}, u32[]{:S(2)}, u32[]{:S(2)}) collective-permute-start(f32[128,512]{1,0:T(8,128)S(1)} %get-tuple-element.87), channel_id=1, source_target_pairs={{0,3},{1,2},{2,1},{3,0},{4,7},{5,6},{6,5},{7,4},{8,11},{9,10},{10,... | collective-permute-start | bytes 786440 | tf_op jit(solution)/shard_map/ppermute | solution.py:1005
  37.7 20.6 %collective-permute-start.11 = (f32[240,512]{1,0:T(8,128)S(1)}, f32[240,512]{1,0:T(8,128)S(1)}, u32[]{:S(2)}, u32[]{:S(2)}) collective-permute-start(f32[240,512]{1,0:T(8,128)S(1)} %shard_map.267.refs_0_), channel_id=1, source_target_pairs={{0,8},{4,12},{8,0},{12,4},{16,24},{20,28},{24,16},{28,20},{1,9},{5... | collective-permute-start | bytes 1474568 | tf_op jit(solution)/shard_map/ppermute | solution.py:1005
  38.6 19.8 %collective-permute-start.12 = (f32[240,512]{1,0:T(8,128)S(1)}, f32[240,512]{1,0:T(8,128)S(1)}, u32[]{:S(2)}, u32[]{:S(2)}) collective-permute-start(f32[240,512]{1,0:T(8,128)S(1)} %shard_map.267.refs_0_), channel_id=1, source_target_pairs={{0,16},{4,20},{8,24},{12,28},{16,0},{20,4},{24,8},{28,12},{1,17},{... | collective-permute-start | bytes 1474568 | tf_op jit(solution)/shard_map/ppermute | solution.py:1005
  39.7 21.5 %collective-permute-start.13 = (f32[240,512]{1,0:T(8,128)S(1)}, f32[240,512]{1,0:T(8,128)S(1)}, u32[]{:S(2)}, u32[]{:S(2)}) collective-permute-start(f32[240,512]{1,0:T(8,128)S(1)} %shard_map.267.refs_0_), channel_id=1, source_target_pairs={{0,24},{4,28},{8,16},{12,20},{16,8},{20,12},{24,0},{28,4},{1,25},{... | collective-permute-start | bytes 1474568 | tf_op jit(solution)/shard_map/ppermute | solution.py:1005
  56.2 12.0 %collective-permute-start.17 = (f32[192,512]{1,0:T(8,128)S(1)}, f32[192,512]{1,0:T(8,128)S(1)}, u32[]{:S(2)}, u32[]{:S(2)}) collective-permute-start(f32[192,512]{1,0:T(8,128)S(1)} %get-tuple-element.88.refs_5_.refs_0_), channel_id=1, source_target_pairs={{0,8},{4,12},{8,0},{12,4},{16,24},{20,28},{24,16},{28,20},{1,9},{5... | collective-permute-start | bytes 1179656 | tf_op jit(solution)/shard_map/ppermute | solution.py:1005
  57.2 11.8 %collective-permute-start.18 = (f32[192,512]{1,0:T(8,128)S(1)}, f32[192,512]{1,0:T(8,128)S(1)}, u32[]{:S(2)}, u32[]{:S(2)}) collective-permute-start(f32[192,512]{1,0:T(8,128)S(1)} %get-tuple-element.89.refs_1_), channel_id=1, source_target_pairs={{0,16},{4,20},{8,24},{12,28},{16,0},{20,4},{24,8},{28,12},{1,17},{... | collective-permute-start | bytes 1179656 | tf_op jit(solution)/shard_map/ppermute | solution.py:1005
  61.4 11.2 %copy-start.3 = (bf16[2,896,512]{2,1,0:T(8,128)(2,1)S(1)}, bf16[2,896,512]{2,1,0:T(8,128)(2,1)}, u32[]{:S(2)}) copy-start(bf16[2,896,512]{2,1,0:T(8,128)(2,1)} %param.31) | copy-start | bytes 5505028
  61.4 11.2 %copy-start.4 = (bf16[512,512]{1,0:T(8,128)(2,1)S(1)}, bf16[512,512]{1,0:T(8,128)(2,1)}, u32[]{:S(2)}) copy-start(bf16[512,512]{1,0:T(8,128)(2,1)} %refs_8_.1) | copy-start | bytes 1572868
  61.4 11.2 %copy-start.5 = (bf16[512,512]{1,0:T(8,128)(2,1)S(1)}, bf16[512,512]{1,0:T(8,128)(2,1)}, u32[]{:S(2)}) copy-start(bf16[512,512]{1,0:T(8,128)(2,1)} %refs_11_.1) | copy-start | bytes 1572868
  61.4 11.2 %copy-start.9 = (bf16[128,512]{1,0:T(8,128)(2,1)S(1)}, bf16[128,512]{1,0:T(8,128)(2,1)}, u32[]{:S(2)}) copy-start(bf16[128,512]{1,0:T(8,128)(2,1)} %refs_9_.1) | copy-start | bytes 393220
  61.5 11.2 %copy-start.13 = (f32[512]{0:T(512)S(1)}, f32[512]{0:T(512)}, u32[]{:S(2)}) copy-start(f32[512]{0:T(512)} %param.25) | copy-start | bytes 6148
  61.5 11.2 %copy-start.14 = (f32[512]{0:T(512)S(1)}, f32[512]{0:T(512)}, u32[]{:S(2)}) copy-start(f32[512]{0:T(512)} %param.26) | copy-start | bytes 6148
  61.5 11.2 %copy-start.15 = (f32[512]{0:T(512)S(1)}, f32[512]{0:T(512)}, u32[]{:S(2)}) copy-start(f32[512]{0:T(512)} %param.30) | copy-start | bytes 6148
  61.5 11.2 %copy-start.16 = (f32[512]{0:T(512)S(1)}, f32[512]{0:T(512)}, u32[]{:S(2)}) copy-start(f32[512]{0:T(512)} %param.28) | copy-start | bytes 6148
  61.5 11.1 %collective-permute-start.16 = (f32[968,512]{1,0:T(8,128)S(1)}, f32[968,512]{1,0:T(8,128)S(1)}, u32[]{:S(2)}, u32[]{:S(2)}) collective-permute-start(f32[968,512]{1,0:T(8,128)S(1)} %shard_map.271.refs_4_.refs_12_), channel_id=1, source_target_pairs={{0,4},{4,0},{8,12},{12,8},{16,20},{20,16},{24,28},{28,24},{1,5},{5... | collective-permute-start | bytes 5947400 | tf_op jit(solution)/shard_map/ppermute | solution.py:1005
  69.2 3.5 %collective-permute-start.19 = (f32[768,512]{1,0:T(8,128)S(1)}, f32[768,512]{1,0:T(8,128)S(1)}, u32[]{:S(2)}, u32[]{:S(2)}) collective-permute-start(f32[768,512]{1,0:T(8,128)S(1)} %shard_map.272.refs_14_), channel_id=1, source_target_pairs={{0,4},{4,0},{8,12},{12,8},{16,20},{20,16},{24,28},{28,24},{1,5},{5... | collective-permute-start | bytes 4718600 | tf_op jit(solution)/shard_map/ppermute | solution.py:1005
  103.7 7.9 %collective-permute-start.22 = (f32[4,128,512]{2,1,0:T(8,128)S(1)}, f32[4,128,512]{2,1,0:T(8,128)S(1)}, u32[]{:S(2)}, u32[]{:S(2)}) collective-permute-start(f32[4,128,512]{2,1,0:T(8,128)S(1)} %get-tuple-element.103), channel_id=1, source_target_pairs={{0,4},{4,0},{8,12},{12,8},{16,20},{20,16},{24,28},{28,24},{1,5},{5... | collective-permute-start | bytes 3145736 | tf_op jit(solution)/shard_map/ppermute | solution.py:1005
  109.6 2.0 %collective-permute-start.23 = (f32[4,64,512]{2,1,0:T(8,128)S(1)}, f32[4,64,512]{2,1,0:T(8,128)S(1)}, u32[]{:S(2)}, u32[]{:S(2)}) collective-permute-start(f32[4,64,512]{2,1,0:T(8,128)S(1)} %get-tuple-element.104), channel_id=1, source_target_pairs={{0,4},{4,0},{8,12},{12,8},{16,20},{20,16},{24,28},{28,24},{1,5},{5... | collective-permute-start | bytes 1572872 | tf_op jit(solution)/shard_map/ppermute | solution.py:1005
  112.3 19.4 %collective-permute-start.24 = (f32[192,512]{1,0:T(8,128)S(1)}, f32[192,512]{1,0:T(8,128)S(1)}, u32[]{:S(2)}, u32[]{:S(2)}) collective-permute-start(f32[192,512]{1,0:T(8,128)S(1)} %get-tuple-element.106), channel_id=1, source_target_pairs={{0,8},{4,12},{8,0},{12,4},{16,24},{20,28},{24,16},{28,20},{1,9},{5... | collective-permute-start | bytes 1179656 | tf_op jit(solution)/shard_map/ppermute | solution.py:1005
  113.2 19.6 %collective-permute-start.25 = (f32[192,512]{1,0:T(8,128)S(1)}, f32[192,512]{1,0:T(8,128)S(1)}, u32[]{:S(2)}, u32[]{:S(2)}) collective-permute-start(f32[192,512]{1,0:T(8,128)S(1)} %get-tuple-element.107), channel_id=1, source_target_pairs={{0,16},{4,20},{8,24},{12,28},{16,0},{20,4},{24,8},{28,12},{1,17},{... | collective-permute-start | bytes 1179656 | tf_op jit(solution)/shard_map/ppermute | solution.py:1005
  114.7 18.1 %collective-permute-start.26 = (f32[192,512]{1,0:T(8,128)S(1)}, f32[192,512]{1,0:T(8,128)S(1)}, u32[]{:S(2)}, u32[]{:S(2)}) collective-permute-start(f32[192,512]{1,0:T(8,128)S(1)} %get-tuple-element.108), channel_id=1, source_target_pairs={{0,24},{4,28},{8,16},{12,20},{16,8},{20,12},{24,0},{28,4},{1,25},{... | collective-permute-start | bytes 1179656 | tf_op jit(solution)/shard_map/ppermute | solution.py:1005
  129.4 7.1 %collective-permute-start.20 = (f32[2,1536]{1,0:T(2,128)S(1)}, f32[2,1536]{1,0:T(2,128)S(1)}, u32[]{:S(2)}, u32[]{:S(2)}) collective-permute-start(f32[2,1536]{1,0:T(2,128)S(1)} %bitcast.26), channel_id=1, source_target_pairs={{0,8},{4,12},{8,0},{12,4},{16,24},{20,28},{24,16},{28,20},{1,9},{5... | collective-permute-start | bytes 36872 | tf_op jit(solution)/shard_map/ppermute | solution.py:1005
  130.2 7.7 %collective-permute-start.21 = (f32[2,1536]{1,0:T(2,128)S(1)}, f32[2,1536]{1,0:T(2,128)S(1)}, u32[]{:S(2)}, u32[]{:S(2)}) collective-permute-start(f32[2,1536]{1,0:T(2,128)S(1)} %bitcast.27), channel_id=1, source_target_pairs={{0,16},{4,20},{8,24},{12,28},{16,0},{20,4},{24,8},{28,12},{1,17},{... | collective-permute-start | bytes 36872 | tf_op jit(solution)/shard_map/ppermute | solution.py:1005
  132.9 5.1 %collective-permute-start.27 = (f32[2,1536]{1,0:T(2,128)S(1)}, f32[2,1536]{1,0:T(2,128)S(1)}, u32[]{:S(2)}, u32[]{:S(2)}) collective-permute-start(f32[2,1536]{1,0:T(2,128)S(1)} %bitcast.29), channel_id=1, source_target_pairs={{0,24},{4,28},{8,16},{12,20},{16,8},{20,12},{24,0},{28,4},{1,25},{... | collective-permute-start | bytes 36872 | tf_op jit(solution)/shard_map/ppermute | solution.py:1005
  134.5 16.3 %collective-permute-start.33 = (f32[192,512]{1,0:T(8,128)S(1)}, f32[192,512]{1,0:T(8,128)S(1)}, u32[]{:S(2)}, u32[]{:S(2)}) collective-permute-start(f32[192,512]{1,0:T(8,128)S(1)} %shard_map.277.refs_1_), channel_id=1, source_target_pairs={{0,8},{4,12},{8,0},{12,4},{16,24},{20,28},{24,16},{28,20},{1,9},{5... | collective-permute-start | bytes 1179656 | tf_op jit(solution)/shard_map/ppermute | solution.py:1005
  136.0 16.3 %collective-permute-start.34 = (f32[192,512]{1,0:T(8,128)S(1)}, f32[192,512]{1,0:T(8,128)S(1)}, u32[]{:S(2)}, u32[]{:S(2)}) collective-permute-start(f32[192,512]{1,0:T(8,128)S(1)} %shard_map.277.refs_1_), channel_id=1, source_target_pairs={{0,16},{4,20},{8,24},{12,28},{16,0},{20,4},{24,8},{28,12},{1,17},{... | collective-permute-start | bytes 1179656 | tf_op jit(solution)/shard_map/ppermute | solution.py:1005
  136.4 17.8 %collective-permute-start.35 = (f32[192,512]{1,0:T(8,128)S(1)}, f32[192,512]{1,0:T(8,128)S(1)}, u32[]{:S(2)}, u32[]{:S(2)}) collective-permute-start(f32[192,512]{1,0:T(8,128)S(1)} %shard_map.277.refs_1_), channel_id=1, source_target_pairs={{0,24},{4,28},{8,16},{12,20},{16,8},{20,12},{24,0},{28,4},{1,25},{... | collective-permute-start | bytes 1179656 | tf_op jit(solution)/shard_map/ppermute | solution.py:1005
  138.0 1.3 collective-permute-start.28
  148.8 5.5 %collective-permute-start.29 = (f32[8,512]{1,0:T(8,128)S(1)}, f32[8,512]{1,0:T(8,128)S(1)}, u32[]{:S(2)}, u32[]{:S(2)}) collective-permute-start(f32[8,512]{1,0:T(8,128)S(1)} %get-tuple-element.115.refs_0_), channel_id=1, source_target_pairs={{0,8},{4,12},{8,0},{12,4},{16,24},{20,28},{24,16},{28,20},{1,9},{5... | collective-permute-start | bytes 49160 | tf_op jit(solution)/shard_map/ppermute | solution.py:1005
  150.3 4.4 %collective-permute-start.30 = (f32[8,512]{1,0:T(8,128)S(1)}, f32[8,512]{1,0:T(8,128)S(1)}, u32[]{:S(2)}, u32[]{:S(2)}) collective-permute-start(f32[8,512]{1,0:T(8,128)S(1)} %get-tuple-element.115.refs_0_), channel_id=1, source_target_pairs={{0,16},{4,20},{8,24},{12,28},{16,0},{20,4},{24,8},{28,12},{1,17},{... | collective-permute-start | bytes 49160 | tf_op jit(solution)/shard_map/ppermute | solution.py:1005
  150.8 4.6 %collective-permute-start.31 = (f32[8,512]{1,0:T(8,128)S(1)}, f32[8,512]{1,0:T(8,128)S(1)}, u32[]{:S(2)}, u32[]{:S(2)}) collective-permute-start(f32[8,512]{1,0:T(8,128)S(1)} %get-tuple-element.115.refs_0_), channel_id=1, source_target_pairs={{0,24},{4,28},{8,16},{12,20},{16,8},{20,12},{24,0},{28,4},{1,25},{... | collective-permute-start | bytes 49160 | tf_op jit(solution)/shard_map/ppermute | solution.py:1005
  152.3 6.1 %collective-permute-start.36 = (f32[192,512]{1,0:T(8,128)S(1)}, f32[192,512]{1,0:T(8,128)S(1)}, u32[]{:S(2)}, u32[]{:S(2)}) collective-permute-start(f32[192,512]{1,0:T(8,128)S(1)} %shard_map.277.refs_1_), channel_id=1, source_target_pairs={{0,4},{4,0},{8,12},{12,8},{16,20},{20,16},{24,28},{28,24},{1,5},{5... | collective-permute-start | bytes 1179656 | tf_op jit(solution)/shard_map/ppermute | solution.py:1005
  154.3 4.1 %collective-permute-start.37 = (f32[192,512]{1,0:T(8,128)S(1)}, f32[192,512]{1,0:T(8,128)S(1)}, u32[]{:S(2)}, u32[]{:S(2)}) collective-permute-start(f32[192,512]{1,0:T(8,128)S(1)} %collective-permute-done.33.refs_2_), channel_id=1, source_target_pairs={{0,4},{4,0},{8,12},{12,8},{16,20},{20,16},{24,28},{28,24},{1,5},{5... | collective-permute-start | bytes 1179656 | tf_op jit(solution)/shard_map/ppermute | solution.py:1005
  154.3 4.1 %collective-permute-start.38 = (f32[192,512]{1,0:T(8,128)S(1)}, f32[192,512]{1,0:T(8,128)S(1)}, u32[]{:S(2)}, u32[]{:S(2)}) collective-permute-start(f32[192,512]{1,0:T(8,128)S(1)} %collective-permute-done.34.refs_3_), channel_id=1, source_target_pairs={{0,4},{4,0},{8,12},{12,8},{16,20},{20,16},{24,28},{28,24},{1,5},{5... | collective-permute-start | bytes 1179656 | tf_op jit(solution)/shard_map/ppermute | solution.py:1005
  154.8 3.6 %collective-permute-start.39 = (f32[192,512]{1,0:T(8,128)S(1)}, f32[192,512]{1,0:T(8,128)S(1)}, u32[]{:S(2)}, u32[]{:S(2)}) collective-permute-start(f32[192,512]{1,0:T(8,128)S(1)} %collective-permute-done.35.refs_4_), channel_id=1, source_target_pairs={{0,4},{4,0},{8,12},{12,8},{16,20},{20,16},{24,28},{28,24},{1,5},{5... | collective-permute-start | bytes 1179656 | tf_op jit(solution)/shard_map/ppermute | solution.py:1005
  155.4 1.8 %collective-permute-start.32 = (f32[32,512]{1,0:T(8,128)S(1)}, f32[32,512]{1,0:T(8,128)S(1)}, u32[]{:S(2)}, u32[]{:S(2)}) collective-permute-start(f32[32,512]{1,0:T(8,128)S(1)} %shard_map.280.refs_1_), channel_id=1, source_target_pairs={{0,4},{4,0},{8,12},{12,8},{16,20},{20,16},{24,28},{28,24},{1,5},{5... | collective-permute-start | bytes 196616 | tf_op jit(solution)/shard_map/ppermute | solution.py:1005
  (9 other events, 39.9 us)
